TPU v7x, 256 devices: a whole 4x4x8 slice. The times are simulated.
256 devices in a mesh: grp: 2 (over core), seq: 32 (over z, y), tp: 4 (over x).
Axes of the slice: x: 4, y: 4, z: 8, core: 2. Of those that a mesh axis runs over, the one named last changes fastest.
Arguments:
- states: bfloat16 [24576, 4096], P('seq', 'tp'), may hold values from -24 to 24
- projections: bfloat16 [2, 4096, 2048], P('grp', None, 'tp'), may hold values from -0.09375 to 0.09375
- neighbours: bfloat16 [768, 64, 2048], P('seq', None, 'tp'), may hold values from -24 to 24
- owner: int32 [384, 2], P('seq'), may hold values from 0 to 31, as said below
- slot: int32 [384, 2], P('seq'), may hold values from 0 to 23, as said below
- cotangent: bfloat16 [24576, 2048], P('seq', 'tp'), may hold values from -48 to 48
Outputs:
- grad_states: bfloat16 [24576, 4096], P('seq', ('grp', 'tp'))
Inputs may be any that keep to these rules, and one draw needn't show every extreme that they name: Each owner receives exactly 24 neighbours over all groups. Among the 24 neighbours of one decoder shard, one owner appears exactly 2 times and the other owners as nearly equally often as possible. The pair (owner, slot) names each of the 768 neighbours exactly once.
All inputs are finite; a program needn't handle non-finite values.
Results may differ from a plain program's by a relative error of at most 0.02.
The roundings to bfloat16 on the way count: a program that leaves them out, or rounds other values in their place, can miss the bound.
Values may be sent and summed in bfloat16 or wider, within the bound.
No kernel may reach another device: no remote copies, remote signals or barrier semaphores. Data moves between devices by JAX's collectives and lax.ppermute only.
A program may use at most 128 MiB of HBM per device.

v0:
```python
import jax
import jax.numpy as jnp
from jax import lax
from jax.sharding import PartitionSpec as P

HD = 128
GROUP = 64
KNB = 2


def from_partner(block, axis, bit):
    count = lax.axis_size(axis)
    route = []
    for low in range(count):
        high = low | 1 << bit
        if high != low and high < count:
            route += [(low, high), (high, low)]
    return lax.ppermute(block, axis, route)


def split_heads(features):
    return features.reshape(features.shape[:-1] + (features.shape[-1] // HD, HD))


def encode_forward(inputs, memory):
    score_scale = HD ** (-0.5)
    input_heads = split_heads(inputs)
    memory_heads = split_heads(memory)
    scores = (
        jnp.einsum("bqhd,bkhd->bhqk", input_heads, memory_heads, preferred_element_type=jnp.float32)
        * score_scale
    )
    attn_probs = jax.nn.softmax(scores, axis=-1)
    weights = attn_probs.astype(jnp.bfloat16)
    attn_mixed = jnp.einsum(
        "bhqk,bkhd->bqhd", weights, memory_heads, preferred_element_type=jnp.float32
    )
    encoded = (input_heads.astype(jnp.float32) + attn_mixed).astype(jnp.bfloat16)
    return (encoded.reshape(inputs.shape), attn_probs, weights)


def encode_backward(inputs, memory, attn_probs, weights, grad_encoded):
    score_scale = HD ** (-0.5)
    input_heads = split_heads(inputs)
    memory_heads = split_heads(memory)
    grad_heads = split_heads(grad_encoded)
    grad_probs = jnp.einsum(
        "bqhd,bkhd->bhqk", grad_heads, memory_heads, preferred_element_type=jnp.float32
    )
    grad_scores = attn_probs * (
        grad_probs - jnp.sum(attn_probs * grad_probs, axis=-1, keepdims=True)
    )
    grad_scores = grad_scores.astype(jnp.bfloat16)
    from_scores = (
        jnp.einsum("bhqk,bqhd->bkhd", grad_scores, input_heads, preferred_element_type=jnp.float32)
        * score_scale
    )
    from_values = jnp.einsum(
        "bhqk,bqhd->bkhd", weights, grad_heads, preferred_element_type=jnp.float32
    )
    return (from_scores + from_values).astype(jnp.bfloat16).reshape(memory.shape)


def cross_backward(queries, keys, grad_output):
    score_scale = HD ** (-0.5)
    query_heads = split_heads(queries)
    key_heads = split_heads(keys)
    grad_heads = split_heads(grad_output)
    scores = (
        jnp.einsum("cqhd,ckhd->chqk", query_heads, key_heads, preferred_element_type=jnp.float32)
        * score_scale
    )
    attn_probs = jax.nn.softmax(scores, axis=-1)
    weights = attn_probs.astype(jnp.bfloat16)
    grad_probs = jnp.einsum(
        "cqhd,ckhd->chqk", grad_heads, key_heads, preferred_element_type=jnp.float32
    )
    grad_scores = attn_probs * (
        grad_probs - jnp.sum(attn_probs * grad_probs, axis=-1, keepdims=True)
    )
    grad_scores = grad_scores.astype(jnp.bfloat16)
    grad_queries = (
        jnp.einsum("chqk,ckhd->cqhd", grad_scores, key_heads, preferred_element_type=jnp.float32)
        * score_scale
    ).astype(jnp.bfloat16)
    from_scores = (
        jnp.einsum("chqk,cqhd->ckhd", grad_scores, query_heads, preferred_element_type=jnp.float32)
        * score_scale
    )
    from_values = jnp.einsum(
        "chqk,cqhd->ckhd", weights, grad_heads, preferred_element_type=jnp.float32
    )
    grad_keys = (from_scores + from_values).astype(jnp.bfloat16)
    return (grad_queries.reshape(queries.shape), grad_keys.reshape(keys.shape))


def select_rows(selector, values):
    flat_values = values.reshape(values.shape[0], -1)
    return jnp.dot(selector, flat_values, preferred_element_type=jnp.float32).astype(jnp.bfloat16)


def shards(states, projections, neighbours, owner, slot, cotangent):
    which_side = lax.axis_index("grp")
    tokens = states.shape[0]
    own_proj = projections[0]
    half = own_proj.shape[1] // 2
    sent_half = lax.dynamic_slice_in_dim(own_proj, (1 - which_side) * half, half, 1)
    other_half = from_partner(sent_half, "grp", 0)
    mine_half = lax.dynamic_slice_in_dim(own_proj, which_side * half, half, 1)
    query_weight = jnp.where(which_side == 0, mine_half, other_half)
    memory_weight = jnp.where(which_side == 0, other_half, mine_half)
    weight = jnp.concatenate([query_weight, memory_weight], axis=1)
    neigh_local = lax.dynamic_slice_in_dim(neighbours, which_side * half, half, 2)
    grad_output = lax.dynamic_slice_in_dim(cotangent, which_side * half, half, 1)
    projected = jnp.dot(
        lax.all_gather(states, "tp", axis=1, tiled=True), weight, preferred_element_type=jnp.float32
    )
    projected = projected.astype(jnp.bfloat16)
    query_part = projected[:, :half]
    memory_part = projected[:, half:]
    head_width = memory_part.shape[1]
    owner_count = lax.axis_size("seq")
    groups = owner.shape[0]
    neigh_count = groups * KNB
    capacity = 2 * ((neigh_count + owner_count - 1) // owner_count)
    slot_count = owner_count * capacity
    owned = neigh_local.shape[0]
    neigh_len = neigh_local.shape[1]
    target = owner.reshape(neigh_count)
    owner_slot = slot.reshape(neigh_count)
    neigh_order = jnp.arange(neigh_count)
    earlier = (target[:, None] == target[None, :]) & (neigh_order[None, :] < neigh_order[:, None])
    send_rank = jnp.sum(earlier.astype(jnp.int32), axis=1)
    position = target * capacity + send_rank
    picked = jnp.arange(slot_count)[:, None] == position[None, :]
    pick_rows = picked.astype(jnp.bfloat16)
    pick_groups = jnp.sum(picked.reshape(slot_count, groups, KNB).astype(jnp.int32), axis=2).astype(
        jnp.bfloat16
    )
    memory_rows = memory_part.reshape(groups, GROUP * head_width)
    own_index = jnp.arange(owned)
    outgoing = select_rows(pick_groups, memory_rows).reshape(
        owner_count, capacity, GROUP, head_width
    )
    labels = (jnp.sum(jnp.where(picked, owner_slot[None, :] + 1, 0), axis=1) - 1).reshape(
        owner_count, capacity
    )
    incoming, arrived_labels = (
        lax.all_to_all(outgoing, "seq", split_axis=0, concat_axis=0, tiled=True),
        lax.all_to_all(labels, "seq", split_axis=0, concat_axis=0, tiled=True),
    )
    spread = (arrived_labels.reshape(slot_count)[None, :] == own_index[:, None]).astype(
        jnp.bfloat16
    )
    encoder_inputs = select_rows(spread.T, neigh_local).reshape(slot_count, neigh_len, head_width)
    encoder_memory = incoming.reshape(slot_count, GROUP, head_width)
    encoded, attn_probs, weights = encode_forward(encoder_inputs, encoder_memory)
    encoded_slots = encoded.reshape(owner_count, capacity, neigh_len, head_width)
    returned = lax.all_to_all(encoded_slots, "seq", split_axis=0, concat_axis=0, tiled=True)
    key_rows = select_rows(
        pick_rows.T, returned.reshape(slot_count, neigh_len, head_width)
    ).reshape(neigh_count, neigh_len, head_width)
    grad_queries, grad_keys = cross_backward(
        query_part.reshape(groups, GROUP, head_width),
        key_rows.reshape(groups, KNB * neigh_len, head_width),
        grad_output.reshape(groups, GROUP, head_width),
    )
    grad_keys = grad_keys.reshape(neigh_count, neigh_len, head_width)
    grad_slots = select_rows(pick_rows, grad_keys).reshape(
        owner_count, capacity, neigh_len, head_width
    )
    grad_arrived = lax.all_to_all(grad_slots, "seq", split_axis=0, concat_axis=0, tiled=True)
    grad_encoded = grad_arrived.reshape(slot_count, neigh_len, head_width)
    grad_memory_each = encode_backward(
        encoder_inputs, encoder_memory, attn_probs, weights, grad_encoded
    )
    grad_memory_slots = grad_memory_each.reshape(owner_count, capacity, GROUP, head_width)
    memory_back = lax.all_to_all(grad_memory_slots, "seq", split_axis=0, concat_axis=0, tiled=True)
    grad_memory = select_rows(
        pick_groups.T, memory_back.reshape(slot_count, GROUP, head_width)
    ).reshape(tokens, head_width)
    grad_queries = grad_queries.reshape(tokens, head_width)
    grad_heads = jnp.concatenate([grad_queries, grad_memory], axis=1)
    partial_term = jnp.dot(grad_heads, weight.T, preferred_element_type=jnp.float32)
    return lax.psum_scatter(
        partial_term.astype(jnp.bfloat16), ("grp", "tp"), scatter_dimension=1, tiled=True
    )


def solution(mesh):
    return jax.shard_map(
        shards,
        mesh=mesh,
        in_specs=(
            P("seq", "tp"),
            P("grp", None, "tp"),
            P("seq", None, "tp"),
            P("seq", None),
            P("seq", None),
            P("seq", "tp"),
        ),
        out_specs=P("seq", ("grp", "tp")),
        check_vma=False,
    )
```

profile of v0, /device:TPU:1, one launch (start us, length us, event | category | flops | bytes accessed | tf_op | source)
XLA Modules:
  0.0 468.3 jit_solution(6351701238019112395)
XLA Ops:
  7.3 3.1 dynamic-slice_bitcast_fusion
  10.4 3.2 collective-permute-start
  15.0 9.5 %all-to-all-start = ((s32[32,1,2]{2,1,0:T(1,128)}), s32[32,1,2]{2,1,0:T(1,128)S(1)}, u32[]{:S(2)}, u32[]{:S(2)}) async-start(s32[32,1,2]{2,1,0:T(1,128)} %bitcast), calls=%async_computation | async-start | bytes 32768 | tf_op jit(solution)/shard_map/all_to_all | solution.py:150
  24.9 5.7 %bitcast_select_fusion.1 = (bf16[4096,256]{1,0:T(8,128)(2,1)}, bf16[4096,256]{1,0:T(8,128)(2,1)}) fusion(bf16[4096,256]{1,0:T(8,128)(2,1)} %collective-permute-done, pred[]{:T(512)S(6)} %eq.65, bf16[1,4096,512]{2,1,0:T(8,128)(2,1)} %param.7, s32[]{:T(128)S(6)} %select_n.25), kind=kLoop, calls=%fused_computation.20 | loop fusion | flops 2097152 | bytes 8388613 | tf_op jit(solution)/shard_map/jit(_where)/select_n | solution.py:110
  30.5 50.7 %all-gather.2.cloned.1.call-done = bf16[768,4096]{1,0:T(8,128)(2,1)} async-done(((bf16[768,1024]{1,0:T(8,128)(2,1)}), bf16[768,4096]{1,0:T(8,128)(2,1)}) %all-gather.2.cloned.1.call-update) | async-done | bytes 6291472 | tf_op jit(solution)/shard_map/all_gather | solution.py:116
  81.2 7.5 %fusion.24 = bf16[768,512]{0,1:T(8,128)(2,1)S(1)} fusion(bf16[768,4096]{1,0:T(8,128)(2,1)} %all-gather.2.cloned.1.call-done, bf16[4096,256]{1,0:T(8,128)(2,1)} %get-tuple-element.6, bf16[4096,256]{1,0:T(8,128)(2,1)} %get-tuple-element.5), kind=kOutput, calls=%fused_computation.38 | convolution fusion | flops 3230007296 | bytes 11272192 | tf_op jit(solution)/shard_map/dot_general | solution.py:115
  90.0 1.8 copy.129
  91.8 9.9 %all-to-all-start.1 = ((bf16[32,2,64,256]{3,2,1,0:T(8,128)(2,1)}), bf16[32,2,64,256]{3,2,1,0:T(8,128)(2,1)}, u32[]{:S(2)}, u32[]{:S(2)}) async-start(bf16[32,2,64,256]{3,2,1,0:T(8,128)(2,1)} %bitcast.53), calls=%async_computation.1 | async-start | bytes 4194304 | tf_op jit(solution)/shard_map/all_to_all | solution.py:149
  103.5 2.1 convolution_convert_fusion.2
  105.6 4.4 reshape_reshape.32
  110.0 39.9 %all-to-all-done.1 = bf16[32,2,64,256]{3,2,1,0:T(8,128)(2,1)} async-done(((bf16[32,2,64,256]{3,2,1,0:T(8,128)(2,1)}), bf16[32,2,64,256]{3,2,1,0:T(8,128)(2,1)}, u32[]{:S(2)}, u32[]{:S(2)}) %all-to-all-start.1) | async-done | bytes 2097184 | tf_op jit(solution)/shard_map/all_to_all | solution.py:149
  150.0 4.0 reshape_reshape.33
  154.0 3.4 fusion.17
  157.4 6.2 %fusion.55 = (f32[64,2,64]{2,1,0:T(2,128)S(1)}, f32[64,2,64,64]{2,3,1,0:T(8,128)S(1)}) fusion(f32[64,2,64,64]{2,3,1,0:T(8,128)S(1)} %fusion.17), kind=kOutput, calls=%fused_computation.87 | output fusion | flops 2097215 | bytes 4227072 | tf_op jit(solution)/shard_map/sub | solution.py:33
  165.6 3.5 copy.111
  169.1 4.4 reshape_reshape.34
  173.5 7.1 %all-to-all-start.2 = ((bf16[32,2,64,256]{3,2,1,0:T(8,128)(2,1)}), bf16[32,2,64,256]{3,2,1,0:T(8,128)(2,1)}, u32[]{:S(2)}, u32[]{:S(2)}) async-start(bf16[32,2,64,256]{3,2,1,0:T(8,128)(2,1)} %reshape_reshape.34), calls=%async_computation.2 | async-start | bytes 4194304 | tf_op jit(solution)/shard_map/all_to_all | solution.py:159
  181.1 46.4 %all-to-all-done.2 = bf16[32,2,64,256]{3,2,1,0:T(8,128)(2,1)} async-done(((bf16[32,2,64,256]{3,2,1,0:T(8,128)(2,1)}), bf16[32,2,64,256]{3,2,1,0:T(8,128)(2,1)}, u32[]{:S(2)}, u32[]{:S(2)}) %all-to-all-start.2) | async-done | bytes 2097184 | tf_op jit(solution)/shard_map/all_to_all | solution.py:159
  227.4 2.9 copy.130
  232.0 4.2 fusion.56
  237.5 1.6 fusion.41
  239.1 4.5 fusion.26
  246.2 54.6 %all_to_all.26 = bf16[32,2,64,256]{3,2,1,0:T(8,128)(2,1)} all-to-all(bf16[32,2,64,256]{3,2,1,0:T(8,128)(2,1)S(1)} %bitcast.56), channel_id=1, replica_groups=mesh['grp'=2,'seq'=32,'tp'=4] {'seq'}, dimensions={0} | all-to-all | bytes 4194304 | tf_op jit(solution)/shard_map/all_to_all | solution.py:172
  300.8 4.0 reshape_reshape.39
  304.9 4.9 %multiply_reduce_fusion = (f32[64,2,64]{2,1,0:T(2,128)S(1)}, f32[64,2,64,64]{2,3,1,0:T(8,128)S(1)}) fusion(f32[64,2,64,64]{2,3,1,0:T(8,128)} %copy-done.5, f32[64,2,64]{2,1,0:T(2,128)S(1)} %copy-done.10, bf16[64,64,2,128]{3,2,1,0:T(2,128)(2,1)} %reshape_reshape.33, bf16[64,64,2,128]{3,2,1,0:T(2,128)(2,1)} %reshape_reshape.39), kind=kOutput, calls=%fused_computation.13 | convolution fusion | flops 135782400 | bytes 8454144 | tf_op jit(solution)/shard_map/bqhd,bkhd->bhqk/dot_general | solution.py:47
  312.7 3.5 copy.126
  316.2 4.4 reshape_reshape.40
  320.6 7.0 %all-to-all-start.4 = ((bf16[32,2,64,256]{3,2,1,0:T(8,128)(2,1)}), bf16[32,2,64,256]{3,2,1,0:T(8,128)(2,1)}, u32[]{:S(2)}, u32[]{:S(2)}) async-start(bf16[32,2,64,256]{3,2,1,0:T(8,128)(2,1)} %reshape_reshape.40), calls=%async_computation.4 | async-start | bytes 4194304 | tf_op jit(solution)/shard_map/all_to_all | solution.py:178
  328.5 44.9 %all-to-all-done.4 = bf16[32,2,64,256]{3,2,1,0:T(8,128)(2,1)} async-done(((bf16[32,2,64,256]{3,2,1,0:T(8,128)(2,1)}), bf16[32,2,64,256]{3,2,1,0:T(8,128)(2,1)}, u32[]{:S(2)}, u32[]{:S(2)}) %all-to-all-start.4) | async-done | bytes 2097184 | tf_op jit(solution)/shard_map/all_to_all | solution.py:178
  373.4 2.9 copy.133
  377.0 8.3 %convolution_convert_fusion.5 = bf16[768,4096]{1,0:T(8,128)(2,1)} fusion(bf16[4096,256]{1,0:T(8,128)(2,1)} %get-tuple-element.6, bf16[4096,256]{1,0:T(8,128)(2,1)} %get-tuple-element.5, bf16[768,256]{1,0:T(8,128)(2,1)S(1)} %reshape.78, bf16[768,256]{1,0:T(8,128)(2,1)S(1)} %bitcast.60), kind=kOutput, calls=%fused_computation.7 | convolution fusion | flops 3234332672 | bytes 11272192 | tf_op jit(solution)/shard_map/dot_general | solution.py:184
  385.4 76.1 %reduce-scatter.2.cloned.1.call-done = bf16[768,512]{1,0:T(8,128)(2,1)} async-done(((bf16[768,4096]{1,0:T(8,128)(2,1)}), bf16[768,512]{1,0:T(8,128)(2,1)}) %reduce-scatter.2.cloned.1.call-update) | async-done | bytes 786448 | tf_op jit(solution)/shard_map/reduce_scatter | solution.py:185
  (79 shorter events, 17.9 us)
Async XLA Ops:
  6.5 95.2 %copy-start = (bf16[24,64,512]{2,1,0:T(8,128)(2,1)S(1)}, bf16[24,64,512]{2,1,0:T(8,128)(2,1)}, u32[]{:S(2)}) copy-start(bf16[24,64,512]{2,1,0:T(8,128)(2,1)} %param.8) | copy-start | bytes 4718596
  6.5 74.7 %all-gather.2.cloned.1.call-start = ((), (), s32[]{:S(2)}) async-start(), calls=%async_computation.6 | async-start | bytes 7864320 | tf_op jit(solution)/shard_map/all_gather | solution.py:116
  7.3 6.3 %copy-start.13 = (s32[12,2]{0,1:T(2,128)S(1)}, s32[12,2]{0,1:T(2,128)}, u32[]{:S(2)}) copy-start(s32[12,2]{0,1:T(2,128)} %param.10) | copy-start | bytes 292
  7.3 6.5 %copy-start.12 = (s32[12,2]{0,1:T(2,128)S(1)}, s32[12,2]{0,1:T(2,128)}, u32[]{:S(2)}) copy-start(s32[12,2]{0,1:T(2,128)} %param.9) | copy-start | bytes 292
  10.4 14.5 %collective-permute-start = (bf16[4096,256]{1,0:T(8,128)(2,1)}, bf16[4096,256]{1,0:T(8,128)(2,1)}, u32[]{:S(2)}, u32[]{:S(2)}) collective-permute-start(bf16[4096,256]{1,0:T(8,128)(2,1)} %dynamic-slice_bitcast_fusion), channel_id=1, source_target_pairs={{0,128},{128,0},{1,129},{129,1},{2,130},{130,2},{3,131},{131,3},{4... | collective-permute-start | bytes 6291464 | tf_op jit(solution)/shard_map/ppermute | solution.py:18
  15.0 76.8 %all-to-all-start = ((s32[32,1,2]{2,1,0:T(1,128)}), s32[32,1,2]{2,1,0:T(1,128)S(1)}, u32[]{:S(2)}, u32[]{:S(2)}) async-start(s32[32,1,2]{2,1,0:T(1,128)} %bitcast), calls=%async_computation | async-start | bytes 32768 | tf_op jit(solution)/shard_map/all_to_all | solution.py:150
  91.8 58.2 %all-to-all-start.1 = ((bf16[32,2,64,256]{3,2,1,0:T(8,128)(2,1)}), bf16[32,2,64,256]{3,2,1,0:T(8,128)(2,1)}, u32[]{:S(2)}, u32[]{:S(2)}) async-start(bf16[32,2,64,256]{3,2,1,0:T(8,128)(2,1)} %bitcast.53), calls=%async_computation.1 | async-start | bytes 4194304 | tf_op jit(solution)/shard_map/all_to_all | solution.py:149
  157.4 6.2 %copy-start.2 = (bf16[64,64,2,128]{3,2,1,0:T(2,128)(2,1)S(1)}, bf16[64,64,2,128]{3,2,1,0:T(2,128)(2,1)}, u32[]{:S(2)}) copy-start(bf16[64,64,2,128]{3,2,1,0:T(2,128)(2,1)} %reshape_reshape.32) | copy-start | bytes 6291460
  157.4 6.2 %copy-start.4 = (bf16[64,64,2,128]{3,2,1,0:T(2,128)(2,1)S(1)}, bf16[64,64,2,128]{3,2,1,0:T(2,128)(2,1)}, u32[]{:S(2)}) copy-start(bf16[64,64,2,128]{3,2,1,0:T(2,128)(2,1)} %reshape_reshape.33) | copy-start | bytes 6291460
  163.6 1.9 copy-start.5
  163.6 2.0 copy-start.9
  173.5 7.1 %copy-start.8 = (bf16[768,512]{1,0:T(8,128)(2,1)S(1)}, bf16[768,512]{1,0:T(8,128)(2,1)}, u32[]{:S(2)}) copy-start(bf16[768,512]{1,0:T(8,128)(2,1)} %param.11) | copy-start | bytes 2359300
  173.5 53.9 %all-to-all-start.2 = ((bf16[32,2,64,256]{3,2,1,0:T(8,128)(2,1)}), bf16[32,2,64,256]{3,2,1,0:T(8,128)(2,1)}, u32[]{:S(2)}, u32[]{:S(2)}) async-start(bf16[32,2,64,256]{3,2,1,0:T(8,128)(2,1)} %reshape_reshape.34), calls=%async_computation.2 | async-start | bytes 4194304 | tf_op jit(solution)/shard_map/all_to_all | solution.py:159
  236.2 0.8 copy-start.11
  300.8 4.0 copy-start.10
  304.9 4.9 %copy-start.3 = (bf16[64,64,2,128]{3,2,1,0:T(2,128)(2,1)S(1)}, bf16[64,64,2,128]{3,2,1,0:T(2,128)(2,1)}, u32[]{:S(2)}) copy-start(bf16[64,64,2,128]{3,2,1,0:T(2,128)(2,1)} %reshape_reshape.32) | copy-start | bytes 6291460
  304.9 5.3 %copy-start.6 = (f32[64,2,64,64]{2,3,1,0:T(8,128)S(1)}, f32[64,2,64,64]{2,3,1,0:T(8,128)}, u32[]{:S(2)}) copy-start(f32[64,2,64,64]{2,3,1,0:T(8,128)} %copy-done.5) | copy-start | bytes 6291460
  310.1 1.6 copy-start.7
  320.6 52.8 %all-to-all-start.4 = ((bf16[32,2,64,256]{3,2,1,0:T(8,128)(2,1)}), bf16[32,2,64,256]{3,2,1,0:T(8,128)(2,1)}, u32[]{:S(2)}, u32[]{:S(2)}) async-start(bf16[32,2,64,256]{3,2,1,0:T(8,128)(2,1)} %reshape_reshape.40), calls=%async_computation.4 | async-start | bytes 4194304 | tf_op jit(solution)/shard_map/all_to_all | solution.py:178
  327.6 133.9 %reduce-scatter.2.cloned.1.call-start = ((), (), s32[]{:S(2)}) async-start(), calls=%async_computation.7 | async-start | bytes 7077888 | tf_op jit(solution)/shard_map/reduce_scatter | solution.py:185
  385.3 76.1 %copy-start.1 = (bf16[24,64,512]{2,1,0:T(8,128)(2,1)S(1)}, bf16[24,64,512]{2,1,0:T(8,128)(2,1)}, u32[]{:S(2)}) copy-start(bf16[24,64,512]{2,1,0:T(8,128)(2,1)} %param.8) | copy-start | bytes 4718596
Sparse Core Ops, SparseCore 0:
  9.2 71.9 all-gather.1
  385.5 75.9 reduce-scatter.1
where the time goes:
time: 469 us; the launch traced here: 468 us
  waiting for transfers between devices  259 us (55%)
  blocking collectives  54.6 us (12%)
  local copies, waits for them, and re-layouts  47.3 us (10%)
  matrix products  39.5 us (8%)
  starting transfers between devices  36.7 us (8%)
  other arithmetic  17.6 us (4%)
  between operations  13.8 us (3%)
    reduce_scatter x1, waiting for transfers between devices, shards(): lax.psum_scatter(partial_term.astype(jnp.bfloat16), ('grp', 'tp'), scatte...  76.1 us
    all_to_all x1, blocking collectives, shards(): lax.all_to_all(grad_slots, 'seq', split_axis=0, concat_axis=0, tiled=True)  54.6 us
    all_gather x1, waiting for transfers between devices, shards(): lax.all_gather(states, 'tp', axis=1, tiled=True)  50.7 us
    all_to_all x1, waiting for transfers between devices, shards(): lax.all_to_all(encoded_slots, 'seq', split_axis=0, concat_axis=0, tiled=T...  46.4 us
    all_to_all x1, waiting for transfers between devices, shards(): lax.all_to_all(grad_memory_slots, 'seq', split_axis=0, concat_axis=0, til...  44.9 us
    all_to_all x1, waiting for transfers between devices, shards(): lax.all_to_all(outgoing, 'seq', split_axis=0, concat_axis=0, tiled=True)  39.9 us
    another operation x6, local copies, waits for them, and re-layouts, split_heads(): features.reshape(features.shape[:-1] + (features.shape[-1] // HD, HD))  13.2 us
    unnamed x35, local copies, waits for them, and re-layouts  10.7 us
  transfers between devices with their start and end apart: 7, of which 5 were waited for; matrix products, arithmetic and copies ran while one was open for 7% of the time, Pallas kernels for 0%

commit v1 on v0

v1 whole, which is shorter than its diff:
```python
import jax
import jax.numpy as jnp
from jax import lax
from jax.experimental import pallas as pl
from jax.experimental.pallas import tpu as pltpu
from jax.sharding import PartitionSpec as P

HD = 128
GROUP = 64
KNB = 2
CAP = 2
SCALE = HD ** (-0.5)
VMEM_LIMIT = 48 * 1024 * 1024


def swap_cores(block):
    return lax.ppermute(block, "grp", [(0, 1), (1, 0)])


def dot_nt(a, b):
    return lax.dot_general(a, b, (((1,), (1,)), ((), ())), preferred_element_type=jnp.float32)


def dot_tn(a, b):
    return lax.dot_general(a, b, (((0,), (0,)), ((), ())), preferred_element_type=jnp.float32)


def dot_nn(a, b):
    return lax.dot_general(a, b, (((1,), (0,)), ((), ())), preferred_element_type=jnp.float32)


def pick_kernel(count, last, index_ref, source_ref, out_ref):
    def step(i, carry):
        out_ref[i] = source_ref[jnp.clip(index_ref[i], 0, last)]
        return carry

    lax.fori_loop(0, count, step, 0)


def pick_blocks(index, source):
    count = index.shape[0]
    rows, columns = source.shape[1:]
    return pl.pallas_call(
        lambda *refs: pick_kernel(count, source.shape[0] - 1, *refs),
        out_shape=jax.ShapeDtypeStruct((count, rows, columns), source.dtype),
        in_specs=[
            pl.BlockSpec(memory_space=pltpu.SMEM),
            pl.BlockSpec(memory_space=pltpu.VMEM),
        ],
        out_specs=pl.BlockSpec(memory_space=pltpu.VMEM),
        compiler_params=pltpu.CompilerParams(vmem_limit_bytes=VMEM_LIMIT),
        name="pick_blocks",
    )(index, source)


def head_gradients(queries, memory, inputs, grad_out):
    scores = dot_nt(memory, inputs) * SCALE
    scores = jnp.exp(scores - jnp.max(scores, axis=0, keepdims=True))
    enc_probs = scores * (1.0 / jnp.sum(scores, axis=0, keepdims=True))
    enc_weights = enc_probs.astype(jnp.bfloat16)
    mixed = dot_tn(enc_weights, memory)
    keys = (inputs.astype(jnp.float32) + mixed).astype(jnp.bfloat16)
    scores = dot_nt(queries, keys) * SCALE
    scores = jnp.exp(scores - jnp.max(scores, axis=1, keepdims=True))
    probs = scores * (1.0 / jnp.sum(scores, axis=1, keepdims=True))
    weights = probs.astype(jnp.bfloat16)
    grad_probs = dot_nt(grad_out, keys)
    grad_scores = probs * (grad_probs - jnp.sum(probs * grad_probs, axis=1, keepdims=True))
    grad_scores = grad_scores.astype(jnp.bfloat16)
    grad_queries = dot_nn(grad_scores, keys) * SCALE
    grad_keys = dot_tn(grad_scores, queries) * SCALE + dot_tn(weights, grad_out)
    grad_keys = grad_keys.astype(jnp.bfloat16)
    grad_probs = dot_nt(memory, grad_keys)
    grad_scores = enc_probs * (grad_probs - jnp.sum(enc_probs * grad_probs, axis=0, keepdims=True))
    grad_scores = grad_scores.astype(jnp.bfloat16)
    grad_memory = dot_nn(grad_scores, inputs) * SCALE + dot_nn(enc_weights, grad_keys)
    return grad_queries.astype(jnp.bfloat16), grad_memory.astype(jnp.bfloat16)


def attend_kernel(side_ref, own_ref, other_ref, cot_ref, near_ref, far_ref, grad_own_ref, grad_other_ref):
    side = side_ref[0]
    half = near_ref.shape[1]
    first = side == 0
    for far in range(2):
        held_ref = far_ref if far else near_ref
        start = ((side + far) % 2) * half
        for low in range(0, half, HD):
            lanes = pl.ds(pl.multiple_of(start + low, HD), HD)
            own = own_ref[:, lanes]
            other = other_ref[:, lanes]
            grad_q, grad_m = head_gradients(
                jnp.where(first, own, other),
                jnp.where(first, other, own),
                held_ref[:, low : low + HD],
                cot_ref[:, lanes],
            )
            grad_own_ref[:, lanes] = jnp.where(first, grad_q, grad_m)
            grad_other_ref[:, lanes] = jnp.where(first, grad_m, grad_q)


def attend(side, own, other, cotangent, near, far):
    tokens, width = own.shape
    half = near.shape[1]
    token_spec = pl.BlockSpec((GROUP, width), lambda c, s: (c, 0))
    neigh_spec = pl.BlockSpec((KNB * near.shape[0] // (tokens // GROUP * KNB), half), lambda c, s: (c, 0))
    return pl.pallas_call(
        attend_kernel,
        grid_spec=pltpu.PrefetchScalarGridSpec(
            num_scalar_prefetch=1,
            grid=(tokens // GROUP,),
            in_specs=[token_spec] * 3 + [neigh_spec] * 2,
            out_specs=[token_spec] * 2,
        ),
        out_shape=[jax.ShapeDtypeStruct((tokens, width), jnp.bfloat16)] * 2,
        compiler_params=pltpu.CompilerParams(vmem_limit_bytes=VMEM_LIMIT),
        name="attend",
    )(side, own, other, cotangent, near, far)


def shards(states, projections, neighbours, owner, slot, cotangent):
    side = lax.axis_index("grp")
    owner_count = lax.axis_size("seq")
    tp_count = lax.axis_size("tp")
    tokens = states.shape[0] // 2
    groups = owner.shape[0]
    neigh_count = groups * KNB
    slot_count = owner_count * CAP
    owned, neigh_len, features = neighbours.shape
    half = features // 2

    target = owner.reshape(neigh_count)
    owner_slot = slot.reshape(neigh_count)
    order = jnp.arange(neigh_count)
    earlier = (target[:, None] == target[None, :]) & (order[None, :] < order[:, None])
    position = target * CAP + jnp.sum(earlier.astype(jnp.int32), axis=1)
    picked = jnp.arange(slot_count)[:, None] == position[None, :]
    labels = jnp.sum(jnp.where(picked, owner_slot[None, :], 0), axis=1).reshape(owner_count, CAP)
    labels = lax.all_to_all(labels, "seq", split_axis=0, concat_axis=0, tiled=True)

    neigh_half = lax.dynamic_slice_in_dim(neighbours, side * half, half, 2)
    outgoing = pick_blocks(labels.reshape(slot_count), neigh_half)
    incoming = lax.all_to_all(
        outgoing.reshape(owner_count, CAP, neigh_len, half), "seq", split_axis=0, concat_axis=0, tiled=True
    ).reshape(slot_count, neigh_len, half)

    rows = lax.dynamic_slice_in_dim(states, side * tokens, tokens, 0)
    gathered = lax.all_gather(rows, "tp", axis=1, tiled=True)
    own_weight = projections[0]
    other_weight = swap_cores(own_weight)
    own = jnp.dot(gathered, own_weight, preferred_element_type=jnp.float32).astype(jnp.bfloat16)
    other = jnp.dot(gathered, other_weight, preferred_element_type=jnp.float32).astype(jnp.bfloat16)

    mine = neigh_count // 2
    keep = lax.dynamic_slice_in_dim(position, side * mine, mine, 0)
    give = lax.dynamic_slice_in_dim(position, (1 - side) * mine, mine, 0)
    far = swap_cores(pick_blocks(give, incoming))
    near = pick_blocks(keep, incoming)
    grad_output = lax.dynamic_slice_in_dim(cotangent, side * tokens, tokens, 0)
    grad_own, grad_other = attend(
        side.reshape(1).astype(jnp.int32),
        own,
        other,
        grad_output,
        near.reshape(mine * neigh_len, half),
        far.reshape(mine * neigh_len, half),
    )

    width = own_weight.shape[0] // 2

    def partial_half(which):
        rows_own = own_weight[which * width : (which + 1) * width]
        rows_other = other_weight[which * width : (which + 1) * width]
        return (dot_nt(grad_own, rows_own) + dot_nt(grad_other, rows_other)).astype(jnp.bfloat16)

    partial_term = jnp.stack([partial_half(0), partial_half(1)])
    summed = lax.psum_scatter(partial_term, "tp", scatter_dimension=2, tiled=True)
    kept = lax.dynamic_index_in_dim(summed, side, 0, keepdims=False)
    given = lax.dynamic_index_in_dim(summed, 1 - side, 0, keepdims=False)
    received = swap_cores(given)
    return jnp.where(
        side == 0, jnp.concatenate([kept, received]), jnp.concatenate([received, kept])
    )


def solution(mesh):
    return jax.shard_map(
        shards,
        mesh=mesh,
        in_specs=(
            P("seq", "tp"),
            P("grp", None, "tp"),
            P("seq", None, "tp"),
            P("seq", None),
            P("seq", None),
            P("seq", "tp"),
        ),
        out_specs=P("seq", ("grp", "tp")),
        check_vma=False,
    )
```

time: 469 us -> 189 us (0.40)
  waiting for transfers between devices: 259 us -> 90.9 us
  blocking collectives: 54.6 us -> 0 us
  local copies, waits for them, and re-layouts: 47.3 us -> 9.3 us
  Pallas kernels: 0 us -> 29.6 us
  matrix products: 39.5 us -> 16.5 us
  other arithmetic: 17.6 us -> 4.04 us
  starting transfers between devices: 36.7 us -> 24.4 us
    all_to_all x3 -> x1, waiting for transfers between devices: 131 us -> 45 us  [shards(): lax.all_to_all(outgoing.reshape(owner_count, CAP, neigh_len, half), 'seq'...]
    all_to_all x1 -> x0, blocking collectives: 54.6 us -> none  [shards(): lax.all_to_all(grad_slots, 'seq', split_axis=0, concat_axis=0, tiled=True)]
    all_gather x1, waiting for transfers between devices: 50.7 us -> 0.02 us  [shards(): gathered = lax.all_gather(rows, 'tp', axis=1, tiled=True)]
    reduce_scatter x1, waiting for transfers between devices: 76.1 us -> 37.2 us  [shards(): lax.psum_scatter(partial_term, 'tp', scatter_dimension=2, tiled=True)]
    pallas_call x0 -> x4, Pallas kernels: none -> 29.6 us  [the longest x1 25.1 us: attend(): pl.pallas_call(attend_kernel, grid_spec=pltpu.PrefetchScalarGridSpec(num_...]
    dot_general x17 -> x6, matrix products: 39.5 us -> 16.5 us  [the longest x4 7.48 us: dot_nt(): lax.dot_general(a, b, (((1,), (1,)), ((), ())), preferred_element_type=jn...]
    another operation x9 -> x0, local copies, waits for them, and re-layouts: 22.6 us -> none  [the longest x6 13.2 us: split_heads(): features.reshape(features.shape[:-1] + (features.shape[-1] // HD, HD))]
    all_to_all x3 -> x1, starting transfers between devices: 24 us -> 4.9 us  [shards(): lax.all_to_all(outgoing.reshape(owner_count, CAP, neigh_len, half), 'seq'...]
  transfers between devices with their start and end apart: 7 -> 7, of which waited for: 5 -> 4; matrix products, arithmetic and copies ran while one was open for 7% -> 7% of each run, Pallas kernels for 0% -> 2%
where the time goes in v1:
time: 189 us; the launch traced here: 188 us
  waiting for transfers between devices  90.9 us (48%)
  Pallas kernels  29.6 us (16%)
  starting transfers between devices  24.4 us (13%)
  matrix products  16.5 us (9%)
  between operations  13.6 us (7%)
  local copies, waits for them, and re-layouts  9.3 us (5%)
  other arithmetic  4.04 us (2%)
    all_to_all x1, waiting for transfers between devices, shards(): lax.all_to_all(outgoing.reshape(owner_count, CAP, neigh_len, half), 'seq'...  45 us
    reduce_scatter x1, waiting for transfers between devices, shards(): lax.psum_scatter(partial_term, 'tp', scatter_dimension=2, tiled=True)  37.2 us
    pallas_call x1, Pallas kernels, attend(): pl.pallas_call(attend_kernel, grid_spec=pltpu.PrefetchScalarGridSpec(num_...  25.1 us
    all_to_all x1, starting transfers between devices, shards(): lax.all_to_all(labels, 'seq', split_axis=0, concat_axis=0, tiled=True)  12 us
    dot_general x4, matrix products, dot_nt(): lax.dot_general(a, b, (((1,), (1,)), ((), ())), preferred_element_type=jn...  7.48 us
    ppermute x3, starting transfers between devices, swap_cores(): return lax.ppermute(block, 'grp', [(0, 1), (1, 0)])  7.46 us
    all_to_all x1, waiting for transfers between devices, shards(): lax.all_to_all(labels, 'seq', split_axis=0, concat_axis=0, tiled=True)  7.34 us
    dot_general x1, matrix products, shards(): jnp.dot(gathered, own_weight, preferred_element_type=jnp.float32)  5.06 us
  transfers between devices with their start and end apart: 7, of which 4 were waited for; matrix products, arithmetic and copies ran while one was open for 7% of the time, Pallas kernels for 2%

profile of v1, /device:TPU:1, one launch (start us, length us, event | category | flops | bytes accessed | tf_op | source)
XLA Modules:
  0.0 188.4 jit_solution(18061760709057538182)
XLA Ops:
  6.5 1.4 copy-done
  7.9 0.9 constant_dynamic-slice_fusion.2
  8.9 0.8 copy.14
  9.8 0.8 copy.15
  10.6 0.2 convert_reduce_fusion
  10.9 0.7 all_to_all.9
  11.6 12.0 %all-to-all-start = ((s32[32,1,2]{2,1,0:T(1,128)}), s32[32,1,2]{2,1,0:T(1,128)S(1)}, u32[]{:S(2)}, u32[]{:S(2)}) async-start(s32[32,1,2]{2,1,0:T(1,128)} %bitcast.2), calls=%async_computation | async-start | bytes 32768 | tf_op jit(solution)/shard_map/all_to_all | solution.py:138
  23.7 1.2 constant_dynamic-slice_fusion.refs_1_
  24.9 7.3 %all-to-all-done = s32[32,1,2]{2,1,0:T(1,128)S(1)} async-done(((s32[32,1,2]{2,1,0:T(1,128)}), s32[32,1,2]{2,1,0:T(1,128)S(1)}, u32[]{:S(2)}, u32[]{:S(2)}) %all-to-all-start) | async-done | bytes 288 | tf_op jit(solution)/shard_map/all_to_all | solution.py:138
  32.2 0.6 broadcast.12
  32.8 0.7 reduce.3
  33.6 1.1 pick_blocks.3
  34.7 1.3 copy-done.1
  36.0 4.9 %all-to-all-start.1 = ((bf16[32,2,64,256]{3,2,1,0:T(8,128)(2,1)}), bf16[32,2,64,256]{3,2,1,0:T(8,128)(2,1)}, u32[]{:S(2)}, u32[]{:S(2)}) async-start(bf16[32,2,64,256]{3,2,1,0:T(8,128)(2,1)} %bitcast.30), calls=%async_computation.1 | async-start | bytes 4194304 | tf_op jit(solution)/shard_map/all_to_all | solution.py:142
  41.0 2.0 %collective-permute-start = (bf16[4096,512]{1,0:T(8,128)(2,1)}, bf16[4096,512]{1,0:T(8,128)(2,1)}, u32[]{:S(2)}, u32[]{:S(2)}) collective-permute-start(bf16[4096,512]{1,0:T(8,128)(2,1)} %bitcast.33), channel_id=1, source_target_pairs={{0,128},{128,0},{1,129},{129,1},{2,130},{130,2},{3,131},{131,3},{4... | collective-permute-start | bytes 12582920 | tf_op jit(solution)/shard_map/ppermute | solution.py:17
  43.1 45.0 %all-to-all-done.1 = bf16[32,2,64,256]{3,2,1,0:T(8,128)(2,1)} async-done(((bf16[32,2,64,256]{3,2,1,0:T(8,128)(2,1)}), bf16[32,2,64,256]{3,2,1,0:T(8,128)(2,1)}, u32[]{:S(2)}, u32[]{:S(2)}) %all-to-all-start.1) | async-done | bytes 2097184 | tf_op jit(solution)/shard_map/all_to_all | solution.py:142
  88.1 1.7 pick_blocks.5
  89.8 4.7 %collective-permute-start.1 = (bf16[12,64,256]{2,1,0:T(8,128)(2,1)S(1)}, bf16[12,64,256]{2,1,0:T(8,128)(2,1)S(1)}, u32[]{:S(2)}, u32[]{:S(2)}) collective-permute-start(bf16[12,64,256]{2,1,0:T(8,128)(2,1)S(1)} %pick_blocks.5), channel_id=1, source_target_pairs={{0,128},{128,0},{1,129},{129,1},{2,130},{130,2},{3,131},{131,3},{4... | collective-permute-start | bytes 1179656 | tf_op jit(solution)/shard_map/ppermute | solution.py:17
  94.5 1.7 pick_blocks.4
  96.2 5.1 %convolution_convert_fusion.1.own_ref = bf16[384,512]{1,0:T(8,128)(2,1)S(1)} fusion(bf16[384,4096]{1,0:T(8,128)(2,1)} %all-gather.2.cloned.1.call-done, bf16[1,4096,512]{2,1,0:T(8,128)(2,1)} %param.7), kind=kOutput, calls=%fused_computation.14 | convolution fusion | flops 1610809344 | bytes 7733248 | tf_op jit(solution)/shard_map/dot_general | solution.py:150
  101.3 4.0 %convolution_convert_fusion.other_ref = bf16[384,512]{1,0:T(8,128)(2,1)S(1)} fusion(bf16[384,4096]{1,0:T(8,128)(2,1)S(1)} %copy-done.4, bf16[4096,512]{1,0:T(8,128)(2,1)} %collective-permute-done), kind=kOutput, calls=%fused_computation.13 | convolution fusion | flops 1610809344 | bytes 7733248 | tf_op jit(solution)/shard_map/dot_general | solution.py:151
  105.3 25.1 %attend.1 = (bf16[384,512]{1,0:T(8,128)(2,1)S(1)}, bf16[384,512]{1,0:T(8,128)(2,1)S(1)}) custom-call(s32[1]{0:T(128)} %bitcast.side_ref, bf16[384,512]{1,0:T(8,128)(2,1)S(1)} %convolution_convert_fusion.1.own_ref, bf16[384,512]{1,0:T(8,128)(2,1)S(1)} %convolution_convert_fusion.other_ref, bf16[384,512]{1,0:T(8,128)(2,1)S(1)} %constant_dynamic-slice_fusion.1.cot_ref, ...), custom_call_target="tpu_custom_call" | custom-call | tf_op jit(solution)/shard_map/attend/pallas_call | solution.py:106
  130.4 2.7 %fusion.4 = f32[384,2048]{1,0:T(8,128)S(1)} fusion(bf16[384,512]{1,0:T(8,128)(2,1)S(1)} %get-tuple-element.8, bf16[4096,512]{1,0:T(8,128)(2,1)} %collective-permute-done), kind=kOutput, calls=%fused_computation.7 | convolution fusion | flops 805306368 | bytes 5636096 | tf_op jit(solution)/shard_map/dot_general | solution.py:21
  133.2 1.1 fusion
  134.3 2.6 %fusion.2 = f32[384,2048]{1,0:T(8,128)S(1)} fusion(bf16[384,512]{1,0:T(8,128)(2,1)S(1)} %get-tuple-element.8, bf16[4096,512]{1,0:T(8,128)(2,1)} %collective-permute-done), kind=kOutput, calls=%fused_computation.5 | convolution fusion | flops 805306368 | bytes 5636096 | tf_op jit(solution)/shard_map/dot_general | solution.py:21
  136.9 1.1 fusion.1
  138.0 1.9 %pad_maximum_fusion = bf16[2,384,2048]{2,1,0:T(8,128)(2,1)} fusion(bf16[1,384,2048]{2,1,0:T(8,128)(2,1)S(1)} %fusion.1, bf16[1,384,2048]{2,1,0:T(8,128)(2,1)S(1)} %fusion), kind=kLoop, calls=%fused_computation | loop fusion | flops 1572864 | bytes 6291456 | tf_op jit(solution)/shard_map/stack | solution.py:175
  139.9 37.2 %reduce-scatter.2.cloned.1.call-done = bf16[2,384,512]{2,1,0:T(8,128)(2,1)} async-done(((bf16[2,384,2048]{2,1,0:T(8,128)(2,1)}), bf16[2,384,512]{2,1,0:T(8,128)(2,1)}) %reduce-scatter.2.cloned.1.call-update) | async-done | bytes 786448 | tf_op jit(solution)/shard_map/reduce_scatter | solution.py:176
  177.1 1.2 dynamic-slice_bitcast_fusion.1
  178.3 0.7 collective-permute-start.2
  179.0 1.3 collective-permute-done.2
  180.4 1.2 maximum_select_fusion
  (22 shorter events, 0.6 us)
Async XLA Ops:
  6.5 1.4 copy-start
  6.5 89.7 %all-gather.2.cloned.1.call-start = ((), (), s32[]{:S(2)}) async-start(), calls=%async_computation.3 | async-start | bytes 3932160 | tf_op jit(solution)/shard_map/all_gather | solution.py:147
  11.6 20.6 %all-to-all-start = ((s32[32,1,2]{2,1,0:T(1,128)}), s32[32,1,2]{2,1,0:T(1,128)S(1)}, u32[]{:S(2)}, u32[]{:S(2)}) async-start(s32[32,1,2]{2,1,0:T(1,128)} %bitcast.2), calls=%async_computation | async-start | bytes 32768 | tf_op jit(solution)/shard_map/all_to_all | solution.py:138
  34.7 1.3 copy-start.1
  36.0 7.1 %copy-start.3 = (bf16[768,512]{1,0:T(8,128)(2,1)S(1)}, bf16[768,512]{1,0:T(8,128)(2,1)}, u32[]{:S(2)}) copy-start(bf16[768,512]{1,0:T(8,128)(2,1)} %param.11) | copy-start | bytes 2359300
  36.0 52.1 %all-to-all-start.1 = ((bf16[32,2,64,256]{3,2,1,0:T(8,128)(2,1)}), bf16[32,2,64,256]{3,2,1,0:T(8,128)(2,1)}, u32[]{:S(2)}, u32[]{:S(2)}) async-start(bf16[32,2,64,256]{3,2,1,0:T(8,128)(2,1)} %bitcast.30), calls=%async_computation.1 | async-start | bytes 4194304 | tf_op jit(solution)/shard_map/all_to_all | solution.py:142
  40.9 136.2 %reduce-scatter.2.cloned.1.call-start = ((), (), s32[]{:S(2)}) async-start(), calls=%async_computation.4 | async-start | bytes 3932160 | tf_op jit(solution)/shard_map/reduce_scatter | solution.py:176
  41.0 60.4 %collective-permute-start = (bf16[4096,512]{1,0:T(8,128)(2,1)}, bf16[4096,512]{1,0:T(8,128)(2,1)}, u32[]{:S(2)}, u32[]{:S(2)}) collective-permute-start(bf16[4096,512]{1,0:T(8,128)(2,1)} %bitcast.33), channel_id=1, source_target_pairs={{0,128},{128,0},{1,129},{129,1},{2,130},{130,2},{3,131},{131,3},{4... | collective-permute-start | bytes 12582920 | tf_op jit(solution)/shard_map/ppermute | solution.py:17
  89.8 15.5 %collective-permute-start.1 = (bf16[12,64,256]{2,1,0:T(8,128)(2,1)S(1)}, bf16[12,64,256]{2,1,0:T(8,128)(2,1)S(1)}, u32[]{:S(2)}, u32[]{:S(2)}) collective-permute-start(bf16[12,64,256]{2,1,0:T(8,128)(2,1)S(1)} %pick_blocks.5), channel_id=1, source_target_pairs={{0,128},{128,0},{1,129},{129,1},{2,130},{130,2},{3,131},{131,3},{4... | collective-permute-start | bytes 1179656 | tf_op jit(solution)/shard_map/ppermute | solution.py:17
  96.2 5.1 %copy-start.4 = (bf16[384,4096]{1,0:T(8,128)(2,1)S(1)}, bf16[384,4096]{1,0:T(8,128)(2,1)}, u32[]{:S(2)}) copy-start(bf16[384,4096]{1,0:T(8,128)(2,1)} %all-gather.2.cloned.1.call-done) | copy-start | bytes 9437188
  130.4 2.8 %copy-start.2 = (bf16[1,4096,512]{2,1,0:T(8,128)(2,1)S(1)}, bf16[1,4096,512]{2,1,0:T(8,128)(2,1)}, u32[]{:S(2)}) copy-start(bf16[1,4096,512]{2,1,0:T(8,128)(2,1)} %param.7) | copy-start | bytes 12582916
  178.3 2.1 %collective-permute-start.2 = (bf16[384,512]{1,0:T(8,128)(2,1)S(1)}, bf16[384,512]{1,0:T(8,128)(2,1)S(1)}, u32[]{:S(2)}, u32[]{:S(2)}) collective-permute-start(bf16[384,512]{1,0:T(8,128)(2,1)S(1)} %get-tuple-element.10), channel_id=1, source_target_pairs={{0,128},{128,0},{1,129},{129,1},{2,130},{130,2},{3,131},{131,3},{4... | collective-permute-start | bytes 1179656 | tf_op jit(solution)/shard_map/ppermute | solution.py:17
Sparse Core Ops, SparseCore 0:
  9.2 45.8 all-gather.1
  140.0 37.0 reduce-scatter.1

commit v2 on v1

v2 whole, which is shorter than its diff:
```python
import jax
import jax.numpy as jnp
from jax import lax
from jax.experimental import pallas as pl
from jax.experimental.pallas import tpu as pltpu
from jax.sharding import PartitionSpec as P

HD = 128
GROUP = 64
KNB = 2
SCALE = HD ** (-0.5)
MIB = 1024 * 1024
BF16 = jnp.bfloat16


def dot_nt(a, b):
    return lax.dot_general(a, b, (((1,), (1,)), ((), ())), preferred_element_type=jnp.float32)


def dot_tn(a, b):
    return lax.dot_general(a, b, (((0,), (0,)), ((), ())), preferred_element_type=jnp.float32)


def dot_nn(a, b):
    return lax.dot_general(a, b, (((1,), (0,)), ((), ())), preferred_element_type=jnp.float32)


def params(mib=16):
    return pltpu.CompilerParams(vmem_limit_bytes=mib * MIB)


def whole(shape):
    return pl.BlockSpec(shape, lambda *i: (0,) * len(shape))


def glance(array):
    return pl.BlockSpec((1,) * (array.ndim - 2) + (16, HD), lambda *i: (0,) * array.ndim)


def swap_cores(block):
    return lax.ppermute(block, "grp", [(0, 1), (1, 0)])


def shift(block, step):
    count = lax.axis_size("tp")
    return lax.ppermute(block, "tp", [(i, (i + step) % count) for i in range(count)])


def swap(block, mask):
    count = lax.axis_size("tp")
    return lax.ppermute(block, "tp", [(i, i ^ mask) for i in range(count)])


TABLE = 8


def batch_of(owned):
    return 8 if owned % 8 == 0 else owned


def order_matrix(batch, parts, deep, back):
    size = batch * parts * deep
    row = lax.broadcasted_iota(jnp.int32, (size, size), 0)
    column = lax.broadcasted_iota(jnp.int32, (size, size), 1)
    travel, home = (column, row) if back else (row, column)
    where = (travel % batch) * (parts * deep) + travel // batch
    return (home == where).astype(jnp.float32).astype(BF16)


def table_rows(owner, slot, owned, half):
    batch = batch_of(owned)
    groups = owner.shape[0]
    number = KNB * lax.broadcasted_iota(jnp.int32, (groups, half), 0)
    column = lax.broadcasted_iota(jnp.int32, (groups, half), 1)
    rows = []
    for values in (slot // batch, owner * batch + slot % batch):
        row = jnp.zeros((1, half), jnp.int32)
        for k in range(KNB):
            spread = jnp.where(column == number + k, values[:, k : k + 1], 0)
            row = row + jnp.sum(spread, axis=0, keepdims=True)
        rows.append(row)
    which = lax.broadcasted_iota(jnp.int32, (TABLE, half), 0)
    table = jnp.where(which == 0, rows[0], jnp.where(which == 1, rows[1], 0))
    return table.astype(jnp.float32).astype(BF16)


def pack_kernel(batch, place_ref, owner_ref, slot_ref, neigh_ref, out_ref):
    owned, rows, half = neigh_ref.shape
    parts = out_ref.shape[0]
    deep = rows // parts
    chooser = order_matrix(batch, parts, deep, False)
    for first in range(0, owned, batch):
        block = neigh_ref[first : first + batch].reshape(batch * rows, half)
        moved = dot_nn(chooser, block).astype(BF16).reshape(parts, deep * batch, half)
        out_ref[:, first * deep : (first + batch) * deep] = moved
    table = table_rows(owner_ref[...], slot_ref[...], owned, half)
    out_ref[:, owned * deep :] = jnp.broadcast_to(table[None], (parts, TABLE, half))


def pack_rows(place, owner, slot, neighbours, parts):
    owned, rows, features = neighbours.shape
    half = features // 2
    message = owned * (rows // parts) + TABLE
    batch = batch_of(owned)
    return pl.pallas_call(
        lambda *refs: pack_kernel(batch, *refs),
        grid_spec=pltpu.PrefetchScalarGridSpec(
            num_scalar_prefetch=1,
            grid=(1,),
            in_specs=[whole(owner.shape)] * 2
            + [pl.BlockSpec((owned, rows, half), lambda i, s: (0, 0, s[0]))],
            out_specs=whole((parts, message, half)),
        ),
        out_shape=jax.ShapeDtypeStruct((parts, message, half), BF16),
        compiler_params=params(60),
        name="pack_rows",
    )(place, owner, slot, neighbours)


def route_kernel(owned, batch, held_ref, *refs):
    out_ref = refs[-1]
    owners, message, half = held_ref.shape
    deep = (message - TABLE) // owned
    total = owners * owned
    table = held_ref[:, owned * deep :, :].astype(jnp.float32).reshape(owners * TABLE, half)[:, :HD].T
    held = []
    for first in range(0, owned, batch):
        block = held_ref[:, first * deep : (first + batch) * deep].astype(jnp.float32)
        rows = [block[:, r * batch : (r + 1) * batch].reshape(owners * batch, half) for r in range(deep)]
        held.append(jnp.concatenate(rows, axis=1).astype(BF16))
    held = jnp.concatenate(held, axis=0)
    columns = lax.broadcasted_iota(jnp.int32, (owned, total), 1).astype(jnp.float32)
    per_dot = min(8, owners)
    for start in range(0, owners, per_dot):
        choose = []
        for s in range(start, start + per_dot):
            high = table[:owned, s * TABLE : s * TABLE + 1]
            low = table[:owned, s * TABLE + 1 : s * TABLE + 2]
            choose.append((high * float(owners * batch) + low == columns).astype(jnp.float32))
        moved = dot_nn(jnp.concatenate(choose, axis=0).astype(BF16), held).reshape(per_dot, owned, deep * half)
        for first in range(0, owned, batch):
            rows = [moved[:, first : first + batch, r * half : (r + 1) * half] for r in range(deep)]
            place = pl.ds(first * deep, batch * deep)
            out_ref[start : start + per_dot, place] = jnp.concatenate(rows, axis=1).astype(BF16)


def route_rows(held, owned, after):
    owners, message, half = held.shape
    batch = batch_of(owned)
    out_shape = (owners, message - TABLE, half)
    return pl.pallas_call(
        lambda *refs: route_kernel(owned, batch, *refs),
        grid=(1,),
        out_shape=jax.ShapeDtypeStruct(out_shape, BF16),
        in_specs=[whole(held.shape)] + [glance(x) for x in after],
        out_specs=whole(out_shape),
        compiler_params=params(),
        name="route_rows",
    )(held, *after)


def unpack_kernel(owned, batch, place_ref, arrived_ref, *refs):
    keep_ref, give_ref = refs[-2:]
    parts, message, half = arrived_ref.shape
    deep = message // owned
    rows = parts * deep
    chooser = order_matrix(batch, parts, deep, True)
    mine = owned // 2
    side = place_ref[0]
    for first in range(0, owned, batch):
        block = arrived_ref[:, first * deep : (first + batch) * deep].reshape(batch * rows, half)
        sorted_rows = dot_nn(chooser, block).astype(BF16)
        for n in range(first, first + batch, KNB):
            group = sorted_rows[(n - first) * rows : (n - first + KNB) * rows]
            place = pl.ds(n % mine * rows, KNB * rows)

            @pl.when(side == n // mine)
            def _():
                keep_ref[place] = group

            @pl.when(side != n // mine)
            def _():
                give_ref[place] = group


def unpack_rows(place, arrived, owned, rows, after):
    parts, message, half = arrived.shape
    batch = batch_of(owned)
    out_shape = (owned // 2 * rows, half)
    return pl.pallas_call(
        lambda *refs: unpack_kernel(owned, batch, *refs),
        grid_spec=pltpu.PrefetchScalarGridSpec(
            num_scalar_prefetch=1,
            grid=(1,),
            in_specs=[whole(arrived.shape)] + [glance(x) for x in after],
            out_specs=[whole(out_shape)] * 2,
        ),
        out_shape=[jax.ShapeDtypeStruct(out_shape, BF16)] * 2,
        compiler_params=params(),
        name="unpack_rows",
    )(place, arrived, *after)


def project_kernel(place_ref, *refs):
    blocks, (own_w, other_w, own_out, other_out) = refs[:-4], refs[-4:]
    step = pl.program_id(0)
    for k, block_ref in enumerate(blocks):

        @pl.when(step == k)
        def _():
            block = block_ref[...]
            own = dot_nn(block, own_w[...])
            other = dot_nn(block, other_w[...])
            own_out[...] = own if k == 0 else own_out[...] + own
            other_out[...] = other if k == 0 else other_out[...] + other


def project_last_kernel(place_ref, *refs):
    pieces, (own_in, other_in, own_w, other_w, own_out, other_out) = refs[:-6], refs[-6:]
    first = 0
    for piece_ref in pieces:
        piece = piece_ref[...]
        rows = slice(first, first + piece.shape[0])
        own_out[rows] = (own_in[rows] + dot_nn(piece, own_w[...])).astype(BF16)
        other_out[rows] = (other_in[rows] + dot_nn(piece, other_w[...])).astype(BF16)
        first += piece.shape[0]


def project(place, masks, blocks, own_weight, other_weight, sums=None):
    depth = blocks[0].shape[1]
    width = own_weight.shape[1]
    final = sums is not None
    tokens = sum(x.shape[0] for x in blocks) if final else blocks[0].shape[0]

    def mask_of(k):
        return sum(jnp.where(k == i, m, 0) for i, m in enumerate(masks))

    weight_spec = pl.BlockSpec((depth, width), lambda k, s: (s[1] ^ mask_of(k), 0))
    out_spec = whole((tokens, width))
    shape = jax.ShapeDtypeStruct((tokens, width), BF16 if final else jnp.float32)
    return pl.pallas_call(
        project_last_kernel if final else project_kernel,
        grid_spec=pltpu.PrefetchScalarGridSpec(
            num_scalar_prefetch=1,
            grid=(len(masks),),
            in_specs=[whole(x.shape) for x in blocks] + [out_spec] * (2 * final) + [weight_spec] * 2,
            out_specs=[out_spec] * 2,
        ),
        out_shape=[shape, shape],
        compiler_params=params(60),
        name="project",
    )(place, *blocks, *(sums or ()), own_weight, other_weight)


def heads_gradients(items):
    queries, memory, inputs, grad_out = zip(*items)
    count = range(len(items))
    scores = [dot_nt(memory[i], inputs[i]) * SCALE for i in count]
    scores = [jnp.exp(s - jnp.max(s, axis=0, keepdims=True)) for s in scores]
    enc_probs = [s * (1.0 / jnp.sum(s, axis=0, keepdims=True)) for s in scores]
    enc_weights = [p.astype(BF16) for p in enc_probs]
    mixed = [dot_tn(enc_weights[i], memory[i]) for i in count]
    keys = [(inputs[i].astype(jnp.float32) + mixed[i]).astype(BF16) for i in count]
    scores = [dot_nt(queries[i], keys[i]) * SCALE for i in count]
    grad_probs = [dot_nt(grad_out[i], keys[i]) for i in count]
    scores = [jnp.exp(s - jnp.max(s, axis=1, keepdims=True)) for s in scores]
    probs = [s * (1.0 / jnp.sum(s, axis=1, keepdims=True)) for s in scores]
    weights = [p.astype(BF16) for p in probs]
    from_values = [dot_tn(weights[i], grad_out[i]) for i in count]
    grad_scores = [p * (g - jnp.sum(p * g, axis=1, keepdims=True)) for p, g in zip(probs, grad_probs)]
    grad_scores = [g.astype(BF16) for g in grad_scores]
    grad_keys = [dot_tn(grad_scores[i], queries[i]) * SCALE + from_values[i] for i in count]
    grad_keys = [g.astype(BF16) for g in grad_keys]
    grad_queries = [(dot_nn(grad_scores[i], keys[i]) * SCALE).astype(BF16) for i in count]
    grad_probs = [dot_nt(memory[i], grad_keys[i]) for i in count]
    from_values = [dot_nn(enc_weights[i], grad_keys[i]) for i in count]
    grad_scores = [p * (g - jnp.sum(p * g, axis=0, keepdims=True)) for p, g in zip(enc_probs, grad_probs)]
    grad_scores = [g.astype(BF16) for g in grad_scores]
    grad_memory = [(dot_nn(grad_scores[i], inputs[i]) * SCALE + from_values[i]).astype(BF16) for i in count]
    return grad_queries, grad_memory


def attend_kernel(
    tp_count, far_step, place_ref, own_ref, other_ref, cot_ref, near_ref, far_ref, own_hbm, other_hbm,
    grad_own_ref, grad_other_ref, low_ref, high_ref, weights, arrived,
):
    step = pl.program_id(0)
    side = place_ref[0]
    columns = weights.shape[1]
    target = (place_ref[1] + far_step) % tp_count
    copies = [
        pltpu.make_async_copy(
            hbm.at[pl.ds(pl.multiple_of((target + core * tp_count) * columns, columns), columns)],
            weights.at[2 * core + i],
            arrived.at[2 * core + i],
        )
        for core in range(2)
        for i, hbm in enumerate((own_hbm, other_hbm))
    ]

    @pl.when(step == 0)
    def _():
        for copy in copies:
            copy.start()

    half = near_ref.shape[1]
    first = side == 0
    tokens = own_ref.shape[0]
    groups = tokens // GROUP
    keys = near_ref.shape[0] // groups
    items, spots = [], []
    for c in range(groups):
        rows = slice(c * GROUP, (c + 1) * GROUP)
        place = pl.ds(pl.multiple_of(step * tokens + c * GROUP, GROUP), GROUP)
        for far, held_ref in enumerate((near_ref, far_ref)):
            start = ((side + far) % 2) * half
            for low in range(0, half, HD):
                lanes = pl.ds(pl.multiple_of(start + low, HD), HD)
                own = own_ref[rows, lanes]
                other = other_ref[rows, lanes]
                items.append(
                    (
                        jnp.where(first, own, other),
                        jnp.where(first, other, own),
                        held_ref[c * keys : (c + 1) * keys, low : low + HD],
                        cot_ref[rows, lanes],
                    )
                )
                spots.append((place, lanes))
    grad_queries, grad_memory = heads_gradients(items)
    for spot, grad_q, grad_m in zip(spots, grad_queries, grad_memory):
        grad_own_ref[spot] = jnp.where(first, grad_q, grad_m)
        grad_other_ref[spot] = jnp.where(first, grad_m, grad_q)

    @pl.when(step == pl.num_programs(0) - 1)
    def _():
        for copy in copies:
            copy.wait()
        low_rows = low_ref.shape[0]
        grad_own, grad_other = grad_own_ref[...], grad_other_ref[...]
        for core in range(2):
            term = dot_nt(grad_own, weights[2 * core]) + dot_nt(grad_other, weights[2 * core + 1])
            term = term.astype(BF16)
            low_ref[:, core * columns : (core + 1) * columns] = term[:low_rows]
            high_ref[:, core * columns : (core + 1) * columns] = term[low_rows:]


def attend(place, own, other, cotangent, near, far, own_weight, other_weight):
    tokens, width = own.shape
    rows, half = near.shape
    groups = tokens // GROUP
    steps = groups // 3 if groups % 3 == 0 else groups
    tp_count = lax.axis_size("tp")
    columns = own_weight.shape[0] // (2 * tp_count)
    token_spec = pl.BlockSpec((tokens // steps, width), lambda c, s: (c, 0))
    cot_spec = pl.BlockSpec((tokens // steps, width), lambda c, s: (s[0] * steps + c, 0))
    neigh_spec = pl.BlockSpec((rows // steps, half), lambda c, s: (c, 0))
    outs = [(tokens, width)] * 2 + [(tokens // 2, 2 * columns)] * 2
    return pl.pallas_call(
        lambda *refs: attend_kernel(tp_count, tp_count // 2, *refs),
        grid_spec=pltpu.PrefetchScalarGridSpec(
            num_scalar_prefetch=1,
            grid=(steps,),
            in_specs=[token_spec] * 2 + [cot_spec] + [neigh_spec] * 2 + [pl.BlockSpec(memory_space=pl.ANY)] * 2,
            out_specs=[whole(shape) for shape in outs],
            scratch_shapes=[pltpu.VMEM((4, columns, width), BF16), pltpu.SemaphoreType.DMA((4,))],
        ),
        out_shape=[jax.ShapeDtypeStruct(shape, BF16) for shape in outs],
        compiler_params=params(57),
        name="attend",
    )(place, own, other, cotangent, near, far, own_weight, other_weight)


def partial_kernel(steps, place_ref, own_ref, other_ref, own_a, own_b, other_a, other_b, *out_refs):
    columns = own_a.shape[0]
    low_rows = own_ref.shape[0] // 2
    for i in range(len(steps)):

        @pl.when(pl.program_id(0) == i)
        def _():
            own, other = own_ref[...], other_ref[...]
            for core, weights in enumerate(((own_a, other_a), (own_b, other_b))):
                term = dot_nt(own, weights[0][...]) + dot_nt(other, weights[1][...])
                term = term.astype(BF16)
                place = slice(core * columns, (core + 1) * columns)
                out_refs[2 * i][:, place] = term[:low_rows]
                out_refs[2 * i + 1][:, place] = term[low_rows:]


def partial_terms(place, steps, grad_own, grad_other, own_weight, other_weight):
    tokens, width = grad_own.shape
    tp_count = lax.axis_size("tp")
    columns = own_weight.shape[0] // (2 * tp_count)

    def weight_spec(core):
        def index(i, s):
            step = sum(jnp.where(i == u, step, 0) for u, step in enumerate(steps))
            return ((s[1] + step) % tp_count + core * tp_count, 0)

        return pl.BlockSpec((columns, width), index)

    shape = (tokens // 2, 2 * columns)
    return pl.pallas_call(
        lambda *refs: partial_kernel(steps, *refs),
        grid_spec=pltpu.PrefetchScalarGridSpec(
            num_scalar_prefetch=1,
            grid=(len(steps),),
            in_specs=[whole((tokens, width))] * 2 + [weight_spec(0), weight_spec(1)] * 2,
            out_specs=[whole(shape)] * (2 * len(steps)),
        ),
        out_shape=[jax.ShapeDtypeStruct(shape, BF16)] * (2 * len(steps)),
        compiler_params=params(57),
        name="partial_terms",
    )(place, grad_own, grad_other, own_weight, own_weight, other_weight, other_weight)


def add_terms(a, b):
    return (a.astype(jnp.float32) + b.astype(jnp.float32)).astype(BF16)


def scatter_ring(place, across_low, across_high, *operands):
    if lax.axis_size("tp") == 2:
        own_low, own_high = partial_terms(place, (0,), *operands)
        return [own_low, shift(across_low, 1)], [own_high, shift(across_high, 1)]
    rising = shift(across_low, 1)
    falling = shift(across_high, -1)
    up_low, up_high, down_low, down_high, own_low, own_high = partial_terms(place, (1, 3, 0), *operands)
    up_high = shift(up_high, 1)
    down_low = shift(down_low, -1)
    up_low = shift(add_terms(up_low, rising), 1)
    down_high = shift(add_terms(down_high, falling), -1)
    return [own_low, down_low, up_low], [own_high, up_high, down_high]


def sum_terms(terms):
    return sum(term[...].astype(jnp.float32) for term in terms).astype(BF16)


def give_kernel(place_ref, *refs):
    terms, out_ref = refs[:-1], refs[-1]
    count, rows = len(terms) // 2, terms[0].shape[0]
    out_ref[:rows] = sum_terms(terms[:count])
    out_ref[rows:] = sum_terms(terms[count:])


def keep_kernel(place_ref, *refs):
    terms, received_ref, out_ref = refs[:-2], refs[-2], refs[-1]
    count, rows = len(terms) // 2, terms[0].shape[0]
    side = place_ref[0]
    mine = pl.multiple_of(side * 2 * rows, 2 * rows)
    other = pl.multiple_of((1 - side) * 2 * rows, 2 * rows)
    out_ref[pl.ds(mine, rows)] = sum_terms(terms[:count])
    out_ref[pl.ds(mine + rows, rows)] = sum_terms(terms[count:])
    out_ref[pl.ds(other, 2 * rows)] = received_ref[...]


def sum_columns(place, lows, highs, received=None):
    rows, columns = lows[0].shape[0], lows[0].shape[1] // 2
    give = received is None
    extra = [] if give else [received]
    spec = pl.BlockSpec((rows, columns), lambda i, s: (0, 1 - s[0] if give else s[0]))
    out_shape = ((2 if give else 4) * rows, columns)
    return pl.pallas_call(
        give_kernel if give else keep_kernel,
        grid_spec=pltpu.PrefetchScalarGridSpec(
            num_scalar_prefetch=1,
            grid=(1,),
            in_specs=[spec] * len(lows + highs) + [whole(x.shape) for x in extra],
            out_specs=whole(out_shape),
        ),
        out_shape=jax.ShapeDtypeStruct(out_shape, BF16),
        compiler_params=params(),
        name="sum_columns",
    )(place, *lows, *highs, *extra)


def shards(states, projections, neighbours, owner, slot, cotangent):
    side = lax.axis_index("grp").astype(jnp.int32)
    place = jnp.stack([side, lax.axis_index("tp").astype(jnp.int32)])
    shards_ = lax.axis_size("seq")
    tp_count = lax.axis_size("tp")
    tokens = states.shape[0] // 2
    owned, rows, features = neighbours.shape

    held = lax.dynamic_slice_in_dim(states, side * tokens, tokens, 0)
    if tp_count == 2:
        blocks, masks, last = [held], [0], [swap(held, 1)]
    else:
        low = tokens // 2
        blocks, masks = [held, swap(held, 1), swap(held, 3)], [0, 1, 3]
        last = [swap(blocks[2][:low], 1), swap(blocks[1][low:], 3)]
    own_weight = projections[0]
    other_weight = swap_cores(own_weight)
    packed = pack_rows(place, owner, slot, neighbours, shards_)
    parts = lax.all_to_all(packed, "seq", split_axis=0, concat_axis=0, tiled=True)
    routed = route_rows(parts, owned, [block[:16, :HD] for block in blocks[1:]])
    arrived = lax.all_to_all(routed, "seq", split_axis=0, concat_axis=0, tiled=True)

    sums = project(place, masks, blocks, own_weight, other_weight)
    own, other = project(place, [tp_count // 2], last, own_weight, other_weight, sums)
    near, give = unpack_rows(place, arrived, owned, rows, [own[:16, :HD]])
    far = swap_cores(give)
    grad_own, grad_other, across_low, across_high = attend(
        place, own, other, cotangent, near, far, own_weight, other_weight
    )
    lows, highs = scatter_ring(place, across_low, across_high, grad_own, grad_other, own_weight, other_weight)

    received = swap_cores(sum_columns(place, lows, highs))
    return sum_columns(place, lows, highs, received)


def solution(mesh):
    return jax.shard_map(
        shards,
        mesh=mesh,
        in_specs=(
            P("seq", "tp"),
            P("grp", None, "tp"),
            P("seq", None, "tp"),
            P("seq", None),
            P("seq", None),
            P("seq", "tp"),
        ),
        out_specs=P("seq", ("grp", "tp")),
        check_vma=False,
    )
```

time: 189 us -> 128 us (0.68)
  waiting for transfers between devices: 90.9 us -> 38.6 us
  matrix products: 16.5 us -> 0 us
  starting transfers between devices: 24.4 us -> 38.8 us
  between operations: 13.6 us -> 0.15 us
  Pallas kernels: 29.6 us -> 38.4 us
    all_to_all x2, waiting for transfers between devices: 52.3 us -> 3.82 us  [the longest x1 2.55 us: shards(): lax.all_to_all(packed, 'seq', split_axis=0, concat_axis=0, tiled=True)]
    reduce_scatter x1 -> x0, waiting for transfers between devices: 37.2 us -> none  [shards(): lax.psum_scatter(partial_term, 'tp', scatter_dimension=2, tiled=True)]
    ppermute x0 -> x10, waiting for transfers between devices: none -> 32.1 us  [the longest x4 18 us: swap(): return lax.ppermute(block, 'tp', [(i, i ^ mask) for i in range(count)])]
    dot_general x6 -> x0, matrix products: 16.5 us -> none  [the longest x4 7.48 us: dot_nt(): lax.dot_general(a, b, (((1,), (1,)), ((), ())), preferred_element_type=jn...]
    ppermute x0 -> x10, starting transfers between devices: none -> 13.1 us  [the longest x6 7.65 us: shift(): lax.ppermute(block, 'tp', [(i, (i + step) % count) for i in range(count)])]
    pallas_call x4 -> x9, Pallas kernels: 29.6 us -> 38.4 us  [the longest x2 12.4 us: project(): pl.pallas_call(project_last_kernel if final else project_kernel, grid_spe...]
    slice x0 -> x5, local copies, waits for them, and re-layouts: none -> 2.72 us  [the longest x2 2.05 us: shards(): last = [swap(blocks[2][:low], 1), swap(blocks[1][low:], 3)]]
    ppermute x3, starting transfers between devices: 7.46 us -> 9.83 us  [swap_cores(): return lax.ppermute(block, 'grp', [(0, 1), (1, 0)])]
  transfers between devices with their start and end apart: 7 -> 15, of which waited for: 4 -> 11; matrix products, arithmetic and copies ran while one was open for 7% -> 7% of each run, Pallas kernels for 2% -> 20%
where the time goes in v2:
time: 128 us; the launch traced here: 127 us
  starting transfers between devices  38.8 us (30%)
  waiting for transfers between devices  38.6 us (30%)
  Pallas kernels  38.4 us (30%)
  local copies, waits for them, and re-layouts  8.65 us (7%)
  other arithmetic  2.85 us (2%)
    ppermute x4, waiting for transfers between devices, swap(): return lax.ppermute(block, 'tp', [(i, i ^ mask) for i in range(count)])  18 us
    ppermute x6, waiting for transfers between devices, shift(): lax.ppermute(block, 'tp', [(i, (i + step) % count) for i in range(count)])  14.1 us
    pallas_call x2, Pallas kernels, project(): pl.pallas_call(project_last_kernel if final else project_kernel, grid_spe...  12.4 us
    ppermute x3, starting transfers between devices, swap_cores(): return lax.ppermute(block, 'grp', [(0, 1), (1, 0)])  9.83 us
    all_to_all x1, starting transfers between devices, shards(): lax.all_to_all(packed, 'seq', split_axis=0, concat_axis=0, tiled=True)  9.47 us
    pallas_call x1, Pallas kernels, attend(): pl.pallas_call(lambda *refs: attend_kernel(tp_count, tp_count // 2, *refs...  9.14 us
    ppermute x6, starting transfers between devices, shift(): lax.ppermute(block, 'tp', [(i, (i + step) % count) for i in range(count)])  7.65 us
    pallas_call x1, Pallas kernels, partial_terms(): pl.pallas_call(lambda *refs: partial_kernel(steps, *refs), grid_spec=pltp...  7.57 us
  transfers between devices with their start and end apart: 15, of which 11 were waited for; matrix products, arithmetic and copies ran while one was open for 7% of the time, Pallas kernels for 20%

profile of v2, /device:TPU:1, one launch (start us, length us, event | category | flops | bytes accessed | tf_op | source)
XLA Modules:
  0.0 127.5 jit_solution(1151402378727336414)
XLA Ops:
  0.0 3.2 %collective-permute-start.4 = (bf16[4096,512]{1,0:T(8,128)(2,1)}, bf16[4096,512]{1,0:T(8,128)(2,1)}, u32[]{:S(2)}, u32[]{:S(2)}) collective-permute-start(bf16[4096,512]{1,0:T(8,128)(2,1)} %bitcast.3), channel_id=1, source_target_pairs={{0,128},{128,0},{1,129},{129,1},{2,130},{130,2},{3,131},{131,3},{4... | collective-permute-start | bytes 12582920 | tf_op jit(solution)/shard_map/ppermute | solution.py:41
  3.2 1.4 %copy.7.refs_1_ = s32[12,2]{1,0:T(8,128)} copy(s32[12,2]{0,1:T(2,128)} %param.9) | data formatting | bytes 192 | tf_op args[3]
  4.6 1.4 %copy.8.refs_2_ = s32[12,2]{1,0:T(8,128)} copy(s32[12,2]{0,1:T(2,128)} %param.10) | data formatting | bytes 192 | tf_op args[4]
  6.6 3.4 %pack_rows.1 = bf16[32,56,256]{2,1,0:T(8,128)(2,1)} custom-call(s32[2]{0:T(128)} %pad_add_fusion.place_ref.refs_0_, s32[12,2]{1,0:T(8,128)} %copy.7.refs_1_, s32[12,2]{1,0:T(8,128)} %copy.8.refs_2_, bf16[24,64,512]{2,1,0:T(8,128)(2,1)} %refs_3_.2), custom_call_target="tpu_custom_call" | custom-call | tf_op jit(solution)/shard_map/pack_rows/pallas_call | solution.py:105
  9.9 9.5 %all-to-all-start = ((bf16[32,56,256]{2,1,0:T(8,128)(2,1)}), bf16[32,56,256]{2,1,0:T(8,128)(2,1)S(1)}, u32[]{:S(2)}, u32[]{:S(2)}) async-start(bf16[32,56,256]{2,1,0:T(8,128)(2,1)} %pack_rows.1), calls=%async_computation | async-start | bytes 1835008 | tf_op jit(solution)/shard_map/all_to_all | solution.py:495
  19.5 1.3 %collective-permute-start.2 = (bf16[384,1024]{1,0:T(8,128)(2,1)S(1)}, bf16[384,1024]{1,0:T(8,128)(2,1)S(1)}, u32[]{:S(2)}, u32[]{:S(2)}) collective-permute-start(bf16[384,1024]{1,0:T(8,128)(2,1)S(1)} %constant_dynamic-slice_fusion.refs_0_), channel_id=1, source_target_pairs={{0,1},{1,0},{2,3},{3,2},{4,5},{5,4},{6,7},{7,6},{8,9},{9,8},{10,11... | collective-permute-start | bytes 2359304 | tf_op jit(solution)/shard_map/ppermute | solution.py:51
  20.8 1.8 %collective-permute-start = (bf16[384,1024]{1,0:T(8,128)(2,1)S(1)}, bf16[384,1024]{1,0:T(8,128)(2,1)S(1)}, u32[]{:S(2)}, u32[]{:S(2)}) collective-permute-start(bf16[384,1024]{1,0:T(8,128)(2,1)S(1)} %constant_dynamic-slice_fusion.refs_0_), channel_id=1, source_target_pairs={{0,3},{1,2},{2,1},{3,0},{4,7},{5,6},{6,5},{7,4},{8,11},{9,10},{10,... | collective-permute-start | bytes 2359304 | tf_op jit(solution)/shard_map/ppermute | solution.py:51
  22.6 15.7 %collective-permute-done.2.refs_1_ = bf16[384,1024]{1,0:T(8,128)(2,1)S(1)} collective-permute-done((bf16[384,1024]{1,0:T(8,128)(2,1)S(1)}, bf16[384,1024]{1,0:T(8,128)(2,1)S(1)}, u32[]{:S(2)}, u32[]{:S(2)}) %collective-permute-start.2) | collective-permute-done | bytes 786464 | tf_op jit(solution)/shard_map/ppermute | solution.py:51
  38.3 2.1 %collective-permute-done.refs_2_ = bf16[384,1024]{1,0:T(8,128)(2,1)S(1)} collective-permute-done((bf16[384,1024]{1,0:T(8,128)(2,1)S(1)}, bf16[384,1024]{1,0:T(8,128)(2,1)S(1)}, u32[]{:S(2)}, u32[]{:S(2)}) %collective-permute-start) | collective-permute-done | bytes 786464 | tf_op jit(solution)/shard_map/ppermute | solution.py:51
  41.3 2.5 %all-to-all-done.refs_0_ = bf16[32,56,256]{2,1,0:T(8,128)(2,1)S(1)} async-done(((bf16[32,56,256]{2,1,0:T(8,128)(2,1)}), bf16[32,56,256]{2,1,0:T(8,128)(2,1)S(1)}, u32[]{:S(2)}, u32[]{:S(2)}) %all-to-all-start) | async-done | bytes 917536 | tf_op jit(solution)/shard_map/all_to_all | solution.py:495
  43.8 1.9 %route_rows.1 = bf16[32,48,256]{2,1,0:T(8,128)(2,1)} custom-call(bf16[32,56,256]{2,1,0:T(8,128)(2,1)S(1)} %all-to-all-done.refs_0_, bf16[16,128]{1,0:T(8,128)(2,1)S(1)} %slice.22.refs_1_, bf16[16,128]{1,0:T(8,128)(2,1)S(1)} %slice.23.refs_2_), custom_call_target="tpu_custom_call" | custom-call | tf_op jit(solution)/shard_map/route_rows/pallas_call | solution.py:151
  45.7 6.3 %all-to-all-start.1 = ((bf16[32,48,256]{2,1,0:T(8,128)(2,1)}), bf16[32,48,256]{2,1,0:T(8,128)(2,1)S(1)}, u32[]{:S(2)}, u32[]{:S(2)}) async-start(bf16[32,48,256]{2,1,0:T(8,128)(2,1)} %route_rows.1), calls=%async_computation.1 | async-start | bytes 1572864 | tf_op jit(solution)/shard_map/all_to_all | solution.py:497
  54.5 1.9 %collective-permute-start.3 = (bf16[192,1024]{1,0:T(8,128)(2,1)S(1)}, bf16[192,1024]{1,0:T(8,128)(2,1)S(1)}, u32[]{:S(2)}, u32[]{:S(2)}) collective-permute-start(bf16[192,1024]{1,0:T(8,128)(2,1)S(1)} %slice.21), channel_id=1, source_target_pairs={{0,3},{1,2},{2,1},{3,0},{4,7},{5,6},{6,5},{7,4},{8,11},{9,10},{10,... | collective-permute-start | bytes 1179656 | tf_op jit(solution)/shard_map/ppermute | solution.py:51
  56.4 7.6 %project.2 = (f32[384,512]{1,0:T(8,128)}, f32[384,512]{1,0:T(8,128)}) custom-call(s32[2]{0:T(128)} %pad_add_fusion.place_ref.refs_0_, bf16[384,1024]{1,0:T(8,128)(2,1)} %copy-done.6, bf16[384,1024]{1,0:T(8,128)(2,1)} %copy-done.7, bf16[384,1024]{1,0:T(8,128)(2,1)} %copy-done.8, bf16[4096,512]{1,0:T(8,128)(2,1)} %bitcast.4, ...), custom_call_target="tpu_custom_call" | custom-call | tf_op jit(solution)/shard_map/project/pallas_call | solution.py:241
  65.0 4.8 %project.3 = (bf16[384,512]{1,0:T(8,128)(2,1)}, bf16[384,512]{1,0:T(8,128)(2,1)}) custom-call(s32[2]{0:T(128)} %pad_add_fusion.place_ref.refs_0_, bf16[192,1024]{1,0:T(8,128)(2,1)} %copy-done.9, bf16[192,1024]{1,0:T(8,128)(2,1)} %copy-done.10, f32[384,512]{1,0:T(8,128)} %get-tuple-element.21.refs_2_, f32[384,512]{1,0:T(8,128)} %get-tuple-element.22.refs_3_, ...), custom_call_target="tpu_custom_call" | custom-call | tf_op jit(solution)/shard_map/project/pallas_call | solution.py:241
  70.5 1.3 %all-to-all-done.1.refs_1_ = bf16[32,48,256]{2,1,0:T(8,128)(2,1)S(1)} async-done(((bf16[32,48,256]{2,1,0:T(8,128)(2,1)}), bf16[32,48,256]{2,1,0:T(8,128)(2,1)S(1)}, u32[]{:S(2)}, u32[]{:S(2)}) %all-to-all-start.1) | async-done | bytes 786464 | tf_op jit(solution)/shard_map/all_to_all | solution.py:497
  71.7 1.8 %unpack_rows.1 = (bf16[768,256]{1,0:T(8,128)(2,1)S(1)}, bf16[768,256]{1,0:T(8,128)(2,1)S(1)}) custom-call(s32[2]{0:T(128)S(1)} %copy-done.4, bf16[32,48,256]{2,1,0:T(8,128)(2,1)S(1)} %all-to-all-done.1.refs_1_, bf16[16,128]{1,0:T(8,128)(2,1)S(1)} %slice.19.refs_2_), custom_call_target="tpu_custom_call" | custom-call | tf_op jit(solution)/shard_map/unpack_rows/pallas_call | solution.py:190
  74.3 4.4 %collective-permute-start.5 = (bf16[768,256]{1,0:T(8,128)(2,1)S(1)}, bf16[768,256]{1,0:T(8,128)(2,1)S(1)}, u32[]{:S(2)}, u32[]{:S(2)}) collective-permute-start(bf16[768,256]{1,0:T(8,128)(2,1)S(1)} %get-tuple-element.26), channel_id=1, source_target_pairs={{0,128},{128,0},{1,129},{129,1},{2,130},{130,2},{3,131},{131,3},{4... | collective-permute-start | bytes 1179656 | tf_op jit(solution)/shard_map/ppermute | solution.py:41
  78.7 1.3 %collective-permute-done.5.refs_5_ = bf16[768,256]{1,0:T(8,128)(2,1)S(1)} collective-permute-done((bf16[768,256]{1,0:T(8,128)(2,1)S(1)}, bf16[768,256]{1,0:T(8,128)(2,1)S(1)}, u32[]{:S(2)}, u32[]{:S(2)}) %collective-permute-start.5) | collective-permute-done | bytes 393248 | tf_op jit(solution)/shard_map/ppermute | solution.py:41
  80.8 9.1 %attend.1 = (bf16[384,512]{1,0:T(8,128)(2,1)}, bf16[384,512]{1,0:T(8,128)(2,1)}, bf16[192,1024]{1,0:T(8,128)(2,1)}, bf16[192,1024]{1,0:T(8,128)(2,1)}) custom-call(s32[2]{0:T(128)} %pad_add_fusion.place_ref.refs_0_, bf16[384,512]{1,0:T(8,128)(2,1)} %get-tuple-element.23.refs_1_, bf16[384,512]{1,0:T(8,128)(2,1)} %get-tuple-element.24.refs_2_, ...), custom_call_target="tpu_custom_call" | custom-call | tf_op jit(solution)/shard_map/attend/pallas_call | solution.py:359
  89.9 2.1 %collective-permute-start.10 = (bf16[192,1024]{1,0:T(8,128)(2,1)}, bf16[192,1024]{1,0:T(8,128)(2,1)S(1)}, u32[]{:S(2)}, u32[]{:S(2)}) collective-permute-start(bf16[192,1024]{1,0:T(8,128)(2,1)} %get-tuple-element.36), channel_id=1, source_target_pairs={{0,3},{1,0},{2,1},{3,2},{4,7},{5,4},{6,5},{7,6},{8,11},{9,8},{10,9... | collective-permute-start | bytes 1179656 | tf_op jit(solution)/shard_map/ppermute | solution.py:46
  92.0 7.6 %partial_terms.1 = (bf16[192,1024]{1,0:T(8,128)(2,1)}, bf16[192,1024]{1,0:T(8,128)(2,1)}, bf16[192,1024]{1,0:T(8,128)(2,1)}, bf16[192,1024]{1,0:T(8,128)(2,1)}, ...) custom-call(s32[2]{0:T(128)} %pad_add_fusion.place_ref.refs_0_, bf16[384,512]{1,0:T(8,128)(2,1)} %get-tuple-element.27.refs_1_, ...), custom_call_target="tpu_custom_call" | custom-call | tf_op jit(solution)/shard_map/partial_terms/pallas_call | solution.py:403
  99.6 2.8 %collective-permute-start.6 = (bf16[192,1024]{1,0:T(8,128)(2,1)}, bf16[192,1024]{1,0:T(8,128)(2,1)S(1)}, u32[]{:S(2)}, u32[]{:S(2)}) collective-permute-start(bf16[192,1024]{1,0:T(8,128)(2,1)} %get-tuple-element.30), channel_id=1, source_target_pairs={{0,3},{1,0},{2,1},{3,2},{4,7},{5,4},{6,5},{7,6},{8,11},{9,8},{10,9... | collective-permute-start | bytes 1179656 | tf_op jit(solution)/shard_map/ppermute | solution.py:46
  102.3 1.1 add_convert_fusion
  103.5 2.8 %collective-permute-start.11 = (bf16[192,1024]{1,0:T(8,128)(2,1)S(1)}, bf16[192,1024]{1,0:T(8,128)(2,1)S(1)}, u32[]{:S(2)}, u32[]{:S(2)}) collective-permute-start(bf16[192,1024]{1,0:T(8,128)(2,1)S(1)} %add_convert_fusion), channel_id=1, source_target_pairs={{0,3},{1,0},{2,1},{3,2},{4,7},{5,4},{6,5},{7,6},{8,11},{9,8},{10,9... | collective-permute-start | bytes 1179656 | tf_op jit(solution)/shard_map/ppermute | solution.py:46
  107.5 2.7 %collective-permute-done.6.refs_1_ = bf16[192,1024]{1,0:T(8,128)(2,1)S(1)} collective-permute-done((bf16[192,1024]{1,0:T(8,128)(2,1)}, bf16[192,1024]{1,0:T(8,128)(2,1)S(1)}, u32[]{:S(2)}, u32[]{:S(2)}) %collective-permute-start.6) | collective-permute-done | bytes 393248 | tf_op jit(solution)/shard_map/ppermute | solution.py:46
  110.2 3.0 %collective-permute-done.9.refs_4_ = bf16[192,1024]{1,0:T(8,128)(2,1)S(1)} collective-permute-done((bf16[192,1024]{1,0:T(8,128)(2,1)}, bf16[192,1024]{1,0:T(8,128)(2,1)S(1)}, u32[]{:S(2)}, u32[]{:S(2)}) %collective-permute-start.9) | collective-permute-done | bytes 393248 | tf_op jit(solution)/shard_map/ppermute | solution.py:46
  113.2 5.3 %collective-permute-done.11.refs_5_ = bf16[192,1024]{1,0:T(8,128)(2,1)S(1)} collective-permute-done((bf16[192,1024]{1,0:T(8,128)(2,1)S(1)}, bf16[192,1024]{1,0:T(8,128)(2,1)S(1)}, u32[]{:S(2)}, u32[]{:S(2)}) %collective-permute-start.11) | collective-permute-done | bytes 393248 | tf_op jit(solution)/shard_map/ppermute | solution.py:46
  118.5 3.1 %collective-permute-done.8.refs_2_ = bf16[192,1024]{1,0:T(8,128)(2,1)S(1)} collective-permute-done((bf16[192,1024]{1,0:T(8,128)(2,1)S(1)}, bf16[192,1024]{1,0:T(8,128)(2,1)S(1)}, u32[]{:S(2)}, u32[]{:S(2)}) %collective-permute-start.8) | collective-permute-done | bytes 393248 | tf_op jit(solution)/shard_map/ppermute | solution.py:46
  122.3 2.2 %collective-permute-start.12 = (bf16[384,512]{1,0:T(8,128)(2,1)S(1)}, bf16[384,512]{1,0:T(8,128)(2,1)S(1)}, u32[]{:S(2)}, u32[]{:S(2)}) collective-permute-start(bf16[384,512]{1,0:T(8,128)(2,1)S(1)} %sum_columns.2), channel_id=1, source_target_pairs={{0,128},{128,0},{1,129},{129,1},{2,130},{130,2},{3,131},{131,3},{4... | collective-permute-start | bytes 1179656 | tf_op jit(solution)/shard_map/ppermute | solution.py:41
  124.5 1.3 %collective-permute-done.12.refs_6_ = bf16[384,512]{1,0:T(8,128)(2,1)S(1)} collective-permute-done((bf16[384,512]{1,0:T(8,128)(2,1)S(1)}, bf16[384,512]{1,0:T(8,128)(2,1)S(1)}, u32[]{:S(2)}, u32[]{:S(2)}) %collective-permute-start.12) | collective-permute-done | bytes 393248 | tf_op jit(solution)/shard_map/ppermute | solution.py:41
  125.9 1.6 %sum_columns.3 = bf16[768,512]{1,0:T(8,128)(2,1)} custom-call(s32[2]{0:T(128)S(1)} %copy-done.5, bf16[192,1024]{1,0:T(8,128)(2,1)S(1)} %copy-done.1, bf16[192,1024]{1,0:T(8,128)(2,1)S(1)} %collective-permute-done.6.refs_1_, bf16[192,1024]{1,0:T(8,128)(2,1)S(1)} %collective-permute-done.8.refs_2_, bf16[192,1024]{1,0:T(8,128)(2,1)S(1)} %copy-done.2, ...), custom_call_target="tpu_custom_call" | custom-call | tf_op jit(solution)/shard_map/sum_columns/pallas_call | solution.py:463
  (42 shorter events, 9.1 us)
Async XLA Ops:
  0.0 19.4 %copy-start = (bf16[768,1024]{1,0:T(8,128)(2,1)S(1)}, bf16[768,1024]{1,0:T(8,128)(2,1)}, u32[]{:S(2)}) copy-start(bf16[768,1024]{1,0:T(8,128)(2,1)} %param.6) | copy-start | bytes 4718596
  0.0 56.4 %collective-permute-start.4 = (bf16[4096,512]{1,0:T(8,128)(2,1)}, bf16[4096,512]{1,0:T(8,128)(2,1)}, u32[]{:S(2)}, u32[]{:S(2)}) collective-permute-start(bf16[4096,512]{1,0:T(8,128)(2,1)} %bitcast.3), channel_id=1, source_target_pairs={{0,128},{128,0},{1,129},{129,1},{2,130},{130,2},{3,131},{131,3},{4... | collective-permute-start | bytes 12582920 | tf_op jit(solution)/shard_map/ppermute | solution.py:41
  9.9 33.9 %all-to-all-start = ((bf16[32,56,256]{2,1,0:T(8,128)(2,1)}), bf16[32,56,256]{2,1,0:T(8,128)(2,1)S(1)}, u32[]{:S(2)}, u32[]{:S(2)}) async-start(bf16[32,56,256]{2,1,0:T(8,128)(2,1)} %pack_rows.1), calls=%async_computation | async-start | bytes 1835008 | tf_op jit(solution)/shard_map/all_to_all | solution.py:495
  19.5 26.2 %copy-start.6 = (bf16[384,1024]{1,0:T(8,128)(2,1)}, bf16[384,1024]{1,0:T(8,128)(2,1)S(1)}, u32[]{:S(2)}) copy-start(bf16[384,1024]{1,0:T(8,128)(2,1)S(1)} %constant_dynamic-slice_fusion.refs_0_) | copy-start | bytes 2359300
  19.5 18.8 %collective-permute-start.2 = (bf16[384,1024]{1,0:T(8,128)(2,1)S(1)}, bf16[384,1024]{1,0:T(8,128)(2,1)S(1)}, u32[]{:S(2)}, u32[]{:S(2)}) collective-permute-start(bf16[384,1024]{1,0:T(8,128)(2,1)S(1)} %constant_dynamic-slice_fusion.refs_0_), channel_id=1, source_target_pairs={{0,1},{1,0},{2,3},{3,2},{4,5},{5,4},{6,7},{7,6},{8,9},{9,8},{10,11... | collective-permute-start | bytes 2359304 | tf_op jit(solution)/shard_map/ppermute | solution.py:51
  20.8 19.6 %collective-permute-start = (bf16[384,1024]{1,0:T(8,128)(2,1)S(1)}, bf16[384,1024]{1,0:T(8,128)(2,1)S(1)}, u32[]{:S(2)}, u32[]{:S(2)}) collective-permute-start(bf16[384,1024]{1,0:T(8,128)(2,1)S(1)} %constant_dynamic-slice_fusion.refs_0_), channel_id=1, source_target_pairs={{0,3},{1,2},{2,1},{3,0},{4,7},{5,6},{6,5},{7,4},{8,11},{9,10},{10,... | collective-permute-start | bytes 2359304 | tf_op jit(solution)/shard_map/ppermute | solution.py:51
  38.3 2.1 %copy-start.7 = (bf16[384,1024]{1,0:T(8,128)(2,1)}, bf16[384,1024]{1,0:T(8,128)(2,1)S(1)}, u32[]{:S(2)}) copy-start(bf16[384,1024]{1,0:T(8,128)(2,1)S(1)} %collective-permute-done.2.refs_1_) | copy-start | bytes 2359300
  40.4 0.9 copy-start.8
  45.7 26.1 %all-to-all-start.1 = ((bf16[32,48,256]{2,1,0:T(8,128)(2,1)}), bf16[32,48,256]{2,1,0:T(8,128)(2,1)S(1)}, u32[]{:S(2)}, u32[]{:S(2)}) async-start(bf16[32,48,256]{2,1,0:T(8,128)(2,1)} %route_rows.1), calls=%async_computation.1 | async-start | bytes 1572864 | tf_op jit(solution)/shard_map/all_to_all | solution.py:497
  53.1 11.0 %collective-permute-start.1 = (bf16[192,1024]{1,0:T(8,128)(2,1)S(1)}, bf16[192,1024]{1,0:T(8,128)(2,1)S(1)}, u32[]{:S(2)}, u32[]{:S(2)}) collective-permute-start(bf16[192,1024]{1,0:T(8,128)(2,1)S(1)} %slice.20), channel_id=1, source_target_pairs={{0,1},{1,0},{2,3},{3,2},{4,5},{5,4},{6,7},{7,6},{8,9},{9,8},{10,11... | collective-permute-start | bytes 1179656 | tf_op jit(solution)/shard_map/ppermute | solution.py:51
  54.5 9.7 %collective-permute-start.3 = (bf16[192,1024]{1,0:T(8,128)(2,1)S(1)}, bf16[192,1024]{1,0:T(8,128)(2,1)S(1)}, u32[]{:S(2)}, u32[]{:S(2)}) collective-permute-start(bf16[192,1024]{1,0:T(8,128)(2,1)S(1)} %slice.21), channel_id=1, source_target_pairs={{0,3},{1,2},{2,1},{3,0},{4,7},{5,6},{6,5},{7,4},{8,11},{9,10},{10,... | collective-permute-start | bytes 1179656 | tf_op jit(solution)/shard_map/ppermute | solution.py:51
  64.0 0.7 copy-start.9
  64.3 0.7 copy-start.10
  65.0 6.7 %copy-start.4 = (s32[2]{0:T(128)S(1)}, s32[2]{0:T(128)}, u32[]{:S(2)}) copy-start(s32[2]{0:T(128)} %pad_add_fusion.place_ref.refs_0_) | copy-start | bytes 28
  73.5 0.7 copy-start.3
  74.3 5.7 %collective-permute-start.5 = (bf16[768,256]{1,0:T(8,128)(2,1)S(1)}, bf16[768,256]{1,0:T(8,128)(2,1)S(1)}, u32[]{:S(2)}, u32[]{:S(2)}) collective-permute-start(bf16[768,256]{1,0:T(8,128)(2,1)S(1)} %get-tuple-element.26), channel_id=1, source_target_pairs={{0,128},{128,0},{1,129},{129,1},{2,130},{130,2},{3,131},{131,3},{4... | collective-permute-start | bytes 1179656 | tf_op jit(solution)/shard_map/ppermute | solution.py:41
  80.0 0.8 copy-start.11
  89.9 12.4 %collective-permute-start.10 = (bf16[192,1024]{1,0:T(8,128)(2,1)}, bf16[192,1024]{1,0:T(8,128)(2,1)S(1)}, u32[]{:S(2)}, u32[]{:S(2)}) collective-permute-start(bf16[192,1024]{1,0:T(8,128)(2,1)} %get-tuple-element.36), channel_id=1, source_target_pairs={{0,3},{1,0},{2,1},{3,2},{4,7},{5,4},{6,5},{7,6},{8,11},{9,8},{10,9... | collective-permute-start | bytes 1179656 | tf_op jit(solution)/shard_map/ppermute | solution.py:46
  92.0 14.2 %collective-permute-start.7 = (bf16[192,1024]{1,0:T(8,128)(2,1)}, bf16[192,1024]{1,0:T(8,128)(2,1)S(1)}, u32[]{:S(2)}, u32[]{:S(2)}) collective-permute-start(bf16[192,1024]{1,0:T(8,128)(2,1)} %get-tuple-element.32), channel_id=1, source_target_pairs={{0,1},{1,2},{2,3},{3,0},{4,5},{5,6},{6,7},{7,4},{8,9},{9,10},{10,1... | collective-permute-start | bytes 1179656 | tf_op jit(solution)/shard_map/ppermute | solution.py:46
  99.6 22.0 %copy-start.1 = (bf16[192,1024]{1,0:T(8,128)(2,1)S(1)}, bf16[192,1024]{1,0:T(8,128)(2,1)}, u32[]{:S(2)}) copy-start(bf16[192,1024]{1,0:T(8,128)(2,1)} %get-tuple-element.29.refs_0_) | copy-start | bytes 1179652
  99.6 22.0 %copy-start.2 = (bf16[192,1024]{1,0:T(8,128)(2,1)S(1)}, bf16[192,1024]{1,0:T(8,128)(2,1)}, u32[]{:S(2)}) copy-start(bf16[192,1024]{1,0:T(8,128)(2,1)} %get-tuple-element.33.refs_3_) | copy-start | bytes 1179652
  99.6 22.0 %copy-start.5 = (s32[2]{0:T(128)S(1)}, s32[2]{0:T(128)}, u32[]{:S(2)}) copy-start(s32[2]{0:T(128)} %pad_add_fusion.place_ref.refs_0_) | copy-start | bytes 28
  99.6 10.6 %collective-permute-start.6 = (bf16[192,1024]{1,0:T(8,128)(2,1)}, bf16[192,1024]{1,0:T(8,128)(2,1)S(1)}, u32[]{:S(2)}, u32[]{:S(2)}) collective-permute-start(bf16[192,1024]{1,0:T(8,128)(2,1)} %get-tuple-element.30), channel_id=1, source_target_pairs={{0,3},{1,0},{2,1},{3,2},{4,7},{5,4},{6,5},{7,6},{8,11},{9,8},{10,9... | collective-permute-start | bytes 1179656 | tf_op jit(solution)/shard_map/ppermute | solution.py:46
  102.3 10.8 %collective-permute-start.9 = (bf16[192,1024]{1,0:T(8,128)(2,1)}, bf16[192,1024]{1,0:T(8,128)(2,1)S(1)}, u32[]{:S(2)}, u32[]{:S(2)}) collective-permute-start(bf16[192,1024]{1,0:T(8,128)(2,1)} %get-tuple-element.34), channel_id=1, source_target_pairs={{0,1},{1,2},{2,3},{3,0},{4,5},{5,6},{6,7},{7,4},{8,9},{9,10},{10,1... | collective-permute-start | bytes 1179656 | tf_op jit(solution)/shard_map/ppermute | solution.py:46
  103.5 15.0 %collective-permute-start.11 = (bf16[192,1024]{1,0:T(8,128)(2,1)S(1)}, bf16[192,1024]{1,0:T(8,128)(2,1)S(1)}, u32[]{:S(2)}, u32[]{:S(2)}) collective-permute-start(bf16[192,1024]{1,0:T(8,128)(2,1)S(1)} %add_convert_fusion), channel_id=1, source_target_pairs={{0,3},{1,0},{2,1},{3,2},{4,7},{5,4},{6,5},{7,6},{8,11},{9,8},{10,9... | collective-permute-start | bytes 1179656 | tf_op jit(solution)/shard_map/ppermute | solution.py:46
  107.4 14.2 %collective-permute-start.8 = (bf16[192,1024]{1,0:T(8,128)(2,1)S(1)}, bf16[192,1024]{1,0:T(8,128)(2,1)S(1)}, u32[]{:S(2)}, u32[]{:S(2)}) collective-permute-start(bf16[192,1024]{1,0:T(8,128)(2,1)S(1)} %add_convert_fusion.1), channel_id=1, source_target_pairs={{0,1},{1,2},{2,3},{3,0},{4,5},{5,6},{6,7},{7,4},{8,9},{9,10},{10,1... | collective-permute-start | bytes 1179656 | tf_op jit(solution)/shard_map/ppermute | solution.py:46
  122.3 3.6 %collective-permute-start.12 = (bf16[384,512]{1,0:T(8,128)(2,1)S(1)}, bf16[384,512]{1,0:T(8,128)(2,1)S(1)}, u32[]{:S(2)}, u32[]{:S(2)}) collective-permute-start(bf16[384,512]{1,0:T(8,128)(2,1)S(1)} %sum_columns.2), channel_id=1, source_target_pairs={{0,128},{128,0},{1,129},{129,1},{2,130},{130,2},{3,131},{131,3},{4... | collective-permute-start | bytes 1179656 | tf_op jit(solution)/shard_map/ppermute | solution.py:41

commit v3 on v2

--- a/solution.py
+++ b/solution.py
@@ -27,6 +27,10 @@
 
 def params(mib=16):
     return pltpu.CompilerParams(vmem_limit_bytes=mib * MIB)
+
+
+def cost(us):
+    return pl.CostEstimate(flops=int(us * 1e9), bytes_accessed=int(us * 1e6), transcendentals=0)
 
 
 def whole(shape):
@@ -113,6 +117,7 @@
         ),
         out_shape=jax.ShapeDtypeStruct((parts, message, half), BF16),
         compiler_params=params(60),
+        cost_estimate=cost(3),
         name="pack_rows",
     )(place, owner, slot, neighbours)
 
@@ -154,7 +159,8 @@
         out_shape=jax.ShapeDtypeStruct(out_shape, BF16),
         in_specs=[whole(held.shape)] + [glance(x) for x in after],
         out_specs=whole(out_shape),
-        compiler_params=params(),
+        compiler_params=params(16),
+        cost_estimate=cost(2),
         name="route_rows",
     )(held, *after)
 
@@ -196,7 +202,8 @@
             out_specs=[whole(out_shape)] * 2,
         ),
         out_shape=[jax.ShapeDtypeStruct(out_shape, BF16)] * 2,
-        compiler_params=params(),
+        compiler_params=params(16),
+        cost_estimate=cost(2),
         name="unpack_rows",
     )(place, arrived, *after)
 
@@ -248,6 +255,7 @@
         ),
         out_shape=[shape, shape],
         compiler_params=params(60),
+        cost_estimate=cost(2.5 * len(masks)),
         name="project",
     )(place, *blocks, *(sums or ()), own_weight, other_weight)
 
@@ -366,12 +374,14 @@
             scratch_shapes=[pltpu.VMEM((4, columns, width), BF16), pltpu.SemaphoreType.DMA((4,))],
         ),
         out_shape=[jax.ShapeDtypeStruct(shape, BF16) for shape in outs],
-        compiler_params=params(57),
+        compiler_params=params(16),
+        cost_estimate=cost(8),
         name="attend",
     )(place, own, other, cotangent, near, far, own_weight, other_weight)
 
 
-def partial_kernel(steps, place_ref, own_ref, other_ref, own_a, own_b, other_a, other_b, *out_refs):
+def partial_kernel(steps, place_ref, own_ref, other_ref, own_a, own_b, other_a, other_b, *refs):
+    out_refs = refs[-2 * len(steps) :]
     columns = own_a.shape[0]
     low_rows = own_ref.shape[0] // 2
     for i in range(len(steps)):
@@ -387,7 +397,7 @@
                 out_refs[2 * i + 1][:, place] = term[low_rows:]
 
 
-def partial_terms(place, steps, grad_own, grad_other, own_weight, other_weight):
+def partial_terms(place, steps, grad_own, grad_other, own_weight, other_weight, after=()):
     tokens, width = grad_own.shape
     tp_count = lax.axis_size("tp")
     columns = own_weight.shape[0] // (2 * tp_count)
@@ -405,17 +415,35 @@
         grid_spec=pltpu.PrefetchScalarGridSpec(
             num_scalar_prefetch=1,
             grid=(len(steps),),
-            in_specs=[whole((tokens, width))] * 2 + [weight_spec(0), weight_spec(1)] * 2,
+            in_specs=[whole((tokens, width))] * 2
+            + [weight_spec(0), weight_spec(1)] * 2
+            + [glance(x) for x in after],
             out_specs=[whole(shape)] * (2 * len(steps)),
         ),
         out_shape=[jax.ShapeDtypeStruct(shape, BF16)] * (2 * len(steps)),
-        compiler_params=params(57),
+        compiler_params=params(16),
+        cost_estimate=cost(2 * len(steps)),
         name="partial_terms",
-    )(place, grad_own, grad_other, own_weight, own_weight, other_weight, other_weight)
-
-
-def add_terms(a, b):
-    return (a.astype(jnp.float32) + b.astype(jnp.float32)).astype(BF16)
+    )(place, grad_own, grad_other, own_weight, own_weight, other_weight, other_weight, *after)
+
+
+def add_kernel(*refs):
+    count = len(refs) // 3
+    for a_ref, b_ref, out_ref in zip(refs[:count], refs[count : 2 * count], refs[2 * count :]):
+        out_ref[...] = (a_ref[...].astype(jnp.float32) + b_ref[...].astype(jnp.float32)).astype(BF16)
+
+
+def add_terms(held, arrived):
+    return pl.pallas_call(
+        add_kernel,
+        grid=(1,),
+        out_shape=[jax.ShapeDtypeStruct(x.shape, BF16) for x in held],
+        in_specs=[whole(x.shape) for x in (*held, *arrived)],
+        out_specs=[whole(x.shape) for x in held],
+        compiler_params=params(16),
+        cost_estimate=cost(1),
+        name="add_terms",
+    )(*held, *arrived)
 
 
 def scatter_ring(place, across_low, across_high, *operands):
@@ -424,11 +452,13 @@
         return [own_low, shift(across_low, 1)], [own_high, shift(across_high, 1)]
     rising = shift(across_low, 1)
     falling = shift(across_high, -1)
-    up_low, up_high, down_low, down_high, own_low, own_high = partial_terms(place, (1, 3, 0), *operands)
+    up_low, up_high, down_low, down_high = partial_terms(place, (1, 3), *operands)
     up_high = shift(up_high, 1)
     down_low = shift(down_low, -1)
-    up_low = shift(add_terms(up_low, rising), 1)
-    down_high = shift(add_terms(down_high, falling), -1)
+    up_low, down_high = add_terms((up_low, down_high), (rising, falling))
+    own_low, own_high = partial_terms(place, (0,), *operands, after=(up_low,))
+    up_low = shift(up_low, 1)
+    down_high = shift(down_high, -1)
     return [own_low, down_low, up_low], [own_high, up_high, down_high]
 
 
@@ -469,7 +499,8 @@
             out_specs=whole(out_shape),
         ),
         out_shape=jax.ShapeDtypeStruct(out_shape, BF16),
-        compiler_params=params(),
+        compiler_params=params(16),
+        cost_estimate=cost(1),
         name="sum_columns",
     )(place, *lows, *highs, *extra)
 

time: 128 us -> 120 us (0.938)
  Pallas kernels: 38.4 us -> 35.2 us
  other arithmetic: 2.85 us -> 0.56 us
  local copies, waits for them, and re-layouts: 8.65 us -> 7.16 us
    pallas_call x1, Pallas kernels: 9.14 us -> 6.68 us  [attend(): pl.pallas_call(lambda *refs: attend_kernel(tp_count, tp_count // 2, *refs...]
    convert_element_type x2 -> x0, other arithmetic: 2.26 us -> none  [add_terms(): return (a.astype(jnp.float32) + b.astype(jnp.float32)).astype(BF16)]
    unnamed x26 -> x24, local copies, waits for them, and re-layouts: 5.87 us -> 4.37 us
    pallas_call x1 -> x2, Pallas kernels: 7.57 us -> 6.61 us  [partial_terms(): pl.pallas_call(lambda *refs: partial_kernel(steps, *refs), grid_spec=pltp...]
  transfers between devices with their start and end apart: 15 -> 15, of which waited for: 11 -> 11; matrix products, arithmetic and copies ran while one was open for 7% -> 5% of each run, Pallas kernels for 20% -> 20%
where the time goes in v3:
time: 120 us
  starting transfers between devices  38.4 us (32%)
  waiting for transfers between devices  38.2 us (32%)
  Pallas kernels  35.2 us (29%)
  local copies, waits for them, and re-layouts  7.16 us (6%)
    ppermute x4, waiting for transfers between devices, swap(): return lax.ppermute(block, 'tp', [(i, i ^ mask) for i in range(count)])  18 us
    ppermute x6, waiting for transfers between devices, shift(): lax.ppermute(block, 'tp', [(i, (i + step) % count) for i in range(count)])  13.7 us
    pallas_call x2, Pallas kernels, project(): pl.pallas_call(project_last_kernel if final else project_kernel, grid_spe...  12.4 us
    all_to_all x1, starting transfers between devices, shards(): lax.all_to_all(packed, 'seq', split_axis=0, concat_axis=0, tiled=True)  9.47 us
    ppermute x3, starting transfers between devices, swap_cores(): return lax.ppermute(block, 'grp', [(0, 1), (1, 0)])  9 us
    ppermute x6, starting transfers between devices, shift(): lax.ppermute(block, 'tp', [(i, (i + step) % count) for i in range(count)])  8.11 us
    pallas_call x1, Pallas kernels, attend(): pl.pallas_call(lambda *refs: attend_kernel(tp_count, tp_count // 2, *refs...  6.68 us
    pallas_call x2, Pallas kernels, partial_terms(): pl.pallas_call(lambda *refs: partial_kernel(steps, *refs), grid_spec=pltp...  6.61 us
  transfers between devices with their start and end apart: 15, of which 11 were waited for; matrix products, arithmetic and copies ran while one was open for 5% of the time, Pallas kernels for 20%

profile of v3, /device:TPU:1, one launch (start us, length us, event | category | flops | bytes accessed | tf_op | source)
XLA Modules:
  0.0 119.6 jit_solution(9149328377964624051)
XLA Ops:
  0.0 3.2 %collective-permute-start.4 = (bf16[4096,512]{1,0:T(8,128)(2,1)}, bf16[4096,512]{1,0:T(8,128)(2,1)}, u32[]{:S(2)}, u32[]{:S(2)}) collective-permute-start(bf16[4096,512]{1,0:T(8,128)(2,1)} %bitcast.3), channel_id=1, source_target_pairs={{0,128},{128,0},{1,129},{129,1},{2,130},{130,2},{3,131},{131,3},{4... | collective-permute-start | bytes 12582920 | tf_op jit(solution)/shard_map/ppermute | solution.py:45
  3.2 1.4 %copy.7.refs_1_ = s32[12,2]{1,0:T(8,128)} copy(s32[12,2]{0,1:T(2,128)} %param.9) | data formatting | bytes 192 | tf_op args[3]
  4.6 1.4 %copy.8.refs_2_ = s32[12,2]{1,0:T(8,128)} copy(s32[12,2]{0,1:T(2,128)} %param.10) | data formatting | bytes 192 | tf_op args[4]
  6.5 3.4 %pack_rows.1 = bf16[32,56,256]{2,1,0:T(8,128)(2,1)} custom-call(s32[2]{0:T(128)} %pad_add_fusion.place_ref.refs_0_, s32[12,2]{1,0:T(8,128)} %copy.7.refs_1_, s32[12,2]{1,0:T(8,128)} %copy.8.refs_2_, bf16[24,64,512]{2,1,0:T(8,128)(2,1)} %refs_3_.2), custom_call_target="tpu_custom_call" | custom-call | flops 3000000000 | bytes 3000000 | tf_op jit(solution)/shard_map/pack_rows/pallas_call | solution.py:109
  9.9 9.5 %all-to-all-start = ((bf16[32,56,256]{2,1,0:T(8,128)(2,1)}), bf16[32,56,256]{2,1,0:T(8,128)(2,1)S(1)}, u32[]{:S(2)}, u32[]{:S(2)}) async-start(bf16[32,56,256]{2,1,0:T(8,128)(2,1)} %pack_rows.1), calls=%async_computation | async-start | bytes 1835008 | tf_op jit(solution)/shard_map/all_to_all | solution.py:526
  19.4 1.3 %collective-permute-start.2 = (bf16[384,1024]{1,0:T(8,128)(2,1)S(1)}, bf16[384,1024]{1,0:T(8,128)(2,1)S(1)}, u32[]{:S(2)}, u32[]{:S(2)}) collective-permute-start(bf16[384,1024]{1,0:T(8,128)(2,1)S(1)} %constant_dynamic-slice_fusion.refs_0_), channel_id=1, source_target_pairs={{0,1},{1,0},{2,3},{3,2},{4,5},{5,4},{6,7},{7,6},{8,9},{9,8},{10,11... | collective-permute-start | bytes 2359304 | tf_op jit(solution)/shard_map/ppermute | solution.py:55
  20.7 1.8 %collective-permute-start = (bf16[384,1024]{1,0:T(8,128)(2,1)S(1)}, bf16[384,1024]{1,0:T(8,128)(2,1)S(1)}, u32[]{:S(2)}, u32[]{:S(2)}) collective-permute-start(bf16[384,1024]{1,0:T(8,128)(2,1)S(1)} %constant_dynamic-slice_fusion.refs_0_), channel_id=1, source_target_pairs={{0,3},{1,2},{2,1},{3,0},{4,7},{5,6},{6,5},{7,4},{8,11},{9,10},{10,... | collective-permute-start | bytes 2359304 | tf_op jit(solution)/shard_map/ppermute | solution.py:55
  22.6 15.7 %collective-permute-done.2.refs_1_ = bf16[384,1024]{1,0:T(8,128)(2,1)S(1)} collective-permute-done((bf16[384,1024]{1,0:T(8,128)(2,1)S(1)}, bf16[384,1024]{1,0:T(8,128)(2,1)S(1)}, u32[]{:S(2)}, u32[]{:S(2)}) %collective-permute-start.2) | collective-permute-done | bytes 786464 | tf_op jit(solution)/shard_map/ppermute | solution.py:55
  38.2 2.1 %collective-permute-done.refs_2_ = bf16[384,1024]{1,0:T(8,128)(2,1)S(1)} collective-permute-done((bf16[384,1024]{1,0:T(8,128)(2,1)S(1)}, bf16[384,1024]{1,0:T(8,128)(2,1)S(1)}, u32[]{:S(2)}, u32[]{:S(2)}) %collective-permute-start) | collective-permute-done | bytes 786464 | tf_op jit(solution)/shard_map/ppermute | solution.py:55
  41.2 2.5 %all-to-all-done.refs_0_ = bf16[32,56,256]{2,1,0:T(8,128)(2,1)S(1)} async-done(((bf16[32,56,256]{2,1,0:T(8,128)(2,1)}), bf16[32,56,256]{2,1,0:T(8,128)(2,1)S(1)}, u32[]{:S(2)}, u32[]{:S(2)}) %all-to-all-start) | async-done | bytes 917536 | tf_op jit(solution)/shard_map/all_to_all | solution.py:526
  43.8 1.9 %route_rows.1 = bf16[32,48,256]{2,1,0:T(8,128)(2,1)} custom-call(bf16[32,56,256]{2,1,0:T(8,128)(2,1)S(1)} %all-to-all-done.refs_0_, bf16[16,128]{1,0:T(8,128)(2,1)S(1)} %slice.22.refs_1_, bf16[16,128]{1,0:T(8,128)(2,1)S(1)} %slice.23.refs_2_), custom_call_target="tpu_custom_call" | custom-call | flops 2000000000 | bytes 2000000 | tf_op jit(solution)/shard_map/route_rows/pallas_call | solution.py:156
  45.6 6.3 %all-to-all-start.1 = ((bf16[32,48,256]{2,1,0:T(8,128)(2,1)}), bf16[32,48,256]{2,1,0:T(8,128)(2,1)S(1)}, u32[]{:S(2)}, u32[]{:S(2)}) async-start(bf16[32,48,256]{2,1,0:T(8,128)(2,1)} %route_rows.1), calls=%async_computation.1 | async-start | bytes 1572864 | tf_op jit(solution)/shard_map/all_to_all | solution.py:528
  54.5 1.9 %collective-permute-start.3 = (bf16[192,1024]{1,0:T(8,128)(2,1)S(1)}, bf16[192,1024]{1,0:T(8,128)(2,1)S(1)}, u32[]{:S(2)}, u32[]{:S(2)}) collective-permute-start(bf16[192,1024]{1,0:T(8,128)(2,1)S(1)} %slice.21), channel_id=1, source_target_pairs={{0,3},{1,2},{2,1},{3,0},{4,7},{5,6},{6,5},{7,4},{8,11},{9,10},{10,... | collective-permute-start | bytes 1179656 | tf_op jit(solution)/shard_map/ppermute | solution.py:55
  56.4 7.6 %project.2 = (f32[384,512]{1,0:T(8,128)}, f32[384,512]{1,0:T(8,128)}) custom-call(s32[2]{0:T(128)} %pad_add_fusion.place_ref.refs_0_, bf16[384,1024]{1,0:T(8,128)(2,1)} %copy-done.6, bf16[384,1024]{1,0:T(8,128)(2,1)} %copy-done.9, bf16[384,1024]{1,0:T(8,128)(2,1)} %copy-done.10, bf16[4096,512]{1,0:T(8,128)(2,1)} %bitcast.4, ...), custom_call_target="tpu_custom_call" | custom-call | flops 7500000256 | bytes 7500000 | tf_op jit(solution)/shard_map/project/pallas_call | solution.py:248
  65.0 4.8 %project.3 = (bf16[384,512]{1,0:T(8,128)(2,1)}, bf16[384,512]{1,0:T(8,128)(2,1)}) custom-call(s32[2]{0:T(128)} %pad_add_fusion.place_ref.refs_0_, bf16[192,1024]{1,0:T(8,128)(2,1)} %copy-done.7, bf16[192,1024]{1,0:T(8,128)(2,1)} %copy-done.8, f32[384,512]{1,0:T(8,128)} %get-tuple-element.23.refs_2_, f32[384,512]{1,0:T(8,128)} %get-tuple-element.24.refs_3_, ...), custom_call_target="tpu_custom_call" | custom-call | flops 2500000000 | bytes 2500000 | tf_op jit(solution)/shard_map/project/pallas_call | solution.py:248
  70.5 1.2 %all-to-all-done.1.refs_1_ = bf16[32,48,256]{2,1,0:T(8,128)(2,1)S(1)} async-done(((bf16[32,48,256]{2,1,0:T(8,128)(2,1)}), bf16[32,48,256]{2,1,0:T(8,128)(2,1)S(1)}, u32[]{:S(2)}, u32[]{:S(2)}) %all-to-all-start.1) | async-done | bytes 786464 | tf_op jit(solution)/shard_map/all_to_all | solution.py:528
  71.7 1.8 %unpack_rows.1 = (bf16[768,256]{1,0:T(8,128)(2,1)S(1)}, bf16[768,256]{1,0:T(8,128)(2,1)S(1)}) custom-call(s32[2]{0:T(128)S(1)} %copy-done.2, bf16[32,48,256]{2,1,0:T(8,128)(2,1)S(1)} %all-to-all-done.1.refs_1_, bf16[16,128]{1,0:T(8,128)(2,1)S(1)} %slice.19.refs_2_), custom_call_target="tpu_custom_call" | custom-call | flops 2000000000 | bytes 2000000 | tf_op jit(solution)/shard_map/unpack_rows/pallas_call | solution.py:196
  73.5 4.5 %collective-permute-start.5 = (bf16[768,256]{1,0:T(8,128)(2,1)S(1)}, bf16[768,256]{1,0:T(8,128)(2,1)S(1)}, u32[]{:S(2)}, u32[]{:S(2)}) collective-permute-start(bf16[768,256]{1,0:T(8,128)(2,1)S(1)} %get-tuple-element.28), channel_id=1, source_target_pairs={{0,128},{128,0},{1,129},{129,1},{2,130},{130,2},{3,131},{131,3},{4... | collective-permute-start | bytes 1179656 | tf_op jit(solution)/shard_map/ppermute | solution.py:45
  78.0 1.3 %collective-permute-done.5.refs_5_ = bf16[768,256]{1,0:T(8,128)(2,1)S(1)} collective-permute-done((bf16[768,256]{1,0:T(8,128)(2,1)S(1)}, bf16[768,256]{1,0:T(8,128)(2,1)S(1)}, u32[]{:S(2)}, u32[]{:S(2)}) %collective-permute-start.5) | collective-permute-done | bytes 393248 | tf_op jit(solution)/shard_map/ppermute | solution.py:45
  79.3 6.7 %attend.1 = (bf16[384,512]{1,0:T(8,128)(2,1)S(1)}, bf16[384,512]{1,0:T(8,128)(2,1)S(1)}, bf16[192,1024]{1,0:T(8,128)(2,1)S(1)}, bf16[192,1024]{1,0:T(8,128)(2,1)S(1)}) custom-call(s32[2]{0:T(128)S(1)} %copy-done.2, bf16[384,512]{1,0:T(8,128)(2,1)S(1)} %copy-done.3, bf16[384,512]{1,0:T(8,128)(2,1)S(1)} %copy-done.5, bf16[768,512]{1,0:T(8,128)(2,1)S(1)} %copy-done.4, ...), custom_call_target="tpu_custom_call" | custom-call | flops 8000000000 | bytes 8000000 | tf_op jit(solution)/shard_map/attend/pallas_call | solution.py:367
  86.3 2.7 %collective-permute-start.7 = (bf16[192,1024]{1,0:T(8,128)(2,1)S(1)}, bf16[192,1024]{1,0:T(8,128)(2,1)S(1)}, u32[]{:S(2)}, u32[]{:S(2)}) collective-permute-start(bf16[192,1024]{1,0:T(8,128)(2,1)S(1)} %get-tuple-element.34), channel_id=1, source_target_pairs={{0,3},{1,0},{2,1},{3,2},{4,7},{5,4},{6,5},{7,6},{8,11},{9,8},{10,9... | collective-permute-start | bytes 1179656 | tf_op jit(solution)/shard_map/ppermute | solution.py:50
  89.0 3.9 %partial_terms.2 = (bf16[192,1024]{1,0:T(8,128)(2,1)S(1)}, bf16[192,1024]{1,0:T(8,128)(2,1)S(1)}, bf16[192,1024]{1,0:T(8,128)(2,1)S(1)}, bf16[192,1024]{1,0:T(8,128)(2,1)S(1)}) custom-call(s32[2]{0:T(128)S(1)} %copy-done.2, bf16[384,512]{1,0:T(8,128)(2,1)S(1)} %get-tuple-element.29.refs_1_, bf16[384,512]{1,0:T(8,128)(2,1)S(1)} %get-tuple-element.30.refs_2_, ...), custom_call_target="tpu_custom_call" | custom-call | flops 4000000000 | bytes 4000000 | tf_op jit(solution)/shard_map/partial_terms/pallas_call | solution.py:413
  92.9 2.7 %collective-permute-start.8 = (bf16[192,1024]{1,0:T(8,128)(2,1)S(1)}, bf16[192,1024]{1,0:T(8,128)(2,1)S(1)}, u32[]{:S(2)}, u32[]{:S(2)}) collective-permute-start(bf16[192,1024]{1,0:T(8,128)(2,1)S(1)} %get-tuple-element.37), channel_id=1, source_target_pairs={{0,3},{1,0},{2,1},{3,2},{4,7},{5,4},{6,5},{7,6},{8,11},{9,8},{10,9... | collective-permute-start | bytes 1179656 | tf_op jit(solution)/shard_map/ppermute | solution.py:50
  95.6 2.2 %collective-permute-done.6.refs_2_ = bf16[192,1024]{1,0:T(8,128)(2,1)S(1)} collective-permute-done((bf16[192,1024]{1,0:T(8,128)(2,1)S(1)}, bf16[192,1024]{1,0:T(8,128)(2,1)S(1)}, u32[]{:S(2)}, u32[]{:S(2)}) %collective-permute-start.6) | collective-permute-done | bytes 393248 | tf_op jit(solution)/shard_map/ppermute | solution.py:50
  98.0 2.4 %collective-permute-start.11 = (bf16[192,1024]{1,0:T(8,128)(2,1)S(1)}, bf16[192,1024]{1,0:T(8,128)(2,1)S(1)}, u32[]{:S(2)}, u32[]{:S(2)}) collective-permute-start(bf16[192,1024]{1,0:T(8,128)(2,1)S(1)} %get-tuple-element.40), channel_id=1, source_target_pairs={{0,3},{1,0},{2,1},{3,2},{4,7},{5,4},{6,5},{7,6},{8,11},{9,8},{10,9... | collective-permute-start | bytes 1179656 | tf_op jit(solution)/shard_map/ppermute | solution.py:50
  100.4 2.7 %partial_terms.3 = (bf16[192,1024]{1,0:T(8,128)(2,1)S(1)}, bf16[192,1024]{1,0:T(8,128)(2,1)S(1)}) custom-call(s32[2]{0:T(128)S(1)} %copy-done.2, bf16[384,512]{1,0:T(8,128)(2,1)S(1)} %get-tuple-element.29.refs_1_, bf16[384,512]{1,0:T(8,128)(2,1)S(1)} %get-tuple-element.30.refs_2_, bf16[4096,512]{1,0:T(8,128)(2,1)S(1)} %bitcast.9, ...), custom_call_target="tpu_custom_call" | custom-call | flops 2000000000 | bytes 2000000 | tf_op jit(solution)/shard_map/partial_terms/pallas_call | solution.py:413
  103.2 3.0 %collective-permute-done.10.refs_4_ = bf16[192,1024]{1,0:T(8,128)(2,1)S(1)} collective-permute-done((bf16[192,1024]{1,0:T(8,128)(2,1)S(1)}, bf16[192,1024]{1,0:T(8,128)(2,1)S(1)}, u32[]{:S(2)}, u32[]{:S(2)}) %collective-permute-start.10) | collective-permute-done | bytes 393248 | tf_op jit(solution)/shard_map/ppermute | solution.py:50
  106.2 7.4 %collective-permute-done.11.refs_5_ = bf16[192,1024]{1,0:T(8,128)(2,1)S(1)} collective-permute-done((bf16[192,1024]{1,0:T(8,128)(2,1)S(1)}, bf16[192,1024]{1,0:T(8,128)(2,1)S(1)}, u32[]{:S(2)}, u32[]{:S(2)}) %collective-permute-start.11) | collective-permute-done | bytes 393248 | tf_op jit(solution)/shard_map/ppermute | solution.py:50
  113.6 1.1 collective-permute-done.9.refs_2_
  115.4 1.3 %collective-permute-start.12 = (bf16[384,512]{1,0:T(8,128)(2,1)S(1)}, bf16[384,512]{1,0:T(8,128)(2,1)S(1)}, u32[]{:S(2)}, u32[]{:S(2)}) collective-permute-start(bf16[384,512]{1,0:T(8,128)(2,1)S(1)} %sum_columns.2), channel_id=1, source_target_pairs={{0,128},{128,0},{1,129},{129,1},{2,130},{130,2},{3,131},{131,3},{4... | collective-permute-start | bytes 1179656 | tf_op jit(solution)/shard_map/ppermute | solution.py:45
  116.7 1.3 %collective-permute-done.12.refs_6_ = bf16[384,512]{1,0:T(8,128)(2,1)S(1)} collective-permute-done((bf16[384,512]{1,0:T(8,128)(2,1)S(1)}, bf16[384,512]{1,0:T(8,128)(2,1)S(1)}, u32[]{:S(2)}, u32[]{:S(2)}) %collective-permute-start.12) | collective-permute-done | bytes 393248 | tf_op jit(solution)/shard_map/ppermute | solution.py:45
  118.0 1.6 %sum_columns.3 = bf16[768,512]{1,0:T(8,128)(2,1)} custom-call(s32[2]{0:T(128)S(1)} %copy-done.2, bf16[192,1024]{1,0:T(8,128)(2,1)S(1)} %get-tuple-element.36.refs_0_, bf16[192,1024]{1,0:T(8,128)(2,1)S(1)} %collective-permute-done.8.refs_1_, bf16[192,1024]{1,0:T(8,128)(2,1)S(1)} %collective-permute-done.9.refs_2_, ...), custom_call_target="tpu_custom_call" | custom-call | flops 1000000000 | bytes 1000000 | tf_op jit(solution)/shard_map/sum_columns/pallas_call | solution.py:493
  (40 shorter events, 6.9 us)
Async XLA Ops:
  0.0 19.4 %copy-start = (bf16[768,1024]{1,0:T(8,128)(2,1)S(1)}, bf16[768,1024]{1,0:T(8,128)(2,1)}, u32[]{:S(2)}) copy-start(bf16[768,1024]{1,0:T(8,128)(2,1)} %param.6) | copy-start | bytes 4718596
  0.0 56.4 %collective-permute-start.4 = (bf16[4096,512]{1,0:T(8,128)(2,1)}, bf16[4096,512]{1,0:T(8,128)(2,1)}, u32[]{:S(2)}, u32[]{:S(2)}) collective-permute-start(bf16[4096,512]{1,0:T(8,128)(2,1)} %bitcast.3), channel_id=1, source_target_pairs={{0,128},{128,0},{1,129},{129,1},{2,130},{130,2},{3,131},{131,3},{4... | collective-permute-start | bytes 12582920 | tf_op jit(solution)/shard_map/ppermute | solution.py:45
  9.9 33.9 %all-to-all-start = ((bf16[32,56,256]{2,1,0:T(8,128)(2,1)}), bf16[32,56,256]{2,1,0:T(8,128)(2,1)S(1)}, u32[]{:S(2)}, u32[]{:S(2)}) async-start(bf16[32,56,256]{2,1,0:T(8,128)(2,1)} %pack_rows.1), calls=%async_computation | async-start | bytes 1835008 | tf_op jit(solution)/shard_map/all_to_all | solution.py:526
  19.4 26.2 %copy-start.6 = (bf16[384,1024]{1,0:T(8,128)(2,1)}, bf16[384,1024]{1,0:T(8,128)(2,1)S(1)}, u32[]{:S(2)}) copy-start(bf16[384,1024]{1,0:T(8,128)(2,1)S(1)} %constant_dynamic-slice_fusion.refs_0_) | copy-start | bytes 2359300
  19.4 18.8 %collective-permute-start.2 = (bf16[384,1024]{1,0:T(8,128)(2,1)S(1)}, bf16[384,1024]{1,0:T(8,128)(2,1)S(1)}, u32[]{:S(2)}, u32[]{:S(2)}) collective-permute-start(bf16[384,1024]{1,0:T(8,128)(2,1)S(1)} %constant_dynamic-slice_fusion.refs_0_), channel_id=1, source_target_pairs={{0,1},{1,0},{2,3},{3,2},{4,5},{5,4},{6,7},{7,6},{8,9},{9,8},{10,11... | collective-permute-start | bytes 2359304 | tf_op jit(solution)/shard_map/ppermute | solution.py:55
  20.7 19.6 %collective-permute-start = (bf16[384,1024]{1,0:T(8,128)(2,1)S(1)}, bf16[384,1024]{1,0:T(8,128)(2,1)S(1)}, u32[]{:S(2)}, u32[]{:S(2)}) collective-permute-start(bf16[384,1024]{1,0:T(8,128)(2,1)S(1)} %constant_dynamic-slice_fusion.refs_0_), channel_id=1, source_target_pairs={{0,3},{1,2},{2,1},{3,0},{4,7},{5,6},{6,5},{7,4},{8,11},{9,10},{10,... | collective-permute-start | bytes 2359304 | tf_op jit(solution)/shard_map/ppermute | solution.py:55
  38.2 2.1 %copy-start.9 = (bf16[384,1024]{1,0:T(8,128)(2,1)}, bf16[384,1024]{1,0:T(8,128)(2,1)S(1)}, u32[]{:S(2)}) copy-start(bf16[384,1024]{1,0:T(8,128)(2,1)S(1)} %collective-permute-done.2.refs_1_) | copy-start | bytes 2359300
  40.3 0.9 copy-start.10
  45.6 26.1 %all-to-all-start.1 = ((bf16[32,48,256]{2,1,0:T(8,128)(2,1)}), bf16[32,48,256]{2,1,0:T(8,128)(2,1)S(1)}, u32[]{:S(2)}, u32[]{:S(2)}) async-start(bf16[32,48,256]{2,1,0:T(8,128)(2,1)} %route_rows.1), calls=%async_computation.1 | async-start | bytes 1572864 | tf_op jit(solution)/shard_map/all_to_all | solution.py:528
  53.0 11.0 %collective-permute-start.1 = (bf16[192,1024]{1,0:T(8,128)(2,1)S(1)}, bf16[192,1024]{1,0:T(8,128)(2,1)S(1)}, u32[]{:S(2)}, u32[]{:S(2)}) collective-permute-start(bf16[192,1024]{1,0:T(8,128)(2,1)S(1)} %slice.20), channel_id=1, source_target_pairs={{0,1},{1,0},{2,3},{3,2},{4,5},{5,4},{6,7},{7,6},{8,9},{9,8},{10,11... | collective-permute-start | bytes 1179656 | tf_op jit(solution)/shard_map/ppermute | solution.py:55
  54.5 9.8 %collective-permute-start.3 = (bf16[192,1024]{1,0:T(8,128)(2,1)S(1)}, bf16[192,1024]{1,0:T(8,128)(2,1)S(1)}, u32[]{:S(2)}, u32[]{:S(2)}) collective-permute-start(bf16[192,1024]{1,0:T(8,128)(2,1)S(1)} %slice.21), channel_id=1, source_target_pairs={{0,3},{1,2},{2,1},{3,0},{4,7},{5,6},{6,5},{7,4},{8,11},{9,10},{10,... | collective-permute-start | bytes 1179656 | tf_op jit(solution)/shard_map/ppermute | solution.py:55
  64.0 0.7 copy-start.7
  64.2 0.8 copy-start.8
  65.0 6.7 %copy-start.2 = (s32[2]{0:T(128)S(1)}, s32[2]{0:T(128)}, u32[]{:S(2)}) copy-start(s32[2]{0:T(128)} %pad_add_fusion.place_ref.refs_0_) | copy-start | bytes 28
  70.4 8.9 %copy-start.3 = (bf16[384,512]{1,0:T(8,128)(2,1)S(1)}, bf16[384,512]{1,0:T(8,128)(2,1)}, u32[]{:S(2)}) copy-start(bf16[384,512]{1,0:T(8,128)(2,1)} %get-tuple-element.25.refs_1_) | copy-start | bytes 1179652
  70.5 8.9 %copy-start.4 = (bf16[768,512]{1,0:T(8,128)(2,1)S(1)}, bf16[768,512]{1,0:T(8,128)(2,1)}, u32[]{:S(2)}) copy-start(bf16[768,512]{1,0:T(8,128)(2,1)} %refs_3_.3) | copy-start | bytes 2359300
  71.7 7.6 %copy-start.1 = (bf16[1,4096,512]{2,1,0:T(8,128)(2,1)S(1)}, bf16[1,4096,512]{2,1,0:T(8,128)(2,1)}, u32[]{:S(2)}) copy-start(bf16[1,4096,512]{2,1,0:T(8,128)(2,1)} %param.7) | copy-start | bytes 12582916
  71.7 7.6 %copy-start.5 = (bf16[384,512]{1,0:T(8,128)(2,1)S(1)}, bf16[384,512]{1,0:T(8,128)(2,1)}, u32[]{:S(2)}) copy-start(bf16[384,512]{1,0:T(8,128)(2,1)} %get-tuple-element.26.refs_2_) | copy-start | bytes 1179652
  73.5 5.8 %collective-permute-start.5 = (bf16[768,256]{1,0:T(8,128)(2,1)S(1)}, bf16[768,256]{1,0:T(8,128)(2,1)S(1)}, u32[]{:S(2)}, u32[]{:S(2)}) collective-permute-start(bf16[768,256]{1,0:T(8,128)(2,1)S(1)} %get-tuple-element.28), channel_id=1, source_target_pairs={{0,128},{128,0},{1,129},{129,1},{2,130},{130,2},{3,131},{131,3},{4... | collective-permute-start | bytes 1179656 | tf_op jit(solution)/shard_map/ppermute | solution.py:45
  86.0 11.8 %collective-permute-start.6 = (bf16[192,1024]{1,0:T(8,128)(2,1)S(1)}, bf16[192,1024]{1,0:T(8,128)(2,1)S(1)}, u32[]{:S(2)}, u32[]{:S(2)}) collective-permute-start(bf16[192,1024]{1,0:T(8,128)(2,1)S(1)} %get-tuple-element.33), channel_id=1, source_target_pairs={{0,1},{1,2},{2,3},{3,0},{4,5},{5,6},{6,7},{7,4},{8,9},{9,10},{10,1... | collective-permute-start | bytes 1179656 | tf_op jit(solution)/shard_map/ppermute | solution.py:50
  86.3 11.5 %collective-permute-start.7 = (bf16[192,1024]{1,0:T(8,128)(2,1)S(1)}, bf16[192,1024]{1,0:T(8,128)(2,1)S(1)}, u32[]{:S(2)}, u32[]{:S(2)}) collective-permute-start(bf16[192,1024]{1,0:T(8,128)(2,1)S(1)} %get-tuple-element.34), channel_id=1, source_target_pairs={{0,3},{1,0},{2,1},{3,2},{4,7},{5,4},{6,5},{7,6},{8,11},{9,8},{10,9... | collective-permute-start | bytes 1179656 | tf_op jit(solution)/shard_map/ppermute | solution.py:50
  92.8 13.4 %collective-permute-start.10 = (bf16[192,1024]{1,0:T(8,128)(2,1)S(1)}, bf16[192,1024]{1,0:T(8,128)(2,1)S(1)}, u32[]{:S(2)}, u32[]{:S(2)}) collective-permute-start(bf16[192,1024]{1,0:T(8,128)(2,1)S(1)} %get-tuple-element.39), channel_id=1, source_target_pairs={{0,1},{1,2},{2,3},{3,0},{4,5},{5,6},{6,7},{7,4},{8,9},{9,10},{10,1... | collective-permute-start | bytes 1179656 | tf_op jit(solution)/shard_map/ppermute | solution.py:50
  92.9 13.3 %collective-permute-start.8 = (bf16[192,1024]{1,0:T(8,128)(2,1)S(1)}, bf16[192,1024]{1,0:T(8,128)(2,1)S(1)}, u32[]{:S(2)}, u32[]{:S(2)}) collective-permute-start(bf16[192,1024]{1,0:T(8,128)(2,1)S(1)} %get-tuple-element.37), channel_id=1, source_target_pairs={{0,3},{1,0},{2,1},{3,2},{4,7},{5,4},{6,5},{7,6},{8,11},{9,8},{10,9... | collective-permute-start | bytes 1179656 | tf_op jit(solution)/shard_map/ppermute | solution.py:50
  98.0 15.6 %collective-permute-start.11 = (bf16[192,1024]{1,0:T(8,128)(2,1)S(1)}, bf16[192,1024]{1,0:T(8,128)(2,1)S(1)}, u32[]{:S(2)}, u32[]{:S(2)}) collective-permute-start(bf16[192,1024]{1,0:T(8,128)(2,1)S(1)} %get-tuple-element.40), channel_id=1, source_target_pairs={{0,3},{1,0},{2,1},{3,2},{4,7},{5,4},{6,5},{7,6},{8,11},{9,8},{10,9... | collective-permute-start | bytes 1179656 | tf_op jit(solution)/shard_map/ppermute | solution.py:50
  100.4 14.2 %collective-permute-start.9 = (bf16[192,1024]{1,0:T(8,128)(2,1)S(1)}, bf16[192,1024]{1,0:T(8,128)(2,1)S(1)}, u32[]{:S(2)}, u32[]{:S(2)}) collective-permute-start(bf16[192,1024]{1,0:T(8,128)(2,1)S(1)} %get-tuple-element.35.refs_7_), channel_id=1, source_target_pairs={{0,1},{1,2},{2,3},{3,0},{4,5},{5,6},{6,7},{7,4},{8,9},{9,10},{10,1... | collective-permute-start | bytes 1179656 | tf_op jit(solution)/shard_map/ppermute | solution.py:50
  115.4 2.6 %collective-permute-start.12 = (bf16[384,512]{1,0:T(8,128)(2,1)S(1)}, bf16[384,512]{1,0:T(8,128)(2,1)S(1)}, u32[]{:S(2)}, u32[]{:S(2)}) collective-permute-start(bf16[384,512]{1,0:T(8,128)(2,1)S(1)} %sum_columns.2), channel_id=1, source_target_pairs={{0,128},{128,0},{1,129},{129,1},{2,130},{130,2},{3,131},{131,3},{4... | collective-permute-start | bytes 1179656 | tf_op jit(solution)/shard_map/ppermute | solution.py:45

commit v4 on v3

--- a/solution.py
+++ b/solution.py
@@ -71,90 +71,97 @@
     return (home == where).astype(jnp.float32).astype(BF16)
 
 
-def table_rows(owner, slot, owned, half):
-    batch = batch_of(owned)
-    groups = owner.shape[0]
-    number = KNB * lax.broadcasted_iota(jnp.int32, (groups, half), 0)
-    column = lax.broadcasted_iota(jnp.int32, (groups, half), 1)
-    rows = []
-    for values in (slot // batch, owner * batch + slot % batch):
-        row = jnp.zeros((1, half), jnp.int32)
+def table_rows(codes, owned):
+    groups = codes.shape[1]
+    number = KNB * lax.broadcasted_iota(jnp.int32, (groups, HD), 0)
+    column = lax.broadcasted_iota(jnp.int32, (groups, HD), 1)
+    which = lax.broadcasted_iota(jnp.int32, (TABLE, HD), 0)
+    table = jnp.zeros((TABLE, HD), jnp.float32)
+    for i, values in enumerate((codes // 256, codes % 256)):
+        values = values.astype(jnp.float32).astype(BF16)
         for k in range(KNB):
-            spread = jnp.where(column == number + k, values[:, k : k + 1], 0)
-            row = row + jnp.sum(spread, axis=0, keepdims=True)
-        rows.append(row)
-    which = lax.broadcasted_iota(jnp.int32, (TABLE, half), 0)
-    table = jnp.where(which == 0, rows[0], jnp.where(which == 1, rows[1], 0))
-    return table.astype(jnp.float32).astype(BF16)
-
-
-def pack_kernel(batch, place_ref, owner_ref, slot_ref, neigh_ref, out_ref):
+            spot = (column == number + k).astype(jnp.float32).astype(BF16)
+            table = table + jnp.where(which == i, dot_nn(values, spot)[k : k + 1], 0.0)
+    return table.astype(BF16)
+
+
+def pack_kernel(batch, place_ref, codes_ref, neigh_ref, out_ref):
     owned, rows, half = neigh_ref.shape
     parts = out_ref.shape[0]
     deep = rows // parts
     chooser = order_matrix(batch, parts, deep, False)
+    size = deep * batch
     for first in range(0, owned, batch):
         block = neigh_ref[first : first + batch].reshape(batch * rows, half)
-        moved = dot_nn(chooser, block).astype(BF16).reshape(parts, deep * batch, half)
-        out_ref[:, first * deep : (first + batch) * deep] = moved
-    table = table_rows(owner_ref[...], slot_ref[...], owned, half)
-    out_ref[:, owned * deep :] = jnp.broadcast_to(table[None], (parts, TABLE, half))
-
-
-def pack_rows(place, owner, slot, neighbours, parts):
+        moved = dot_nn(chooser, block).astype(BF16).reshape(parts, size, half)
+        for t in range(half // HD):
+            start = (first // batch * (half // HD) + t) * size
+            out_ref[:, start : start + size] = moved[:, :, t * HD : (t + 1) * HD]
+    table = table_rows(codes_ref[...], owned)
+    out_ref[:, owned * deep * half // HD :] = jnp.broadcast_to(table[None], (parts, TABLE, HD))
+
+
+def pack_rows(place, codes, neighbours, parts):
     owned, rows, features = neighbours.shape
     half = features // 2
-    message = owned * (rows // parts) + TABLE
+    message = owned * (rows // parts) * (half // HD) + TABLE
     batch = batch_of(owned)
     return pl.pallas_call(
         lambda *refs: pack_kernel(batch, *refs),
         grid_spec=pltpu.PrefetchScalarGridSpec(
             num_scalar_prefetch=1,
             grid=(1,),
-            in_specs=[whole(owner.shape)] * 2
-            + [pl.BlockSpec((owned, rows, half), lambda i, s: (0, 0, s[0]))],
-            out_specs=whole((parts, message, half)),
-        ),
-        out_shape=jax.ShapeDtypeStruct((parts, message, half), BF16),
-        compiler_params=params(60),
+            in_specs=[whole(codes.shape), pl.BlockSpec((owned, rows, half), lambda i, s: (0, 0, s[0]))],
+            out_specs=whole((parts, message, HD)),
+        ),
+        out_shape=jax.ShapeDtypeStruct((parts, message, HD), BF16),
+        compiler_params=params(16),
         cost_estimate=cost(3),
         name="pack_rows",
-    )(place, owner, slot, neighbours)
-
-
-def route_kernel(owned, batch, held_ref, *refs):
+    )(place, codes, neighbours)
+
+
+def route_kernel(owned, batch, columns, held_ref, *refs):
     out_ref = refs[-1]
-    owners, message, half = held_ref.shape
-    deep = (message - TABLE) // owned
+    owners, message, _ = held_ref.shape
+    size = (message - TABLE) * batch // (owned * columns)
+    deep = size // batch
     total = owners * owned
-    table = held_ref[:, owned * deep :, :].astype(jnp.float32).reshape(owners * TABLE, half)[:, :HD].T
+    table = held_ref[:, message - TABLE :].astype(jnp.float32).reshape(owners * TABLE, HD).T
     held = []
     for first in range(0, owned, batch):
-        block = held_ref[:, first * deep : (first + batch) * deep].astype(jnp.float32)
-        rows = [block[:, r * batch : (r + 1) * batch].reshape(owners * batch, half) for r in range(deep)]
-        held.append(jnp.concatenate(rows, axis=1).astype(BF16))
+        pieces = []
+        for t in range(columns):
+            start = (first // batch * columns + t) * size
+            block = held_ref[:, start : start + size].astype(jnp.float32)
+            pieces += [block[:, r * batch : (r + 1) * batch].reshape(owners * batch, HD) for r in range(deep)]
+        held.append(jnp.concatenate(pieces, axis=1).astype(BF16))
     held = jnp.concatenate(held, axis=0)
-    columns = lax.broadcasted_iota(jnp.int32, (owned, total), 1).astype(jnp.float32)
+    lanes = lax.broadcasted_iota(jnp.int32, (owned, total), 1).astype(jnp.float32)
     per_dot = min(8, owners)
-    for start in range(0, owners, per_dot):
+    for begin in range(0, owners, per_dot):
         choose = []
-        for s in range(start, start + per_dot):
+        for s in range(begin, begin + per_dot):
             high = table[:owned, s * TABLE : s * TABLE + 1]
             low = table[:owned, s * TABLE + 1 : s * TABLE + 2]
-            choose.append((high * float(owners * batch) + low == columns).astype(jnp.float32))
-        moved = dot_nn(jnp.concatenate(choose, axis=0).astype(BF16), held).reshape(per_dot, owned, deep * half)
+            choose.append((high * 256.0 + low == lanes).astype(jnp.float32))
+        moved = dot_nn(jnp.concatenate(choose, axis=0).astype(BF16), held)
+        moved = moved.reshape(per_dot, owned, columns * deep * HD)
         for first in range(0, owned, batch):
-            rows = [moved[:, first : first + batch, r * half : (r + 1) * half] for r in range(deep)]
-            place = pl.ds(first * deep, batch * deep)
-            out_ref[start : start + per_dot, place] = jnp.concatenate(rows, axis=1).astype(BF16)
-
-
-def route_rows(held, owned, after):
-    owners, message, half = held.shape
+            for t in range(columns):
+                start = (first // batch * columns + t) * size
+                pieces = [
+                    moved[:, first : first + batch, (t * deep + r) * HD : (t * deep + r + 1) * HD] for r in range(deep)
+                ]
+                out_ref[begin : begin + per_dot, start : start + size] = jnp.concatenate(pieces, axis=1).astype(BF16)
+
+
+def route_rows(held, owned, columns, after):
+    owners, message, _ = held.shape
     batch = batch_of(owned)
-    out_shape = (owners, message - TABLE, half)
-    return pl.pallas_call(
-        lambda *refs: route_kernel(owned, batch, *refs),
+    out_shape = (owners, message - TABLE, HD)
+    return pl.pallas_call(
+        lambda *refs: route_kernel(owned, batch, columns, *refs),
         grid=(1,),
         out_shape=jax.ShapeDtypeStruct(out_shape, BF16),
         in_specs=[whole(held.shape)] + [glance(x) for x in after],
@@ -165,16 +172,17 @@
     )(held, *after)
 
 
-def unpack_kernel(owned, batch, place_ref, arrived_ref, *refs):
+def unpack_kernel(owned, batch, columns, place_ref, arrived_ref, *refs):
     keep_ref, give_ref = refs[-2:]
-    parts, message, half = arrived_ref.shape
-    deep = message // owned
-    rows = parts * deep
-    chooser = order_matrix(batch, parts, deep, True)
+    parts, message, _ = arrived_ref.shape
+    size = message * batch // (owned * columns)
+    rows = parts * size // batch
+    chooser = order_matrix(batch, parts, size // batch, True)
     mine = owned // 2
     side = place_ref[0]
     for first in range(0, owned, batch):
-        block = arrived_ref[:, first * deep : (first + batch) * deep].reshape(batch * rows, half)
+        starts = [(first // batch * columns + t) * size for t in range(columns)]
+        block = jnp.concatenate([arrived_ref[:, x : x + size].reshape(parts * size, HD) for x in starts], axis=1)
         sorted_rows = dot_nn(chooser, block).astype(BF16)
         for n in range(first, first + batch, KNB):
             group = sorted_rows[(n - first) * rows : (n - first + KNB) * rows]
@@ -189,12 +197,11 @@
                 give_ref[place] = group
 
 
-def unpack_rows(place, arrived, owned, rows, after):
-    parts, message, half = arrived.shape
+def unpack_rows(place, arrived, owned, rows, columns, after):
     batch = batch_of(owned)
-    out_shape = (owned // 2 * rows, half)
-    return pl.pallas_call(
-        lambda *refs: unpack_kernel(owned, batch, *refs),
+    out_shape = (owned // 2 * rows, columns * HD)
+    return pl.pallas_call(
+        lambda *refs: unpack_kernel(owned, batch, columns, *refs),
         grid_spec=pltpu.PrefetchScalarGridSpec(
             num_scalar_prefetch=1,
             grid=(1,),
@@ -209,13 +216,13 @@
 
 
 def project_kernel(place_ref, *refs):
-    blocks, (own_w, other_w, own_out, other_out) = refs[:-4], refs[-4:]
+    pieces, (own_w, other_w, own_out, other_out) = refs[:-4], refs[-4:]
     step = pl.program_id(0)
-    for k, block_ref in enumerate(blocks):
+    for k in range(len(pieces) // 2):
 
         @pl.when(step == k)
         def _():
-            block = block_ref[...]
+            block = jnp.concatenate([pieces[2 * k][...], pieces[2 * k + 1][...]])
             own = dot_nn(block, own_w[...])
             other = dot_nn(block, other_w[...])
             own_out[...] = own if k == 0 else own_out[...] + own
@@ -224,20 +231,16 @@
 
 def project_last_kernel(place_ref, *refs):
     pieces, (own_in, other_in, own_w, other_w, own_out, other_out) = refs[:-6], refs[-6:]
-    first = 0
-    for piece_ref in pieces:
-        piece = piece_ref[...]
-        rows = slice(first, first + piece.shape[0])
-        own_out[rows] = (own_in[rows] + dot_nn(piece, own_w[...])).astype(BF16)
-        other_out[rows] = (other_in[rows] + dot_nn(piece, other_w[...])).astype(BF16)
-        first += piece.shape[0]
+    block = jnp.concatenate([piece_ref[...] for piece_ref in pieces])
+    own_out[...] = (own_in[...] + dot_nn(block, own_w[...])).astype(BF16)
+    other_out[...] = (other_in[...] + dot_nn(block, other_w[...])).astype(BF16)
 
 
 def project(place, masks, blocks, own_weight, other_weight, sums=None):
     depth = blocks[0].shape[1]
     width = own_weight.shape[1]
     final = sums is not None
-    tokens = sum(x.shape[0] for x in blocks) if final else blocks[0].shape[0]
+    tokens = 2 * blocks[0].shape[0]
 
     def mask_of(k):
         return sum(jnp.where(k == i, m, 0) for i, m in enumerate(masks))
@@ -254,7 +257,7 @@
             out_specs=[out_spec] * 2,
         ),
         out_shape=[shape, shape],
-        compiler_params=params(60),
+        compiler_params=params(24),
         cost_estimate=cost(2.5 * len(masks)),
         name="project",
     )(place, *blocks, *(sums or ()), own_weight, other_weight)
@@ -513,23 +516,31 @@
     tokens = states.shape[0] // 2
     owned, rows, features = neighbours.shape
 
-    held = lax.dynamic_slice_in_dim(states, side * tokens, tokens, 0)
+    low = tokens // 2
+    held = [lax.dynamic_slice_in_dim(states, side * tokens + first, low, 0) for first in (0, low)]
     if tp_count == 2:
-        blocks, masks, last = [held], [0], [swap(held, 1)]
+        blocks, masks, early, last = held, [0], [], [swap(x, 1) for x in held]
     else:
-        low = tokens // 2
-        blocks, masks = [held, swap(held, 1), swap(held, 3)], [0, 1, 3]
-        last = [swap(blocks[2][:low], 1), swap(blocks[1][low:], 3)]
+        masks = [0, 1, 3]
+        near1, near3 = ([swap(x, mask) for x in held] for mask in masks[1:])
+        blocks = held + near1 + near3
+        last = [swap(near3[0], 1), swap(near1[1], 3)]
+        early = near1 + near3
     own_weight = projections[0]
     other_weight = swap_cores(own_weight)
-    packed = pack_rows(place, owner, slot, neighbours, shards_)
+
+    batch = batch_of(owned)
+    columns = features // 2 // HD
+    owner, slot = owner.T, slot.T
+    codes = slot // batch * (shards_ * batch) + owner * batch + slot % batch
+    packed = pack_rows(place, codes, neighbours, shards_)
     parts = lax.all_to_all(packed, "seq", split_axis=0, concat_axis=0, tiled=True)
-    routed = route_rows(parts, owned, [block[:16, :HD] for block in blocks[1:]])
+    routed = route_rows(parts, owned, columns, [x[:16, :HD] for x in early])
     arrived = lax.all_to_all(routed, "seq", split_axis=0, concat_axis=0, tiled=True)
 
     sums = project(place, masks, blocks, own_weight, other_weight)
     own, other = project(place, [tp_count // 2], last, own_weight, other_weight, sums)
-    near, give = unpack_rows(place, arrived, owned, rows, [own[:16, :HD]])
+    near, give = unpack_rows(place, arrived, owned, rows, columns, [own[:16, :HD]])
     far = swap_cores(give)
     grad_own, grad_other, across_low, across_high = attend(
         place, own, other, cotangent, near, far, own_weight, other_weight

time: 120 us -> 117 us (0.975)
  waiting for transfers between devices: 38.2 us -> 43.9 us
  Pallas kernels: 35.2 us -> 29.6 us
  local copies, waits for them, and re-layouts: 7.16 us -> 3.68 us
    all_to_all x1, waiting for transfers between devices: 1.25 us -> 6.91 us  [shards(): lax.all_to_all(routed, 'seq', split_axis=0, concat_axis=0, tiled=True)]
    pallas_call x2, Pallas kernels: 12.4 us -> 8.05 us  [project(): pl.pallas_call(project_last_kernel if final else project_kernel, grid_spe...]
    slice x5, local copies, waits for them, and re-layouts: 2.73 us -> 0.01 us  [the longest x4 0.01 us: shards(): routed = route_rows(parts, owned, columns, [x[:16, :HD] for x in early])]
    pallas_call x1, Pallas kernels: 3.36 us -> 2.06 us  [pack_rows(): pl.pallas_call(lambda *refs: pack_kernel(batch, *refs), grid_spec=pltpu.P...]
    unnamed x24 -> x12, local copies, waits for them, and re-layouts: 4.37 us -> 3.61 us
    ppermute x4 -> x6, starting transfers between devices: 5.46 us -> 6.02 us  [swap(): return lax.ppermute(block, 'tp', [(i, i ^ mask) for i in range(count)])]
    ppermute x4 -> x6, waiting for transfers between devices: 18 us -> 17.5 us  [swap(): return lax.ppermute(block, 'tp', [(i, i ^ mask) for i in range(count)])]
  transfers between devices with their start and end apart: 15 -> 17, of which waited for: 11 -> 13; matrix products, arithmetic and copies ran while one was open for 5% -> 1% of each run, Pallas kernels for 20% -> 16%
where the time goes in v4:
time: 117 us; the launch traced here: 116 us
  waiting for transfers between devices  43.9 us (38%)
  starting transfers between devices  38.2 us (33%)
  Pallas kernels  29.6 us (25%)
  local copies, waits for them, and re-layouts  3.68 us (3%)
    ppermute x6, waiting for transfers between devices, swap(): return lax.ppermute(block, 'tp', [(i, i ^ mask) for i in range(count)])  17.5 us
    ppermute x6, waiting for transfers between devices, shift(): lax.ppermute(block, 'tp', [(i, (i + step) % count) for i in range(count)])  14.6 us
    all_to_all x1, starting transfers between devices, shards(): lax.all_to_all(packed, 'seq', split_axis=0, concat_axis=0, tiled=True)  9.6 us
    ppermute x3, starting transfers between devices, swap_cores(): return lax.ppermute(block, 'grp', [(0, 1), (1, 0)])  8.91 us
    pallas_call x2, Pallas kernels, project(): pl.pallas_call(project_last_kernel if final else project_kernel, grid_spe...  8.05 us
    ppermute x6, starting transfers between devices, shift(): lax.ppermute(block, 'tp', [(i, (i + step) % count) for i in range(count)])  7.04 us
    all_to_all x1, waiting for transfers between devices, shards(): lax.all_to_all(routed, 'seq', split_axis=0, concat_axis=0, tiled=True)  6.91 us
    pallas_call x1, Pallas kernels, attend(): pl.pallas_call(lambda *refs: attend_kernel(tp_count, tp_count // 2, *refs...  6.69 us
  transfers between devices with their start and end apart: 17, of which 13 were waited for; matrix products, arithmetic and copies ran while one was open for 1% of the time, Pallas kernels for 16%

profile of v4, /device:TPU:1, one launch (start us, length us, event | category | flops | bytes accessed | tf_op | source)
XLA Modules:
  0.0 116.3 jit_solution(3057574521390164928)
XLA Ops:
  0.0 3.2 %collective-permute-start.6 = (bf16[4096,512]{1,0:T(8,128)(2,1)}, bf16[4096,512]{1,0:T(8,128)(2,1)}, u32[]{:S(2)}, u32[]{:S(2)}) collective-permute-start(bf16[4096,512]{1,0:T(8,128)(2,1)} %bitcast.21), channel_id=1, source_target_pairs={{0,128},{128,0},{1,129},{129,1},{2,130},{130,2},{3,131},{131,3},{4... | collective-permute-start | bytes 12582920 | tf_op jit(solution)/shard_map/ppermute | solution.py:45
  4.0 1.4 %copy-done.3 = bf16[24,64,512]{2,1,0:T(8,128)(2,1)S(1)} copy-done((bf16[24,64,512]{2,1,0:T(8,128)(2,1)S(1)}, bf16[24,64,512]{2,1,0:T(8,128)(2,1)}, u32[]{:S(2)}) %copy-start.3) | copy-done | bytes 1572888
  5.4 2.1 %pack_rows.1 = bf16[32,104,128]{2,1,0:T(8,128)(2,1)} custom-call(s32[2]{0:T(128)S(1)} %pad_add_fusion.place_ref.refs_0_, s32[2,12]{1,0:T(2,128)S(1)} %fusion.refs_1_, bf16[24,64,512]{2,1,0:T(8,128)(2,1)S(1)} %copy-done.3), custom_call_target="tpu_custom_call" | custom-call | flops 3000000000 | bytes 3000000 | tf_op jit(solution)/shard_map/pack_rows/pallas_call | solution.py:109
  7.5 9.6 %all-to-all-start = ((bf16[32,104,128]{2,1,0:T(8,128)(2,1)}), bf16[32,104,128]{2,1,0:T(8,128)(2,1)S(1)}, u32[]{:S(2)}, u32[]{:S(2)}) async-start(bf16[32,104,128]{2,1,0:T(8,128)(2,1)} %pack_rows.1), calls=%async_computation | async-start | bytes 1703936 | tf_op jit(solution)/shard_map/all_to_all | solution.py:537
  17.2 1.3 %collective-permute-start.2 = (bf16[192,1024]{1,0:T(8,128)(2,1)S(1)}, bf16[192,1024]{1,0:T(8,128)(2,1)S(1)}, u32[]{:S(2)}, u32[]{:S(2)}) collective-permute-start(bf16[192,1024]{1,0:T(8,128)(2,1)S(1)} %get-tuple-element.41.refs_1_), channel_id=1, source_target_pairs={{0,1},{1,0},{2,3},{3,2},{4,5},{5,4},{6,7},{7,6},{8,9},{9,8},{10,11... | collective-permute-start | bytes 1179656 | tf_op jit(solution)/shard_map/ppermute | solution.py:55
  18.5 1.8 %collective-permute-start = (bf16[192,1024]{1,0:T(8,128)(2,1)S(1)}, bf16[192,1024]{1,0:T(8,128)(2,1)S(1)}, u32[]{:S(2)}, u32[]{:S(2)}) collective-permute-start(bf16[192,1024]{1,0:T(8,128)(2,1)S(1)} %get-tuple-element.42.refs_0_), channel_id=1, source_target_pairs={{0,3},{1,2},{2,1},{3,0},{4,7},{5,6},{6,5},{7,4},{8,11},{9,10},{10,... | collective-permute-start | bytes 1179656 | tf_op jit(solution)/shard_map/ppermute | solution.py:55
  21.2 6.5 %collective-permute-done.2.refs_3_ = bf16[192,1024]{1,0:T(8,128)(2,1)S(1)} collective-permute-done((bf16[192,1024]{1,0:T(8,128)(2,1)S(1)}, bf16[192,1024]{1,0:T(8,128)(2,1)S(1)}, u32[]{:S(2)}, u32[]{:S(2)}) %collective-permute-start.2) | collective-permute-done | bytes 393248 | tf_op jit(solution)/shard_map/ppermute | solution.py:55
  27.7 2.1 %collective-permute-done.refs_4_ = bf16[192,1024]{1,0:T(8,128)(2,1)S(1)} collective-permute-done((bf16[192,1024]{1,0:T(8,128)(2,1)S(1)}, bf16[192,1024]{1,0:T(8,128)(2,1)S(1)}, u32[]{:S(2)}, u32[]{:S(2)}) %collective-permute-start) | collective-permute-done | bytes 393248 | tf_op jit(solution)/shard_map/ppermute | solution.py:55
  29.8 6.3 %collective-permute-done.4.refs_2_ = bf16[192,1024]{1,0:T(8,128)(2,1)S(1)} collective-permute-done((bf16[192,1024]{1,0:T(8,128)(2,1)S(1)}, bf16[192,1024]{1,0:T(8,128)(2,1)S(1)}, u32[]{:S(2)}, u32[]{:S(2)}) %collective-permute-start.4) | collective-permute-done | bytes 393248 | tf_op jit(solution)/shard_map/ppermute | solution.py:55
  36.1 2.1 %collective-permute-done.5.refs_5_ = bf16[192,1024]{1,0:T(8,128)(2,1)S(1)} collective-permute-done((bf16[192,1024]{1,0:T(8,128)(2,1)S(1)}, bf16[192,1024]{1,0:T(8,128)(2,1)S(1)}, u32[]{:S(2)}, u32[]{:S(2)}) %collective-permute-start.5) | collective-permute-done | bytes 393248 | tf_op jit(solution)/shard_map/ppermute | solution.py:55
  38.2 2.3 %all-to-all-done.refs_0_ = bf16[32,104,128]{2,1,0:T(8,128)(2,1)S(1)} async-done(((bf16[32,104,128]{2,1,0:T(8,128)(2,1)}), bf16[32,104,128]{2,1,0:T(8,128)(2,1)S(1)}, u32[]{:S(2)}, u32[]{:S(2)}) %all-to-all-start) | async-done | bytes 852000 | tf_op jit(solution)/shard_map/all_to_all | solution.py:537
  40.5 1.9 %route_rows.1 = bf16[32,96,128]{2,1,0:T(8,128)(2,1)} custom-call(bf16[32,104,128]{2,1,0:T(8,128)(2,1)S(1)} %all-to-all-done.refs_0_, bf16[16,128]{1,0:T(8,128)(2,1)S(1)} %slice.20.refs_1_, bf16[16,128]{1,0:T(8,128)(2,1)S(1)} %slice.21.refs_2_, bf16[16,128]{1,0:T(8,128)(2,1)S(1)} %slice.22.refs_3_, bf16[16,128]{1,0:T(8,128)(2,1)S(1)} %slice.23.refs_4_), custom_call_target="tpu_custom_call" | custom-call | flops 2000000000 | bytes 2000000 | tf_op jit(solution)/shard_map/route_rows/pallas_call | solution.py:163
  42.4 6.6 %all-to-all-start.1 = ((bf16[32,96,128]{2,1,0:T(8,128)(2,1)}), bf16[32,96,128]{2,1,0:T(8,128)(2,1)S(1)}, u32[]{:S(2)}, u32[]{:S(2)}) async-start(bf16[32,96,128]{2,1,0:T(8,128)(2,1)} %route_rows.1), calls=%async_computation.1 | async-start | bytes 1572864 | tf_op jit(solution)/shard_map/all_to_all | solution.py:539
  49.1 1.9 %collective-permute-start.3 = (bf16[192,1024]{1,0:T(8,128)(2,1)S(1)}, bf16[192,1024]{1,0:T(8,128)(2,1)S(1)}, u32[]{:S(2)}, u32[]{:S(2)}) collective-permute-start(bf16[192,1024]{1,0:T(8,128)(2,1)S(1)} %collective-permute-done.2.refs_3_), channel_id=1, source_target_pairs={{0,3},{1,2},{2,1},{3,0},{4,7},{5,6},{6,5},{7,4},{8,11},{9,10},{10,... | collective-permute-start | bytes 1179656 | tf_op jit(solution)/shard_map/ppermute | solution.py:55
  51.0 2.2 %copy-done = bf16[1,4096,512]{2,1,0:T(8,128)(2,1)S(1)} copy-done((bf16[1,4096,512]{2,1,0:T(8,128)(2,1)S(1)}, bf16[1,4096,512]{2,1,0:T(8,128)(2,1)}, u32[]{:S(2)}) %copy-start) | copy-done | bytes 4194328
  53.2 5.3 %project.2 = (f32[384,512]{1,0:T(8,128)S(1)}, f32[384,512]{1,0:T(8,128)S(1)}) custom-call(s32[2]{0:T(128)S(1)} %pad_add_fusion.place_ref.refs_0_, bf16[192,1024]{1,0:T(8,128)(2,1)S(1)} %get-tuple-element.42.refs_0_, bf16[192,1024]{1,0:T(8,128)(2,1)S(1)} %get-tuple-element.41.refs_1_, bf16[192,1024]{1,0:T(8,128)(2,1)S(1)} %collective-permute-done.4.refs_2_, ...), custom_call_target="tpu_custom_call" | custom-call | flops 7500000256 | bytes 7500000 | tf_op jit(solution)/shard_map/project/pallas_call | solution.py:251
  59.0 2.8 %project.3 = (bf16[384,512]{1,0:T(8,128)(2,1)S(1)}, bf16[384,512]{1,0:T(8,128)(2,1)S(1)}) custom-call(s32[2]{0:T(128)S(1)} %pad_add_fusion.place_ref.refs_0_, bf16[192,1024]{1,0:T(8,128)(2,1)S(1)} %collective-permute-done.1.refs_0_, bf16[192,1024]{1,0:T(8,128)(2,1)S(1)} %collective-permute-done.3.refs_1_, f32[384,512]{1,0:T(8,128)S(1)} %get-tuple-element.23.refs_2_, ...), custom_call_target="tpu_custom_call" | custom-call | flops 2500000000 | bytes 2500000 | tf_op jit(solution)/shard_map/project/pallas_call | solution.py:251
  61.8 6.9 %all-to-all-done.1.refs_1_ = bf16[32,96,128]{2,1,0:T(8,128)(2,1)S(1)} async-done(((bf16[32,96,128]{2,1,0:T(8,128)(2,1)}), bf16[32,96,128]{2,1,0:T(8,128)(2,1)S(1)}, u32[]{:S(2)}, u32[]{:S(2)}) %all-to-all-start.1) | async-done | bytes 786464 | tf_op jit(solution)/shard_map/all_to_all | solution.py:539
  68.7 1.8 %unpack_rows.1 = (bf16[768,256]{1,0:T(8,128)(2,1)S(1)}, bf16[768,256]{1,0:T(8,128)(2,1)S(1)}) custom-call(s32[2]{0:T(128)S(1)} %pad_add_fusion.place_ref.refs_0_, bf16[32,96,128]{2,1,0:T(8,128)(2,1)S(1)} %all-to-all-done.1.refs_1_, bf16[16,128]{1,0:T(8,128)(2,1)S(1)} %slice.19.refs_2_), custom_call_target="tpu_custom_call" | custom-call | flops 2000000000 | bytes 2000000 | tf_op jit(solution)/shard_map/unpack_rows/pallas_call | solution.py:203
  70.5 4.4 %collective-permute-start.7 = (bf16[768,256]{1,0:T(8,128)(2,1)S(1)}, bf16[768,256]{1,0:T(8,128)(2,1)S(1)}, u32[]{:S(2)}, u32[]{:S(2)}) collective-permute-start(bf16[768,256]{1,0:T(8,128)(2,1)S(1)} %get-tuple-element.28), channel_id=1, source_target_pairs={{0,128},{128,0},{1,129},{129,1},{2,130},{130,2},{3,131},{131,3},{4... | collective-permute-start | bytes 1179656 | tf_op jit(solution)/shard_map/ppermute | solution.py:45
  74.9 1.3 %collective-permute-done.7.refs_5_ = bf16[768,256]{1,0:T(8,128)(2,1)S(1)} collective-permute-done((bf16[768,256]{1,0:T(8,128)(2,1)S(1)}, bf16[768,256]{1,0:T(8,128)(2,1)S(1)}, u32[]{:S(2)}, u32[]{:S(2)}) %collective-permute-start.7) | collective-permute-done | bytes 393248 | tf_op jit(solution)/shard_map/ppermute | solution.py:45
  76.2 6.7 %attend.1 = (bf16[384,512]{1,0:T(8,128)(2,1)S(1)}, bf16[384,512]{1,0:T(8,128)(2,1)S(1)}, bf16[192,1024]{1,0:T(8,128)(2,1)S(1)}, bf16[192,1024]{1,0:T(8,128)(2,1)S(1)}) custom-call(s32[2]{0:T(128)S(1)} %pad_add_fusion.place_ref.refs_0_, bf16[384,512]{1,0:T(8,128)(2,1)S(1)} %get-tuple-element.25.refs_1_, bf16[384,512]{1,0:T(8,128)(2,1)S(1)} %get-tuple-element.26.refs_2_, ...), custom_call_target="tpu_custom_call" | custom-call | flops 8000000000 | bytes 8000000 | tf_op jit(solution)/shard_map/attend/pallas_call | solution.py:370
  83.0 2.7 %collective-permute-start.9 = (bf16[192,1024]{1,0:T(8,128)(2,1)S(1)}, bf16[192,1024]{1,0:T(8,128)(2,1)S(1)}, u32[]{:S(2)}, u32[]{:S(2)}) collective-permute-start(bf16[192,1024]{1,0:T(8,128)(2,1)S(1)} %get-tuple-element.34), channel_id=1, source_target_pairs={{0,3},{1,0},{2,1},{3,2},{4,7},{5,4},{6,5},{7,6},{8,11},{9,8},{10,9... | collective-permute-start | bytes 1179656 | tf_op jit(solution)/shard_map/ppermute | solution.py:50
  85.7 3.9 %partial_terms.2 = (bf16[192,1024]{1,0:T(8,128)(2,1)S(1)}, bf16[192,1024]{1,0:T(8,128)(2,1)S(1)}, bf16[192,1024]{1,0:T(8,128)(2,1)S(1)}, bf16[192,1024]{1,0:T(8,128)(2,1)S(1)}) custom-call(s32[2]{0:T(128)S(1)} %pad_add_fusion.place_ref.refs_0_, bf16[384,512]{1,0:T(8,128)(2,1)S(1)} %get-tuple-element.29.refs_1_, ...), custom_call_target="tpu_custom_call" | custom-call | flops 4000000000 | bytes 4000000 | tf_op jit(solution)/shard_map/partial_terms/pallas_call | solution.py:416
  91.1 3.4 %collective-permute-done.8.refs_2_ = bf16[192,1024]{1,0:T(8,128)(2,1)S(1)} collective-permute-done((bf16[192,1024]{1,0:T(8,128)(2,1)S(1)}, bf16[192,1024]{1,0:T(8,128)(2,1)S(1)}, u32[]{:S(2)}, u32[]{:S(2)}) %collective-permute-start.8) | collective-permute-done | bytes 393248 | tf_op jit(solution)/shard_map/ppermute | solution.py:50
  94.8 2.7 %collective-permute-start.13 = (bf16[192,1024]{1,0:T(8,128)(2,1)S(1)}, bf16[192,1024]{1,0:T(8,128)(2,1)S(1)}, u32[]{:S(2)}, u32[]{:S(2)}) collective-permute-start(bf16[192,1024]{1,0:T(8,128)(2,1)S(1)} %get-tuple-element.40), channel_id=1, source_target_pairs={{0,3},{1,0},{2,1},{3,2},{4,7},{5,4},{6,5},{7,6},{8,11},{9,8},{10,9... | collective-permute-start | bytes 1179656 | tf_op jit(solution)/shard_map/ppermute | solution.py:50
  97.5 2.8 %partial_terms.3 = (bf16[192,1024]{1,0:T(8,128)(2,1)S(1)}, bf16[192,1024]{1,0:T(8,128)(2,1)S(1)}) custom-call(s32[2]{0:T(128)S(1)} %pad_add_fusion.place_ref.refs_0_, bf16[384,512]{1,0:T(8,128)(2,1)S(1)} %get-tuple-element.29.refs_1_, bf16[384,512]{1,0:T(8,128)(2,1)S(1)} %get-tuple-element.30.refs_2_, bf16[4096,512]{1,0:T(8,128)(2,1)S(1)} %bitcast.27, ...), custom_call_target="tpu_custom_call" | custom-call | flops 2000000000 | bytes 2000000 | tf_op jit(solution)/shard_map/partial_terms/pallas_call | solution.py:416
  100.2 1.7 %collective-permute-done.10.refs_1_ = bf16[192,1024]{1,0:T(8,128)(2,1)S(1)} collective-permute-done((bf16[192,1024]{1,0:T(8,128)(2,1)S(1)}, bf16[192,1024]{1,0:T(8,128)(2,1)S(1)}, u32[]{:S(2)}, u32[]{:S(2)}) %collective-permute-start.10) | collective-permute-done | bytes 393248 | tf_op jit(solution)/shard_map/ppermute | solution.py:50
  103.0 8.4 %collective-permute-done.11.refs_2_ = bf16[192,1024]{1,0:T(8,128)(2,1)S(1)} collective-permute-done((bf16[192,1024]{1,0:T(8,128)(2,1)S(1)}, bf16[192,1024]{1,0:T(8,128)(2,1)S(1)}, u32[]{:S(2)}, u32[]{:S(2)}) %collective-permute-start.11) | collective-permute-done | bytes 393248 | tf_op jit(solution)/shard_map/ppermute | solution.py:50
  112.1 1.3 %collective-permute-start.14 = (bf16[384,512]{1,0:T(8,128)(2,1)S(1)}, bf16[384,512]{1,0:T(8,128)(2,1)S(1)}, u32[]{:S(2)}, u32[]{:S(2)}) collective-permute-start(bf16[384,512]{1,0:T(8,128)(2,1)S(1)} %sum_columns.2), channel_id=1, source_target_pairs={{0,128},{128,0},{1,129},{129,1},{2,130},{130,2},{3,131},{131,3},{4... | collective-permute-start | bytes 1179656 | tf_op jit(solution)/shard_map/ppermute | solution.py:45
  113.4 1.3 %collective-permute-done.14.refs_6_ = bf16[384,512]{1,0:T(8,128)(2,1)S(1)} collective-permute-done((bf16[384,512]{1,0:T(8,128)(2,1)S(1)}, bf16[384,512]{1,0:T(8,128)(2,1)S(1)}, u32[]{:S(2)}, u32[]{:S(2)}) %collective-permute-start.14) | collective-permute-done | bytes 393248 | tf_op jit(solution)/shard_map/ppermute | solution.py:45
  114.7 1.6 %sum_columns.3 = bf16[768,512]{1,0:T(8,128)(2,1)} custom-call(s32[2]{0:T(128)S(1)} %pad_add_fusion.place_ref.refs_0_, bf16[192,1024]{1,0:T(8,128)(2,1)S(1)} %get-tuple-element.36.refs_0_, bf16[192,1024]{1,0:T(8,128)(2,1)S(1)} %collective-permute-done.10.refs_1_, bf16[192,1024]{1,0:T(8,128)(2,1)S(1)} %collective-permute-done.11.refs_2_, ...), custom_call_target="tpu_custom_call" | custom-call | flops 1000000000 | bytes 1000000 | tf_op jit(solution)/shard_map/sum_columns/pallas_call | solution.py:496
  (33 shorter events, 6.1 us)
Async XLA Ops:
  0.0 51.0 %collective-permute-start.6 = (bf16[4096,512]{1,0:T(8,128)(2,1)}, bf16[4096,512]{1,0:T(8,128)(2,1)}, u32[]{:S(2)}, u32[]{:S(2)}) collective-permute-start(bf16[4096,512]{1,0:T(8,128)(2,1)} %bitcast.21), channel_id=1, source_target_pairs={{0,128},{128,0},{1,129},{129,1},{2,130},{130,2},{3,131},{131,3},{4... | collective-permute-start | bytes 12582920 | tf_op jit(solution)/shard_map/ppermute | solution.py:45
  4.0 1.4 %copy-start.3 = (bf16[24,64,512]{2,1,0:T(8,128)(2,1)S(1)}, bf16[24,64,512]{2,1,0:T(8,128)(2,1)}, u32[]{:S(2)}) copy-start(bf16[24,64,512]{2,1,0:T(8,128)(2,1)} %refs_2_.1) | copy-start | bytes 4718596
  7.5 9.6 %copy-start.5 = (bf16[768,1024]{1,0:T(8,128)(2,1)S(1)}, bf16[768,1024]{1,0:T(8,128)(2,1)}, u32[]{:S(2)}) copy-start(bf16[768,1024]{1,0:T(8,128)(2,1)} %param.6) | copy-start | bytes 4718596
  7.5 33.0 %all-to-all-start = ((bf16[32,104,128]{2,1,0:T(8,128)(2,1)}), bf16[32,104,128]{2,1,0:T(8,128)(2,1)S(1)}, u32[]{:S(2)}, u32[]{:S(2)}) async-start(bf16[32,104,128]{2,1,0:T(8,128)(2,1)} %pack_rows.1), calls=%async_computation | async-start | bytes 1703936 | tf_op jit(solution)/shard_map/all_to_all | solution.py:537
  17.2 10.5 %collective-permute-start.2 = (bf16[192,1024]{1,0:T(8,128)(2,1)S(1)}, bf16[192,1024]{1,0:T(8,128)(2,1)S(1)}, u32[]{:S(2)}, u32[]{:S(2)}) collective-permute-start(bf16[192,1024]{1,0:T(8,128)(2,1)S(1)} %get-tuple-element.41.refs_1_), channel_id=1, source_target_pairs={{0,1},{1,0},{2,3},{3,2},{4,5},{5,4},{6,7},{7,6},{8,9},{9,8},{10,11... | collective-permute-start | bytes 1179656 | tf_op jit(solution)/shard_map/ppermute | solution.py:55
  18.5 11.3 %collective-permute-start = (bf16[192,1024]{1,0:T(8,128)(2,1)S(1)}, bf16[192,1024]{1,0:T(8,128)(2,1)S(1)}, u32[]{:S(2)}, u32[]{:S(2)}) collective-permute-start(bf16[192,1024]{1,0:T(8,128)(2,1)S(1)} %get-tuple-element.42.refs_0_), channel_id=1, source_target_pairs={{0,3},{1,2},{2,1},{3,0},{4,7},{5,6},{6,5},{7,4},{8,11},{9,10},{10,... | collective-permute-start | bytes 1179656 | tf_op jit(solution)/shard_map/ppermute | solution.py:55
  20.3 15.8 %collective-permute-start.4 = (bf16[192,1024]{1,0:T(8,128)(2,1)S(1)}, bf16[192,1024]{1,0:T(8,128)(2,1)S(1)}, u32[]{:S(2)}, u32[]{:S(2)}) collective-permute-start(bf16[192,1024]{1,0:T(8,128)(2,1)S(1)} %get-tuple-element.42.refs_0_), channel_id=1, source_target_pairs={{0,1},{1,0},{2,3},{3,2},{4,5},{5,4},{6,7},{7,6},{8,9},{9,8},{10,11... | collective-permute-start | bytes 1179656 | tf_op jit(solution)/shard_map/ppermute | solution.py:55
  20.6 17.6 %collective-permute-start.5 = (bf16[192,1024]{1,0:T(8,128)(2,1)S(1)}, bf16[192,1024]{1,0:T(8,128)(2,1)S(1)}, u32[]{:S(2)}, u32[]{:S(2)}) collective-permute-start(bf16[192,1024]{1,0:T(8,128)(2,1)S(1)} %get-tuple-element.41.refs_1_), channel_id=1, source_target_pairs={{0,3},{1,2},{2,1},{3,0},{4,7},{5,6},{6,5},{7,4},{8,11},{9,10},{10,... | collective-permute-start | bytes 1179656 | tf_op jit(solution)/shard_map/ppermute | solution.py:55
  42.4 26.3 %all-to-all-start.1 = ((bf16[32,96,128]{2,1,0:T(8,128)(2,1)}), bf16[32,96,128]{2,1,0:T(8,128)(2,1)S(1)}, u32[]{:S(2)}, u32[]{:S(2)}) async-start(bf16[32,96,128]{2,1,0:T(8,128)(2,1)} %route_rows.1), calls=%async_computation.1 | async-start | bytes 1572864 | tf_op jit(solution)/shard_map/all_to_all | solution.py:539
  49.0 9.5 %collective-permute-start.1 = (bf16[192,1024]{1,0:T(8,128)(2,1)S(1)}, bf16[192,1024]{1,0:T(8,128)(2,1)S(1)}, u32[]{:S(2)}, u32[]{:S(2)}) collective-permute-start(bf16[192,1024]{1,0:T(8,128)(2,1)S(1)} %collective-permute-done.refs_4_), channel_id=1, source_target_pairs={{0,1},{1,0},{2,3},{3,2},{4,5},{5,4},{6,7},{7,6},{8,9},{9,8},{10,11... | collective-permute-start | bytes 1179656 | tf_op jit(solution)/shard_map/ppermute | solution.py:55
  49.1 9.9 %collective-permute-start.3 = (bf16[192,1024]{1,0:T(8,128)(2,1)S(1)}, bf16[192,1024]{1,0:T(8,128)(2,1)S(1)}, u32[]{:S(2)}, u32[]{:S(2)}) collective-permute-start(bf16[192,1024]{1,0:T(8,128)(2,1)S(1)} %collective-permute-done.2.refs_3_), channel_id=1, source_target_pairs={{0,3},{1,2},{2,1},{3,0},{4,7},{5,6},{6,5},{7,4},{8,11},{9,10},{10,... | collective-permute-start | bytes 1179656 | tf_op jit(solution)/shard_map/ppermute | solution.py:55
  51.0 2.2 %copy-start = (bf16[1,4096,512]{2,1,0:T(8,128)(2,1)S(1)}, bf16[1,4096,512]{2,1,0:T(8,128)(2,1)}, u32[]{:S(2)}) copy-start(bf16[1,4096,512]{2,1,0:T(8,128)(2,1)} %param.7) | copy-start | bytes 12582916
  53.2 5.8 %copy-start.1 = (bf16[1,4096,512]{2,1,0:T(8,128)(2,1)S(1)}, bf16[1,4096,512]{2,1,0:T(8,128)(2,1)}, u32[]{:S(2)}) copy-start(bf16[1,4096,512]{2,1,0:T(8,128)(2,1)} %param.7) | copy-start | bytes 12582916
  61.8 14.4 %copy-start.4 = (bf16[768,512]{1,0:T(8,128)(2,1)S(1)}, bf16[768,512]{1,0:T(8,128)(2,1)}, u32[]{:S(2)}) copy-start(bf16[768,512]{1,0:T(8,128)(2,1)} %refs_3_.1) | copy-start | bytes 2359300
  68.7 7.5 %copy-start.2 = (bf16[1,4096,512]{2,1,0:T(8,128)(2,1)S(1)}, bf16[1,4096,512]{2,1,0:T(8,128)(2,1)}, u32[]{:S(2)}) copy-start(bf16[1,4096,512]{2,1,0:T(8,128)(2,1)} %param.7) | copy-start | bytes 12582916
  70.5 5.7 %collective-permute-start.7 = (bf16[768,256]{1,0:T(8,128)(2,1)S(1)}, bf16[768,256]{1,0:T(8,128)(2,1)S(1)}, u32[]{:S(2)}, u32[]{:S(2)}) collective-permute-start(bf16[768,256]{1,0:T(8,128)(2,1)S(1)} %get-tuple-element.28), channel_id=1, source_target_pairs={{0,128},{128,0},{1,129},{129,1},{2,130},{130,2},{3,131},{131,3},{4... | collective-permute-start | bytes 1179656 | tf_op jit(solution)/shard_map/ppermute | solution.py:45
  82.9 11.6 %collective-permute-start.8 = (bf16[192,1024]{1,0:T(8,128)(2,1)S(1)}, bf16[192,1024]{1,0:T(8,128)(2,1)S(1)}, u32[]{:S(2)}, u32[]{:S(2)}) collective-permute-start(bf16[192,1024]{1,0:T(8,128)(2,1)S(1)} %get-tuple-element.33), channel_id=1, source_target_pairs={{0,1},{1,2},{2,3},{3,0},{4,5},{5,6},{6,7},{7,4},{8,9},{9,10},{10,1... | collective-permute-start | bytes 1179656 | tf_op jit(solution)/shard_map/ppermute | solution.py:50
  83.0 11.5 %collective-permute-start.9 = (bf16[192,1024]{1,0:T(8,128)(2,1)S(1)}, bf16[192,1024]{1,0:T(8,128)(2,1)S(1)}, u32[]{:S(2)}, u32[]{:S(2)}) collective-permute-start(bf16[192,1024]{1,0:T(8,128)(2,1)S(1)} %get-tuple-element.34), channel_id=1, source_target_pairs={{0,3},{1,0},{2,1},{3,2},{4,7},{5,4},{6,5},{7,6},{8,11},{9,8},{10,9... | collective-permute-start | bytes 1179656 | tf_op jit(solution)/shard_map/ppermute | solution.py:50
  89.6 12.3 %collective-permute-start.10 = (bf16[192,1024]{1,0:T(8,128)(2,1)S(1)}, bf16[192,1024]{1,0:T(8,128)(2,1)S(1)}, u32[]{:S(2)}, u32[]{:S(2)}) collective-permute-start(bf16[192,1024]{1,0:T(8,128)(2,1)S(1)} %get-tuple-element.37), channel_id=1, source_target_pairs={{0,3},{1,0},{2,1},{3,2},{4,7},{5,4},{6,5},{7,6},{8,11},{9,8},{10,9... | collective-permute-start | bytes 1179656 | tf_op jit(solution)/shard_map/ppermute | solution.py:50
  90.2 12.7 %collective-permute-start.12 = (bf16[192,1024]{1,0:T(8,128)(2,1)S(1)}, bf16[192,1024]{1,0:T(8,128)(2,1)S(1)}, u32[]{:S(2)}, u32[]{:S(2)}) collective-permute-start(bf16[192,1024]{1,0:T(8,128)(2,1)S(1)} %get-tuple-element.39), channel_id=1, source_target_pairs={{0,1},{1,2},{2,3},{3,0},{4,5},{5,6},{6,7},{7,4},{8,9},{9,10},{10,1... | collective-permute-start | bytes 1179656 | tf_op jit(solution)/shard_map/ppermute | solution.py:50
  94.7 16.7 %collective-permute-start.11 = (bf16[192,1024]{1,0:T(8,128)(2,1)S(1)}, bf16[192,1024]{1,0:T(8,128)(2,1)S(1)}, u32[]{:S(2)}, u32[]{:S(2)}) collective-permute-start(bf16[192,1024]{1,0:T(8,128)(2,1)S(1)} %get-tuple-element.35.refs_7_), channel_id=1, source_target_pairs={{0,1},{1,2},{2,3},{3,0},{4,5},{5,6},{6,7},{7,4},{8,9},{9,10},{10,1... | collective-permute-start | bytes 1179656 | tf_op jit(solution)/shard_map/ppermute | solution.py:50
  94.8 16.6 %collective-permute-start.13 = (bf16[192,1024]{1,0:T(8,128)(2,1)S(1)}, bf16[192,1024]{1,0:T(8,128)(2,1)S(1)}, u32[]{:S(2)}, u32[]{:S(2)}) collective-permute-start(bf16[192,1024]{1,0:T(8,128)(2,1)S(1)} %get-tuple-element.40), channel_id=1, source_target_pairs={{0,3},{1,0},{2,1},{3,2},{4,7},{5,4},{6,5},{7,6},{8,11},{9,8},{10,9... | collective-permute-start | bytes 1179656 | tf_op jit(solution)/shard_map/ppermute | solution.py:50
  112.1 2.6 %collective-permute-start.14 = (bf16[384,512]{1,0:T(8,128)(2,1)S(1)}, bf16[384,512]{1,0:T(8,128)(2,1)S(1)}, u32[]{:S(2)}, u32[]{:S(2)}) collective-permute-start(bf16[384,512]{1,0:T(8,128)(2,1)S(1)} %sum_columns.2), channel_id=1, source_target_pairs={{0,128},{128,0},{1,129},{129,1},{2,130},{130,2},{3,131},{131,3},{4... | collective-permute-start | bytes 1179656 | tf_op jit(solution)/shard_map/ppermute | solution.py:45

commit v5 on v4

--- a/solution.py
+++ b/solution.py
@@ -43,11 +43,6 @@
 
 def swap_cores(block):
     return lax.ppermute(block, "grp", [(0, 1), (1, 0)])
-
-
-def shift(block, step):
-    count = lax.axis_size("tp")
-    return lax.ppermute(block, "tp", [(i, (i + step) % count) for i in range(count)])
 
 
 def swap(block, mask):
@@ -73,7 +68,10 @@
 
 def table_rows(codes, owned):
     groups = codes.shape[1]
-    number = KNB * lax.broadcasted_iota(jnp.int32, (groups, HD), 0)
+    group = lax.broadcasted_iota(jnp.int32, (groups, HD), 0)
+    count = batch_of(owned) // (2 * KNB)
+    core, group = group // (groups // 2), group % (groups // 2)
+    number = KNB * (group // count * (2 * count) + core * count + group % count)
     column = lax.broadcasted_iota(jnp.int32, (groups, HD), 1)
     which = lax.broadcasted_iota(jnp.int32, (TABLE, HD), 0)
     table = jnp.zeros((TABLE, HD), jnp.float32)
@@ -138,7 +136,7 @@
         held.append(jnp.concatenate(pieces, axis=1).astype(BF16))
     held = jnp.concatenate(held, axis=0)
     lanes = lax.broadcasted_iota(jnp.int32, (owned, total), 1).astype(jnp.float32)
-    per_dot = min(8, owners)
+    per_dot = min(16, owners)
     for begin in range(0, owners, per_dot):
         choose = []
         for s in range(begin, begin + per_dot):
@@ -172,45 +170,35 @@
     )(held, *after)
 
 
-def unpack_kernel(owned, batch, columns, place_ref, arrived_ref, *refs):
-    keep_ref, give_ref = refs[-2:]
+def unpack_kernel(owned, batch, columns, partner, place_ref, arrived_ref, *refs):
+    out_ref = refs[-1]
     parts, message, _ = arrived_ref.shape
     size = message * batch // (owned * columns)
     rows = parts * size // batch
     chooser = order_matrix(batch, parts, size // batch, True)
-    mine = owned // 2
-    side = place_ref[0]
+    count = batch // 2
+    side = place_ref[0] ^ partner
     for first in range(0, owned, batch):
         starts = [(first // batch * columns + t) * size for t in range(columns)]
         block = jnp.concatenate([arrived_ref[:, x : x + size].reshape(parts * size, HD) for x in starts], axis=1)
-        sorted_rows = dot_nn(chooser, block).astype(BF16)
-        for n in range(first, first + batch, KNB):
-            group = sorted_rows[(n - first) * rows : (n - first + KNB) * rows]
-            place = pl.ds(n % mine * rows, KNB * rows)
-
-            @pl.when(side == n // mine)
-            def _():
-                keep_ref[place] = group
-
-            @pl.when(side != n // mine)
-            def _():
-                give_ref[place] = group
-
-
-def unpack_rows(place, arrived, owned, rows, columns, after):
+        chosen = jnp.where(side == 0, chooser[: count * rows], chooser[count * rows :])
+        out_ref[first // 2 * rows : (first // 2 + count) * rows] = dot_nn(chosen, block).astype(BF16)
+
+
+def unpack_rows(place, arrived, owned, rows, columns, partner, after):
     batch = batch_of(owned)
     out_shape = (owned // 2 * rows, columns * HD)
     return pl.pallas_call(
-        lambda *refs: unpack_kernel(owned, batch, columns, *refs),
+        lambda *refs: unpack_kernel(owned, batch, columns, partner, *refs),
         grid_spec=pltpu.PrefetchScalarGridSpec(
             num_scalar_prefetch=1,
             grid=(1,),
             in_specs=[whole(arrived.shape)] + [glance(x) for x in after],
-            out_specs=[whole(out_shape)] * 2,
-        ),
-        out_shape=[jax.ShapeDtypeStruct(out_shape, BF16)] * 2,
-        compiler_params=params(16),
-        cost_estimate=cost(2),
+            out_specs=whole(out_shape),
+        ),
+        out_shape=jax.ShapeDtypeStruct(out_shape, BF16),
+        compiler_params=params(16),
+        cost_estimate=cost(1),
         name="unpack_rows",
     )(place, arrived, *after)
 
@@ -292,13 +280,13 @@
 
 
 def attend_kernel(
-    tp_count, far_step, place_ref, own_ref, other_ref, cot_ref, near_ref, far_ref, own_hbm, other_hbm,
+    tp_count, place_ref, own_ref, other_ref, cot_ref, near_ref, far_ref, own_hbm, other_hbm,
     grad_own_ref, grad_other_ref, low_ref, high_ref, weights, arrived,
 ):
     step = pl.program_id(0)
     side = place_ref[0]
     columns = weights.shape[1]
-    target = (place_ref[1] + far_step) % tp_count
+    target = place_ref[1] ^ (tp_count // 2)
     copies = [
         pltpu.make_async_copy(
             hbm.at[pl.ds(pl.multiple_of((target + core * tp_count) * columns, columns), columns)],
@@ -368,7 +356,7 @@
     neigh_spec = pl.BlockSpec((rows // steps, half), lambda c, s: (c, 0))
     outs = [(tokens, width)] * 2 + [(tokens // 2, 2 * columns)] * 2
     return pl.pallas_call(
-        lambda *refs: attend_kernel(tp_count, tp_count // 2, *refs),
+        lambda *refs: attend_kernel(tp_count, *refs),
         grid_spec=pltpu.PrefetchScalarGridSpec(
             num_scalar_prefetch=1,
             grid=(steps,),
@@ -383,11 +371,11 @@
     )(place, own, other, cotangent, near, far, own_weight, other_weight)
 
 
-def partial_kernel(steps, place_ref, own_ref, other_ref, own_a, own_b, other_a, other_b, *refs):
-    out_refs = refs[-2 * len(steps) :]
+def partial_kernel(masks, place_ref, own_ref, other_ref, own_a, own_b, other_a, other_b, *refs):
+    out_refs = refs[-2 * len(masks) :]
     columns = own_a.shape[0]
     low_rows = own_ref.shape[0] // 2
-    for i in range(len(steps)):
+    for i in range(len(masks)):
 
         @pl.when(pl.program_id(0) == i)
         def _():
@@ -400,32 +388,32 @@
                 out_refs[2 * i + 1][:, place] = term[low_rows:]
 
 
-def partial_terms(place, steps, grad_own, grad_other, own_weight, other_weight, after=()):
+def partial_terms(place, masks, grad_own, grad_other, own_weight, other_weight, after=()):
     tokens, width = grad_own.shape
     tp_count = lax.axis_size("tp")
     columns = own_weight.shape[0] // (2 * tp_count)
 
     def weight_spec(core):
         def index(i, s):
-            step = sum(jnp.where(i == u, step, 0) for u, step in enumerate(steps))
-            return ((s[1] + step) % tp_count + core * tp_count, 0)
+            mask = sum(jnp.where(i == u, mask, 0) for u, mask in enumerate(masks))
+            return ((s[1] ^ mask) + core * tp_count, 0)
 
         return pl.BlockSpec((columns, width), index)
 
     shape = (tokens // 2, 2 * columns)
     return pl.pallas_call(
-        lambda *refs: partial_kernel(steps, *refs),
+        lambda *refs: partial_kernel(masks, *refs),
         grid_spec=pltpu.PrefetchScalarGridSpec(
             num_scalar_prefetch=1,
-            grid=(len(steps),),
+            grid=(len(masks),),
             in_specs=[whole((tokens, width))] * 2
             + [weight_spec(0), weight_spec(1)] * 2
             + [glance(x) for x in after],
-            out_specs=[whole(shape)] * (2 * len(steps)),
-        ),
-        out_shape=[jax.ShapeDtypeStruct(shape, BF16)] * (2 * len(steps)),
-        compiler_params=params(16),
-        cost_estimate=cost(2 * len(steps)),
+            out_specs=[whole(shape)] * (2 * len(masks)),
+        ),
+        out_shape=[jax.ShapeDtypeStruct(shape, BF16)] * (2 * len(masks)),
+        compiler_params=params(16),
+        cost_estimate=cost(2 * len(masks)),
         name="partial_terms",
     )(place, grad_own, grad_other, own_weight, own_weight, other_weight, other_weight, *after)
 
@@ -452,17 +440,17 @@
 def scatter_ring(place, across_low, across_high, *operands):
     if lax.axis_size("tp") == 2:
         own_low, own_high = partial_terms(place, (0,), *operands)
-        return [own_low, shift(across_low, 1)], [own_high, shift(across_high, 1)]
-    rising = shift(across_low, 1)
-    falling = shift(across_high, -1)
-    up_low, up_high, down_low, down_high = partial_terms(place, (1, 3), *operands)
-    up_high = shift(up_high, 1)
-    down_low = shift(down_low, -1)
-    up_low, down_high = add_terms((up_low, down_high), (rising, falling))
-    own_low, own_high = partial_terms(place, (0,), *operands, after=(up_low,))
-    up_low = shift(up_low, 1)
-    down_high = shift(down_high, -1)
-    return [own_low, down_low, up_low], [own_high, up_high, down_high]
+        return [own_low, swap(across_low, 1)], [own_high, swap(across_high, 1)]
+    from1 = swap(across_low, 1)
+    from3 = swap(across_high, 3)
+    low3, high3, low1, high1 = partial_terms(place, (3, 1), *operands)
+    high3 = swap(high3, 3)
+    low1 = swap(low1, 1)
+    low3, high1 = add_terms((low3, high1), (from1, from3))
+    own_low, own_high = partial_terms(place, (0,), *operands, after=(low3,))
+    low3 = swap(low3, 3)
+    high1 = swap(high1, 1)
+    return [own_low, low1, low3], [own_high, high3, high1]
 
 
 def sum_terms(terms):
@@ -540,8 +528,9 @@
 
     sums = project(place, masks, blocks, own_weight, other_weight)
     own, other = project(place, [tp_count // 2], last, own_weight, other_weight, sums)
-    near, give = unpack_rows(place, arrived, owned, rows, columns, [own[:16, :HD]])
+    give = unpack_rows(place, arrived, owned, rows, columns, 1, [own[:16, :HD]])
     far = swap_cores(give)
+    near = unpack_rows(place, arrived, owned, rows, columns, 0, [give])
     grad_own, grad_other, across_low, across_high = attend(
         place, own, other, cotangent, near, far, own_weight, other_weight
     )

time: 117 us -> 116 us (level)
  starting transfers between devices: 38.2 us -> 36.8 us
    ppermute x6 -> x12, waiting for transfers between devices: 17.5 us -> 33.6 us  [swap(): return lax.ppermute(block, 'tp', [(i, i ^ mask) for i in range(count)])]
    ppermute x6 -> x0, waiting for transfers between devices: 14.6 us -> none  [shift(): lax.ppermute(block, 'tp', [(i, (i + step) % count) for i in range(count)])]
    ppermute x6 -> x0, starting transfers between devices: 7.04 us -> none  [shift(): lax.ppermute(block, 'tp', [(i, (i + step) % count) for i in range(count)])]
    ppermute x6 -> x12, starting transfers between devices: 6.02 us -> 11.6 us  [swap(): return lax.ppermute(block, 'tp', [(i, i ^ mask) for i in range(count)])]
    pallas_call x4 -> x5, Pallas kernels: 15.1 us -> 15.1 us  [the longest x1 6.68 us: attend(): pl.pallas_call(lambda *refs: attend_kernel(tp_count, *refs), grid_spec=pl...]
  transfers between devices with their start and end apart: 17 -> 17, of which waited for: 13 -> 14; matrix products, arithmetic and copies ran while one was open for 1% -> 1% of each run, Pallas kernels for 16% -> 17%
where the time goes in v5:
time: 116 us
  waiting for transfers between devices  44.6 us (38%)
  starting transfers between devices  36.8 us (32%)
  Pallas kernels  29.6 us (26%)
  local copies, waits for them, and re-layouts  3.68 us (3%)
    ppermute x12, waiting for transfers between devices, swap(): return lax.ppermute(block, 'tp', [(i, i ^ mask) for i in range(count)])  33.6 us
    ppermute x12, starting transfers between devices, swap(): return lax.ppermute(block, 'tp', [(i, i ^ mask) for i in range(count)])  11.6 us
    all_to_all x1, starting transfers between devices, shards(): lax.all_to_all(packed, 'seq', split_axis=0, concat_axis=0, tiled=True)  9.6 us
    ppermute x3, starting transfers between devices, swap_cores(): return lax.ppermute(block, 'grp', [(0, 1), (1, 0)])  8.9 us
    pallas_call x2, Pallas kernels, project(): pl.pallas_call(project_last_kernel if final else project_kernel, grid_spe...  8.04 us
    all_to_all x1, waiting for transfers between devices, shards(): lax.all_to_all(routed, 'seq', split_axis=0, concat_axis=0, tiled=True)  6.93 us
    pallas_call x1, Pallas kernels, attend(): pl.pallas_call(lambda *refs: attend_kernel(tp_count, *refs), grid_spec=pl...  6.68 us
    all_to_all x1, starting transfers between devices, shards(): lax.all_to_all(routed, 'seq', split_axis=0, concat_axis=0, tiled=True)  6.64 us
  transfers between devices with their start and end apart: 17, of which 14 were waited for; matrix products, arithmetic and copies ran while one was open for 1% of the time, Pallas kernels for 17%

profile of v5, /device:TPU:1, one launch (start us, length us, event | category | flops | bytes accessed | tf_op | source)
XLA Modules:
  0.0 115.6 jit_solution(5704324005725984623)
XLA Ops:
  0.0 3.2 %collective-permute-start.6 = (bf16[4096,512]{1,0:T(8,128)(2,1)}, bf16[4096,512]{1,0:T(8,128)(2,1)}, u32[]{:S(2)}, u32[]{:S(2)}) collective-permute-start(bf16[4096,512]{1,0:T(8,128)(2,1)} %bitcast.21), channel_id=1, source_target_pairs={{0,128},{128,0},{1,129},{129,1},{2,130},{130,2},{3,131},{131,3},{4... | collective-permute-start | bytes 12582920 | tf_op jit(solution)/shard_map/ppermute | solution.py:45
  4.0 1.4 %copy-done.3 = bf16[24,64,512]{2,1,0:T(8,128)(2,1)S(1)} copy-done((bf16[24,64,512]{2,1,0:T(8,128)(2,1)S(1)}, bf16[24,64,512]{2,1,0:T(8,128)(2,1)}, u32[]{:S(2)}) %copy-start.3) | copy-done | bytes 1572888
  5.4 2.0 %pack_rows.1 = bf16[32,104,128]{2,1,0:T(8,128)(2,1)} custom-call(s32[2]{0:T(128)S(1)} %pad_add_fusion.place_ref.refs_0_, s32[2,12]{1,0:T(2,128)S(1)} %fusion.refs_1_, bf16[24,64,512]{2,1,0:T(8,128)(2,1)S(1)} %copy-done.3), custom_call_target="tpu_custom_call" | custom-call | flops 3000000000 | bytes 3000000 | tf_op jit(solution)/shard_map/pack_rows/pallas_call | solution.py:107
  7.5 9.6 %all-to-all-start = ((bf16[32,104,128]{2,1,0:T(8,128)(2,1)}), bf16[32,104,128]{2,1,0:T(8,128)(2,1)S(1)}, u32[]{:S(2)}, u32[]{:S(2)}) async-start(bf16[32,104,128]{2,1,0:T(8,128)(2,1)} %pack_rows.1), calls=%async_computation | async-start | bytes 1703936 | tf_op jit(solution)/shard_map/all_to_all | solution.py:525
  17.2 1.3 %collective-permute-start.2 = (bf16[192,1024]{1,0:T(8,128)(2,1)S(1)}, bf16[192,1024]{1,0:T(8,128)(2,1)S(1)}, u32[]{:S(2)}, u32[]{:S(2)}) collective-permute-start(bf16[192,1024]{1,0:T(8,128)(2,1)S(1)} %get-tuple-element.37.refs_1_), channel_id=1, source_target_pairs={{0,1},{1,0},{2,3},{3,2},{4,5},{5,4},{6,7},{7,6},{8,9},{9,8},{10,11... | collective-permute-start | bytes 1179656 | tf_op jit(solution)/shard_map/ppermute | solution.py:50
  18.5 1.8 %collective-permute-start = (bf16[192,1024]{1,0:T(8,128)(2,1)S(1)}, bf16[192,1024]{1,0:T(8,128)(2,1)S(1)}, u32[]{:S(2)}, u32[]{:S(2)}) collective-permute-start(bf16[192,1024]{1,0:T(8,128)(2,1)S(1)} %get-tuple-element.38.refs_0_), channel_id=1, source_target_pairs={{0,3},{1,2},{2,1},{3,0},{4,7},{5,6},{6,5},{7,4},{8,11},{9,10},{10,... | collective-permute-start | bytes 1179656 | tf_op jit(solution)/shard_map/ppermute | solution.py:50
  21.2 6.5 %collective-permute-done.2.refs_3_ = bf16[192,1024]{1,0:T(8,128)(2,1)S(1)} collective-permute-done((bf16[192,1024]{1,0:T(8,128)(2,1)S(1)}, bf16[192,1024]{1,0:T(8,128)(2,1)S(1)}, u32[]{:S(2)}, u32[]{:S(2)}) %collective-permute-start.2) | collective-permute-done | bytes 393248 | tf_op jit(solution)/shard_map/ppermute | solution.py:50
  27.7 2.1 %collective-permute-done.refs_4_ = bf16[192,1024]{1,0:T(8,128)(2,1)S(1)} collective-permute-done((bf16[192,1024]{1,0:T(8,128)(2,1)S(1)}, bf16[192,1024]{1,0:T(8,128)(2,1)S(1)}, u32[]{:S(2)}, u32[]{:S(2)}) %collective-permute-start) | collective-permute-done | bytes 393248 | tf_op jit(solution)/shard_map/ppermute | solution.py:50
  29.8 6.3 %collective-permute-done.4.refs_2_ = bf16[192,1024]{1,0:T(8,128)(2,1)S(1)} collective-permute-done((bf16[192,1024]{1,0:T(8,128)(2,1)S(1)}, bf16[192,1024]{1,0:T(8,128)(2,1)S(1)}, u32[]{:S(2)}, u32[]{:S(2)}) %collective-permute-start.4) | collective-permute-done | bytes 393248 | tf_op jit(solution)/shard_map/ppermute | solution.py:50
  36.1 2.1 %collective-permute-done.5.refs_5_ = bf16[192,1024]{1,0:T(8,128)(2,1)S(1)} collective-permute-done((bf16[192,1024]{1,0:T(8,128)(2,1)S(1)}, bf16[192,1024]{1,0:T(8,128)(2,1)S(1)}, u32[]{:S(2)}, u32[]{:S(2)}) %collective-permute-start.5) | collective-permute-done | bytes 393248 | tf_op jit(solution)/shard_map/ppermute | solution.py:50
  38.2 2.3 %all-to-all-done.refs_0_ = bf16[32,104,128]{2,1,0:T(8,128)(2,1)S(1)} async-done(((bf16[32,104,128]{2,1,0:T(8,128)(2,1)}), bf16[32,104,128]{2,1,0:T(8,128)(2,1)S(1)}, u32[]{:S(2)}, u32[]{:S(2)}) %all-to-all-start) | async-done | bytes 852000 | tf_op jit(solution)/shard_map/all_to_all | solution.py:525
  40.5 1.9 %route_rows.1 = bf16[32,96,128]{2,1,0:T(8,128)(2,1)} custom-call(bf16[32,104,128]{2,1,0:T(8,128)(2,1)S(1)} %all-to-all-done.refs_0_, bf16[16,128]{1,0:T(8,128)(2,1)S(1)} %slice.20.refs_1_, bf16[16,128]{1,0:T(8,128)(2,1)S(1)} %slice.21.refs_2_, bf16[16,128]{1,0:T(8,128)(2,1)S(1)} %slice.22.refs_3_, bf16[16,128]{1,0:T(8,128)(2,1)S(1)} %slice.23.refs_4_), custom_call_target="tpu_custom_call" | custom-call | flops 2000000000 | bytes 2000000 | tf_op jit(solution)/shard_map/route_rows/pallas_call | solution.py:161
  42.3 6.6 %all-to-all-start.1 = ((bf16[32,96,128]{2,1,0:T(8,128)(2,1)}), bf16[32,96,128]{2,1,0:T(8,128)(2,1)S(1)}, u32[]{:S(2)}, u32[]{:S(2)}) async-start(bf16[32,96,128]{2,1,0:T(8,128)(2,1)} %route_rows.1), calls=%async_computation.1 | async-start | bytes 1572864 | tf_op jit(solution)/shard_map/all_to_all | solution.py:527
  49.1 1.9 %collective-permute-start.3 = (bf16[192,1024]{1,0:T(8,128)(2,1)S(1)}, bf16[192,1024]{1,0:T(8,128)(2,1)S(1)}, u32[]{:S(2)}, u32[]{:S(2)}) collective-permute-start(bf16[192,1024]{1,0:T(8,128)(2,1)S(1)} %collective-permute-done.2.refs_3_), channel_id=1, source_target_pairs={{0,3},{1,2},{2,1},{3,0},{4,7},{5,6},{6,5},{7,4},{8,11},{9,10},{10,... | collective-permute-start | bytes 1179656 | tf_op jit(solution)/shard_map/ppermute | solution.py:50
  51.0 2.2 %copy-done = bf16[1,4096,512]{2,1,0:T(8,128)(2,1)S(1)} copy-done((bf16[1,4096,512]{2,1,0:T(8,128)(2,1)S(1)}, bf16[1,4096,512]{2,1,0:T(8,128)(2,1)}, u32[]{:S(2)}) %copy-start) | copy-done | bytes 4194328
  53.2 5.3 %project.2 = (f32[384,512]{1,0:T(8,128)S(1)}, f32[384,512]{1,0:T(8,128)S(1)}) custom-call(s32[2]{0:T(128)S(1)} %pad_add_fusion.place_ref.refs_0_, bf16[192,1024]{1,0:T(8,128)(2,1)S(1)} %get-tuple-element.38.refs_0_, bf16[192,1024]{1,0:T(8,128)(2,1)S(1)} %get-tuple-element.37.refs_1_, bf16[192,1024]{1,0:T(8,128)(2,1)S(1)} %collective-permute-done.4.refs_2_, ...), custom_call_target="tpu_custom_call" | custom-call | flops 7500000256 | bytes 7500000 | tf_op jit(solution)/shard_map/project/pallas_call | solution.py:239
  59.0 2.8 %project.3 = (bf16[384,512]{1,0:T(8,128)(2,1)S(1)}, bf16[384,512]{1,0:T(8,128)(2,1)S(1)}) custom-call(s32[2]{0:T(128)S(1)} %pad_add_fusion.place_ref.refs_0_, bf16[192,1024]{1,0:T(8,128)(2,1)S(1)} %collective-permute-done.1.refs_0_, bf16[192,1024]{1,0:T(8,128)(2,1)S(1)} %collective-permute-done.3.refs_1_, f32[384,512]{1,0:T(8,128)S(1)} %get-tuple-element.21.refs_2_, ...), custom_call_target="tpu_custom_call" | custom-call | flops 2500000000 | bytes 2500000 | tf_op jit(solution)/shard_map/project/pallas_call | solution.py:239
  61.8 6.9 %all-to-all-done.1.refs_1_ = bf16[32,96,128]{2,1,0:T(8,128)(2,1)S(1)} async-done(((bf16[32,96,128]{2,1,0:T(8,128)(2,1)}), bf16[32,96,128]{2,1,0:T(8,128)(2,1)S(1)}, u32[]{:S(2)}, u32[]{:S(2)}) %all-to-all-start.1) | async-done | bytes 786464 | tf_op jit(solution)/shard_map/all_to_all | solution.py:527
  69.6 4.4 %collective-permute-start.7 = (bf16[768,256]{1,0:T(8,128)(2,1)S(1)}, bf16[768,256]{1,0:T(8,128)(2,1)S(1)}, u32[]{:S(2)}, u32[]{:S(2)}) collective-permute-start(bf16[768,256]{1,0:T(8,128)(2,1)S(1)} %unpack_rows.2.refs_2_), channel_id=1, source_target_pairs={{0,128},{128,0},{1,129},{129,1},{2,130},{130,2},{3,131},{131,3},{4... | collective-permute-start | bytes 1179656 | tf_op jit(solution)/shard_map/ppermute | solution.py:45
  75.4 6.7 %attend.1 = (bf16[384,512]{1,0:T(8,128)(2,1)S(1)}, bf16[384,512]{1,0:T(8,128)(2,1)S(1)}, bf16[192,1024]{1,0:T(8,128)(2,1)S(1)}, bf16[192,1024]{1,0:T(8,128)(2,1)S(1)}) custom-call(s32[2]{0:T(128)S(1)} %pad_add_fusion.place_ref.refs_0_, bf16[384,512]{1,0:T(8,128)(2,1)S(1)} %get-tuple-element.23.refs_1_, bf16[384,512]{1,0:T(8,128)(2,1)S(1)} %get-tuple-element.24.refs_2_, ...), custom_call_target="tpu_custom_call" | custom-call | flops 8000000000 | bytes 8000000 | tf_op jit(solution)/shard_map/attend/pallas_call | solution.py:358
  82.2 1.9 %collective-permute-start.9 = (bf16[192,1024]{1,0:T(8,128)(2,1)S(1)}, bf16[192,1024]{1,0:T(8,128)(2,1)S(1)}, u32[]{:S(2)}, u32[]{:S(2)}) collective-permute-start(bf16[192,1024]{1,0:T(8,128)(2,1)S(1)} %get-tuple-element.30), channel_id=1, source_target_pairs={{0,3},{1,2},{2,1},{3,0},{4,7},{5,6},{6,5},{7,4},{8,11},{9,10},{10,... | collective-permute-start | bytes 1179656 | tf_op jit(solution)/shard_map/ppermute | solution.py:50
  84.1 3.9 %partial_terms.2 = (bf16[192,1024]{1,0:T(8,128)(2,1)S(1)}, bf16[192,1024]{1,0:T(8,128)(2,1)S(1)}, bf16[192,1024]{1,0:T(8,128)(2,1)S(1)}, bf16[192,1024]{1,0:T(8,128)(2,1)S(1)}) custom-call(s32[2]{0:T(128)S(1)} %pad_add_fusion.place_ref.refs_0_, bf16[384,512]{1,0:T(8,128)(2,1)S(1)} %get-tuple-element.25.refs_1_, ...), custom_call_target="tpu_custom_call" | custom-call | flops 4000000000 | bytes 4000000 | tf_op jit(solution)/shard_map/partial_terms/pallas_call | solution.py:404
  89.6 2.8 %collective-permute-done.8.refs_2_ = bf16[192,1024]{1,0:T(8,128)(2,1)S(1)} collective-permute-done((bf16[192,1024]{1,0:T(8,128)(2,1)S(1)}, bf16[192,1024]{1,0:T(8,128)(2,1)S(1)}, u32[]{:S(2)}, u32[]{:S(2)}) %collective-permute-start.8) | collective-permute-done | bytes 393248 | tf_op jit(solution)/shard_map/ppermute | solution.py:50
  92.5 1.3 %collective-permute-done.9.refs_3_ = bf16[192,1024]{1,0:T(8,128)(2,1)S(1)} collective-permute-done((bf16[192,1024]{1,0:T(8,128)(2,1)S(1)}, bf16[192,1024]{1,0:T(8,128)(2,1)S(1)}, u32[]{:S(2)}, u32[]{:S(2)}) %collective-permute-start.9) | collective-permute-done | bytes 393248 | tf_op jit(solution)/shard_map/ppermute | solution.py:50
  94.0 1.9 %collective-permute-start.11 = (bf16[192,1024]{1,0:T(8,128)(2,1)S(1)}, bf16[192,1024]{1,0:T(8,128)(2,1)S(1)}, u32[]{:S(2)}, u32[]{:S(2)}) collective-permute-start(bf16[192,1024]{1,0:T(8,128)(2,1)S(1)} %get-tuple-element.31.refs_7_), channel_id=1, source_target_pairs={{0,3},{1,2},{2,1},{3,0},{4,7},{5,6},{6,5},{7,4},{8,11},{9,10},{10,... | collective-permute-start | bytes 1179656 | tf_op jit(solution)/shard_map/ppermute | solution.py:50
  95.9 2.8 %partial_terms.3 = (bf16[192,1024]{1,0:T(8,128)(2,1)S(1)}, bf16[192,1024]{1,0:T(8,128)(2,1)S(1)}) custom-call(s32[2]{0:T(128)S(1)} %pad_add_fusion.place_ref.refs_0_, bf16[384,512]{1,0:T(8,128)(2,1)S(1)} %get-tuple-element.25.refs_1_, bf16[384,512]{1,0:T(8,128)(2,1)S(1)} %get-tuple-element.26.refs_2_, bf16[4096,512]{1,0:T(8,128)(2,1)S(1)} %bitcast.27, ...), custom_call_target="tpu_custom_call" | custom-call | flops 2000000000 | bytes 2000000 | tf_op jit(solution)/shard_map/partial_terms/pallas_call | solution.py:404
  98.7 2.2 %collective-permute-done.10.refs_1_ = bf16[192,1024]{1,0:T(8,128)(2,1)S(1)} collective-permute-done((bf16[192,1024]{1,0:T(8,128)(2,1)S(1)}, bf16[192,1024]{1,0:T(8,128)(2,1)S(1)}, u32[]{:S(2)}, u32[]{:S(2)}) %collective-permute-start.10) | collective-permute-done | bytes 393248 | tf_op jit(solution)/shard_map/ppermute | solution.py:50
  100.9 1.3 %collective-permute-done.12.refs_4_ = bf16[192,1024]{1,0:T(8,128)(2,1)S(1)} collective-permute-done((bf16[192,1024]{1,0:T(8,128)(2,1)S(1)}, bf16[192,1024]{1,0:T(8,128)(2,1)S(1)}, u32[]{:S(2)}, u32[]{:S(2)}) %collective-permute-start.12) | collective-permute-done | bytes 393248 | tf_op jit(solution)/shard_map/ppermute | solution.py:50
  102.2 8.4 %collective-permute-done.11.refs_2_ = bf16[192,1024]{1,0:T(8,128)(2,1)S(1)} collective-permute-done((bf16[192,1024]{1,0:T(8,128)(2,1)S(1)}, bf16[192,1024]{1,0:T(8,128)(2,1)S(1)}, u32[]{:S(2)}, u32[]{:S(2)}) %collective-permute-start.11) | collective-permute-done | bytes 393248 | tf_op jit(solution)/shard_map/ppermute | solution.py:50
  111.3 1.3 %collective-permute-start.14 = (bf16[384,512]{1,0:T(8,128)(2,1)S(1)}, bf16[384,512]{1,0:T(8,128)(2,1)S(1)}, u32[]{:S(2)}, u32[]{:S(2)}) collective-permute-start(bf16[384,512]{1,0:T(8,128)(2,1)S(1)} %sum_columns.2), channel_id=1, source_target_pairs={{0,128},{128,0},{1,129},{129,1},{2,130},{130,2},{3,131},{131,3},{4... | collective-permute-start | bytes 1179656 | tf_op jit(solution)/shard_map/ppermute | solution.py:45
  112.6 1.3 %collective-permute-done.14.refs_6_ = bf16[384,512]{1,0:T(8,128)(2,1)S(1)} collective-permute-done((bf16[384,512]{1,0:T(8,128)(2,1)S(1)}, bf16[384,512]{1,0:T(8,128)(2,1)S(1)}, u32[]{:S(2)}, u32[]{:S(2)}) %collective-permute-start.14) | collective-permute-done | bytes 393248 | tf_op jit(solution)/shard_map/ppermute | solution.py:45
  114.0 1.6 %sum_columns.3 = bf16[768,512]{1,0:T(8,128)(2,1)} custom-call(s32[2]{0:T(128)S(1)} %pad_add_fusion.place_ref.refs_0_, bf16[192,1024]{1,0:T(8,128)(2,1)S(1)} %get-tuple-element.32.refs_0_, bf16[192,1024]{1,0:T(8,128)(2,1)S(1)} %collective-permute-done.10.refs_1_, bf16[192,1024]{1,0:T(8,128)(2,1)S(1)} %collective-permute-done.11.refs_2_, ...), custom_call_target="tpu_custom_call" | custom-call | flops 1000000000 | bytes 1000000 | tf_op jit(solution)/shard_map/sum_columns/pallas_call | solution.py:484
  (34 shorter events, 7.4 us)
Async XLA Ops:
  0.0 51.0 %collective-permute-start.6 = (bf16[4096,512]{1,0:T(8,128)(2,1)}, bf16[4096,512]{1,0:T(8,128)(2,1)}, u32[]{:S(2)}, u32[]{:S(2)}) collective-permute-start(bf16[4096,512]{1,0:T(8,128)(2,1)} %bitcast.21), channel_id=1, source_target_pairs={{0,128},{128,0},{1,129},{129,1},{2,130},{130,2},{3,131},{131,3},{4... | collective-permute-start | bytes 12582920 | tf_op jit(solution)/shard_map/ppermute | solution.py:45
  4.0 1.4 %copy-start.3 = (bf16[24,64,512]{2,1,0:T(8,128)(2,1)S(1)}, bf16[24,64,512]{2,1,0:T(8,128)(2,1)}, u32[]{:S(2)}) copy-start(bf16[24,64,512]{2,1,0:T(8,128)(2,1)} %refs_2_.1) | copy-start | bytes 4718596
  7.5 9.6 %copy-start.5 = (bf16[768,1024]{1,0:T(8,128)(2,1)S(1)}, bf16[768,1024]{1,0:T(8,128)(2,1)}, u32[]{:S(2)}) copy-start(bf16[768,1024]{1,0:T(8,128)(2,1)} %param.6) | copy-start | bytes 4718596
  7.5 33.0 %all-to-all-start = ((bf16[32,104,128]{2,1,0:T(8,128)(2,1)}), bf16[32,104,128]{2,1,0:T(8,128)(2,1)S(1)}, u32[]{:S(2)}, u32[]{:S(2)}) async-start(bf16[32,104,128]{2,1,0:T(8,128)(2,1)} %pack_rows.1), calls=%async_computation | async-start | bytes 1703936 | tf_op jit(solution)/shard_map/all_to_all | solution.py:525
  17.2 10.5 %collective-permute-start.2 = (bf16[192,1024]{1,0:T(8,128)(2,1)S(1)}, bf16[192,1024]{1,0:T(8,128)(2,1)S(1)}, u32[]{:S(2)}, u32[]{:S(2)}) collective-permute-start(bf16[192,1024]{1,0:T(8,128)(2,1)S(1)} %get-tuple-element.37.refs_1_), channel_id=1, source_target_pairs={{0,1},{1,0},{2,3},{3,2},{4,5},{5,4},{6,7},{7,6},{8,9},{9,8},{10,11... | collective-permute-start | bytes 1179656 | tf_op jit(solution)/shard_map/ppermute | solution.py:50
  18.5 11.3 %collective-permute-start = (bf16[192,1024]{1,0:T(8,128)(2,1)S(1)}, bf16[192,1024]{1,0:T(8,128)(2,1)S(1)}, u32[]{:S(2)}, u32[]{:S(2)}) collective-permute-start(bf16[192,1024]{1,0:T(8,128)(2,1)S(1)} %get-tuple-element.38.refs_0_), channel_id=1, source_target_pairs={{0,3},{1,2},{2,1},{3,0},{4,7},{5,6},{6,5},{7,4},{8,11},{9,10},{10,... | collective-permute-start | bytes 1179656 | tf_op jit(solution)/shard_map/ppermute | solution.py:50
  20.3 15.8 %collective-permute-start.4 = (bf16[192,1024]{1,0:T(8,128)(2,1)S(1)}, bf16[192,1024]{1,0:T(8,128)(2,1)S(1)}, u32[]{:S(2)}, u32[]{:S(2)}) collective-permute-start(bf16[192,1024]{1,0:T(8,128)(2,1)S(1)} %get-tuple-element.38.refs_0_), channel_id=1, source_target_pairs={{0,1},{1,0},{2,3},{3,2},{4,5},{5,4},{6,7},{7,6},{8,9},{9,8},{10,11... | collective-permute-start | bytes 1179656 | tf_op jit(solution)/shard_map/ppermute | solution.py:50
  20.6 17.6 %collective-permute-start.5 = (bf16[192,1024]{1,0:T(8,128)(2,1)S(1)}, bf16[192,1024]{1,0:T(8,128)(2,1)S(1)}, u32[]{:S(2)}, u32[]{:S(2)}) collective-permute-start(bf16[192,1024]{1,0:T(8,128)(2,1)S(1)} %get-tuple-element.37.refs_1_), channel_id=1, source_target_pairs={{0,3},{1,2},{2,1},{3,0},{4,7},{5,6},{6,5},{7,4},{8,11},{9,10},{10,... | collective-permute-start | bytes 1179656 | tf_op jit(solution)/shard_map/ppermute | solution.py:50
  42.3 26.4 %all-to-all-start.1 = ((bf16[32,96,128]{2,1,0:T(8,128)(2,1)}), bf16[32,96,128]{2,1,0:T(8,128)(2,1)S(1)}, u32[]{:S(2)}, u32[]{:S(2)}) async-start(bf16[32,96,128]{2,1,0:T(8,128)(2,1)} %route_rows.1), calls=%async_computation.1 | async-start | bytes 1572864 | tf_op jit(solution)/shard_map/all_to_all | solution.py:527
  49.0 9.5 %collective-permute-start.1 = (bf16[192,1024]{1,0:T(8,128)(2,1)S(1)}, bf16[192,1024]{1,0:T(8,128)(2,1)S(1)}, u32[]{:S(2)}, u32[]{:S(2)}) collective-permute-start(bf16[192,1024]{1,0:T(8,128)(2,1)S(1)} %collective-permute-done.refs_4_), channel_id=1, source_target_pairs={{0,1},{1,0},{2,3},{3,2},{4,5},{5,4},{6,7},{7,6},{8,9},{9,8},{10,11... | collective-permute-start | bytes 1179656 | tf_op jit(solution)/shard_map/ppermute | solution.py:50
  49.1 9.9 %collective-permute-start.3 = (bf16[192,1024]{1,0:T(8,128)(2,1)S(1)}, bf16[192,1024]{1,0:T(8,128)(2,1)S(1)}, u32[]{:S(2)}, u32[]{:S(2)}) collective-permute-start(bf16[192,1024]{1,0:T(8,128)(2,1)S(1)} %collective-permute-done.2.refs_3_), channel_id=1, source_target_pairs={{0,3},{1,2},{2,1},{3,0},{4,7},{5,6},{6,5},{7,4},{8,11},{9,10},{10,... | collective-permute-start | bytes 1179656 | tf_op jit(solution)/shard_map/ppermute | solution.py:50
  51.0 2.2 %copy-start = (bf16[1,4096,512]{2,1,0:T(8,128)(2,1)S(1)}, bf16[1,4096,512]{2,1,0:T(8,128)(2,1)}, u32[]{:S(2)}) copy-start(bf16[1,4096,512]{2,1,0:T(8,128)(2,1)} %param.7) | copy-start | bytes 12582916
  53.2 5.8 %copy-start.1 = (bf16[1,4096,512]{2,1,0:T(8,128)(2,1)S(1)}, bf16[1,4096,512]{2,1,0:T(8,128)(2,1)}, u32[]{:S(2)}) copy-start(bf16[1,4096,512]{2,1,0:T(8,128)(2,1)} %param.7) | copy-start | bytes 12582916
  68.7 6.7 %copy-start.2 = (bf16[1,4096,512]{2,1,0:T(8,128)(2,1)S(1)}, bf16[1,4096,512]{2,1,0:T(8,128)(2,1)}, u32[]{:S(2)}) copy-start(bf16[1,4096,512]{2,1,0:T(8,128)(2,1)} %param.7) | copy-start | bytes 12582916
  69.6 5.7 %copy-start.4 = (bf16[768,512]{1,0:T(8,128)(2,1)S(1)}, bf16[768,512]{1,0:T(8,128)(2,1)}, u32[]{:S(2)}) copy-start(bf16[768,512]{1,0:T(8,128)(2,1)} %refs_3_.1) | copy-start | bytes 2359300
  69.6 5.7 %collective-permute-start.7 = (bf16[768,256]{1,0:T(8,128)(2,1)S(1)}, bf16[768,256]{1,0:T(8,128)(2,1)S(1)}, u32[]{:S(2)}, u32[]{:S(2)}) collective-permute-start(bf16[768,256]{1,0:T(8,128)(2,1)S(1)} %unpack_rows.2.refs_2_), channel_id=1, source_target_pairs={{0,128},{128,0},{1,129},{129,1},{2,130},{130,2},{3,131},{131,3},{4... | collective-permute-start | bytes 1179656 | tf_op jit(solution)/shard_map/ppermute | solution.py:45
  82.1 10.4 %collective-permute-start.8 = (bf16[192,1024]{1,0:T(8,128)(2,1)S(1)}, bf16[192,1024]{1,0:T(8,128)(2,1)S(1)}, u32[]{:S(2)}, u32[]{:S(2)}) collective-permute-start(bf16[192,1024]{1,0:T(8,128)(2,1)S(1)} %get-tuple-element.29), channel_id=1, source_target_pairs={{0,1},{1,0},{2,3},{3,2},{4,5},{5,4},{6,7},{7,6},{8,9},{9,8},{10,11... | collective-permute-start | bytes 1179656 | tf_op jit(solution)/shard_map/ppermute | solution.py:50
  82.2 11.6 %collective-permute-start.9 = (bf16[192,1024]{1,0:T(8,128)(2,1)S(1)}, bf16[192,1024]{1,0:T(8,128)(2,1)S(1)}, u32[]{:S(2)}, u32[]{:S(2)}) collective-permute-start(bf16[192,1024]{1,0:T(8,128)(2,1)S(1)} %get-tuple-element.30), channel_id=1, source_target_pairs={{0,3},{1,2},{2,1},{3,0},{4,7},{5,6},{6,5},{7,4},{8,11},{9,10},{10,... | collective-permute-start | bytes 1179656 | tf_op jit(solution)/shard_map/ppermute | solution.py:50
  87.9 13.0 %collective-permute-start.10 = (bf16[192,1024]{1,0:T(8,128)(2,1)S(1)}, bf16[192,1024]{1,0:T(8,128)(2,1)S(1)}, u32[]{:S(2)}, u32[]{:S(2)}) collective-permute-start(bf16[192,1024]{1,0:T(8,128)(2,1)S(1)} %get-tuple-element.33), channel_id=1, source_target_pairs={{0,1},{1,0},{2,3},{3,2},{4,5},{5,4},{6,7},{7,6},{8,9},{9,8},{10,11... | collective-permute-start | bytes 1179656 | tf_op jit(solution)/shard_map/ppermute | solution.py:50
  88.8 13.4 %collective-permute-start.12 = (bf16[192,1024]{1,0:T(8,128)(2,1)S(1)}, bf16[192,1024]{1,0:T(8,128)(2,1)S(1)}, u32[]{:S(2)}, u32[]{:S(2)}) collective-permute-start(bf16[192,1024]{1,0:T(8,128)(2,1)S(1)} %get-tuple-element.35), channel_id=1, source_target_pairs={{0,3},{1,2},{2,1},{3,0},{4,7},{5,6},{6,5},{7,4},{8,11},{9,10},{10,... | collective-permute-start | bytes 1179656 | tf_op jit(solution)/shard_map/ppermute | solution.py:50
  94.0 16.7 %collective-permute-start.11 = (bf16[192,1024]{1,0:T(8,128)(2,1)S(1)}, bf16[192,1024]{1,0:T(8,128)(2,1)S(1)}, u32[]{:S(2)}, u32[]{:S(2)}) collective-permute-start(bf16[192,1024]{1,0:T(8,128)(2,1)S(1)} %get-tuple-element.31.refs_7_), channel_id=1, source_target_pairs={{0,3},{1,2},{2,1},{3,0},{4,7},{5,6},{6,5},{7,4},{8,11},{9,10},{10,... | collective-permute-start | bytes 1179656 | tf_op jit(solution)/shard_map/ppermute | solution.py:50
  95.9 14.7 %collective-permute-start.13 = (bf16[192,1024]{1,0:T(8,128)(2,1)S(1)}, bf16[192,1024]{1,0:T(8,128)(2,1)S(1)}, u32[]{:S(2)}, u32[]{:S(2)}) collective-permute-start(bf16[192,1024]{1,0:T(8,128)(2,1)S(1)} %get-tuple-element.36), channel_id=1, source_target_pairs={{0,1},{1,0},{2,3},{3,2},{4,5},{5,4},{6,7},{7,6},{8,9},{9,8},{10,11... | collective-permute-start | bytes 1179656 | tf_op jit(solution)/shard_map/ppermute | solution.py:50
  111.3 2.6 %collective-permute-start.14 = (bf16[384,512]{1,0:T(8,128)(2,1)S(1)}, bf16[384,512]{1,0:T(8,128)(2,1)S(1)}, u32[]{:S(2)}, u32[]{:S(2)}) collective-permute-start(bf16[384,512]{1,0:T(8,128)(2,1)S(1)} %sum_columns.2), channel_id=1, source_target_pairs={{0,128},{128,0},{1,129},{129,1},{2,130},{130,2},{3,131},{131,3},{4... | collective-permute-start | bytes 1179656 | tf_op jit(solution)/shard_map/ppermute | solution.py:45

commit v6 on v5

--- a/solution.py
+++ b/solution.py
@@ -457,43 +457,51 @@
     return sum(term[...].astype(jnp.float32) for term in terms).astype(BF16)
 
 
-def give_kernel(place_ref, *refs):
+def columns_kernel(place_ref, *refs):
     terms, out_ref = refs[:-1], refs[-1]
     count, rows = len(terms) // 2, terms[0].shape[0]
     out_ref[:rows] = sum_terms(terms[:count])
     out_ref[rows:] = sum_terms(terms[count:])
 
 
-def keep_kernel(place_ref, *refs):
-    terms, received_ref, out_ref = refs[:-2], refs[-2], refs[-1]
-    count, rows = len(terms) // 2, terms[0].shape[0]
-    side = place_ref[0]
-    mine = pl.multiple_of(side * 2 * rows, 2 * rows)
-    other = pl.multiple_of((1 - side) * 2 * rows, 2 * rows)
-    out_ref[pl.ds(mine, rows)] = sum_terms(terms[:count])
-    out_ref[pl.ds(mine + rows, rows)] = sum_terms(terms[count:])
-    out_ref[pl.ds(other, 2 * rows)] = received_ref[...]
-
-
-def sum_columns(place, lows, highs, received=None):
+def sum_columns(place, partner, lows, highs):
     rows, columns = lows[0].shape[0], lows[0].shape[1] // 2
-    give = received is None
-    extra = [] if give else [received]
-    spec = pl.BlockSpec((rows, columns), lambda i, s: (0, 1 - s[0] if give else s[0]))
-    out_shape = ((2 if give else 4) * rows, columns)
-    return pl.pallas_call(
-        give_kernel if give else keep_kernel,
+    blocks = 1 if partner else 2
+    return pl.pallas_call(
+        columns_kernel,
         grid_spec=pltpu.PrefetchScalarGridSpec(
             num_scalar_prefetch=1,
             grid=(1,),
-            in_specs=[spec] * len(lows + highs) + [whole(x.shape) for x in extra],
-            out_specs=whole(out_shape),
-        ),
-        out_shape=jax.ShapeDtypeStruct(out_shape, BF16),
+            in_specs=[pl.BlockSpec((rows, columns), lambda i, s: (0, s[0] ^ partner))] * len(lows + highs),
+            out_specs=pl.BlockSpec((2 * rows, columns), lambda i, s: (0 if partner else s[0], 0)),
+        ),
+        out_shape=jax.ShapeDtypeStruct((2 * rows * blocks, columns), BF16),
         compiler_params=params(16),
         cost_estimate=cost(1),
         name="sum_columns",
-    )(place, *lows, *highs, *extra)
+    )(place, *lows, *highs)
+
+
+def place_kernel(place_ref, received_ref, kept_ref, out_ref):
+    out_ref[...] = received_ref[...]
+
+
+def place_rows(place, received, kept):
+    rows, columns = received.shape
+    return pl.pallas_call(
+        place_kernel,
+        grid_spec=pltpu.PrefetchScalarGridSpec(
+            num_scalar_prefetch=1,
+            grid=(1,),
+            in_specs=[whole(received.shape), pl.BlockSpec(memory_space=pl.ANY)],
+            out_specs=pl.BlockSpec((rows, columns), lambda i, s: (1 - s[0], 0)),
+        ),
+        out_shape=jax.ShapeDtypeStruct(kept.shape, BF16),
+        input_output_aliases={2: 0},
+        compiler_params=params(16),
+        cost_estimate=cost(1),
+        name="place_rows",
+    )(place, received, kept)
 
 
 def shards(states, projections, neighbours, owner, slot, cotangent):
@@ -536,8 +544,8 @@
     )
     lows, highs = scatter_ring(place, across_low, across_high, grad_own, grad_other, own_weight, other_weight)
 
-    received = swap_cores(sum_columns(place, lows, highs))
-    return sum_columns(place, lows, highs, received)
+    received = swap_cores(sum_columns(place, 1, lows, highs))
+    return place_rows(place, received, sum_columns(place, 0, lows, highs))
 
 
 def solution(mesh):

time: 116 us -> 116 us (level)
  waiting for transfers between devices: 44.6 us -> 43.2 us
    ppermute x3, waiting for transfers between devices: 1.77 us -> 0.42 us  [swap_cores(): return lax.ppermute(block, 'grp', [(0, 1), (1, 0)])]
    pallas_call x2 -> x3, Pallas kernels: 2.31 us -> 3.43 us  [the longest x2 2.12 us: sum_columns(): pl.pallas_call(columns_kernel, grid_spec=pltpu.PrefetchScalarGridSpec(num...]
  transfers between devices with their start and end apart: 17 -> 17, of which waited for: 14 -> 13; matrix products, arithmetic and copies ran while one was open for 1% -> 1% of each run, Pallas kernels for 17% -> 18%
where the time goes in v6:
time: 116 us; the launch traced here: 115 us
  waiting for transfers between devices  43.2 us (37%)
  starting transfers between devices  36.8 us (32%)
  Pallas kernels  30.7 us (26%)
  local copies, waits for them, and re-layouts  3.68 us (3%)
    ppermute x12, waiting for transfers between devices, swap(): return lax.ppermute(block, 'tp', [(i, i ^ mask) for i in range(count)])  33.6 us
    ppermute x12, starting transfers between devices, swap(): return lax.ppermute(block, 'tp', [(i, i ^ mask) for i in range(count)])  11.6 us
    all_to_all x1, starting transfers between devices, shards(): lax.all_to_all(packed, 'seq', split_axis=0, concat_axis=0, tiled=True)  9.6 us
    ppermute x3, starting transfers between devices, swap_cores(): return lax.ppermute(block, 'grp', [(0, 1), (1, 0)])  8.9 us
    pallas_call x2, Pallas kernels, project(): pl.pallas_call(project_last_kernel if final else project_kernel, grid_spe...  8.04 us
    all_to_all x1, waiting for transfers between devices, shards(): lax.all_to_all(routed, 'seq', split_axis=0, concat_axis=0, tiled=True)  6.93 us
    pallas_call x1, Pallas kernels, attend(): pl.pallas_call(lambda *refs: attend_kernel(tp_count, *refs), grid_spec=pl...  6.68 us
    all_to_all x1, starting transfers between devices, shards(): lax.all_to_all(routed, 'seq', split_axis=0, concat_axis=0, tiled=True)  6.64 us
  transfers between devices with their start and end apart: 17, of which 13 were waited for; matrix products, arithmetic and copies ran while one was open for 1% of the time, Pallas kernels for 18%

profile of v6, /device:TPU:1, one launch (start us, length us, event | category | flops | bytes accessed | tf_op | source)
XLA Modules:
  0.0 115.4 jit_solution(6000355324334960313)
XLA Ops:
  0.0 3.2 %collective-permute-start.6 = (bf16[4096,512]{1,0:T(8,128)(2,1)}, bf16[4096,512]{1,0:T(8,128)(2,1)}, u32[]{:S(2)}, u32[]{:S(2)}) collective-permute-start(bf16[4096,512]{1,0:T(8,128)(2,1)} %bitcast.21), channel_id=1, source_target_pairs={{0,128},{128,0},{1,129},{129,1},{2,130},{130,2},{3,131},{131,3},{4... | collective-permute-start | bytes 12582920 | tf_op jit(solution)/shard_map/ppermute | solution.py:45
  4.0 1.4 %copy-done.3 = bf16[24,64,512]{2,1,0:T(8,128)(2,1)S(1)} copy-done((bf16[24,64,512]{2,1,0:T(8,128)(2,1)S(1)}, bf16[24,64,512]{2,1,0:T(8,128)(2,1)}, u32[]{:S(2)}) %copy-start.3) | copy-done | bytes 1572888
  5.4 2.0 %pack_rows.1 = bf16[32,104,128]{2,1,0:T(8,128)(2,1)} custom-call(s32[2]{0:T(128)S(1)} %pad_add_fusion.place_ref.refs_0_, s32[2,12]{1,0:T(2,128)S(1)} %fusion.refs_1_, bf16[24,64,512]{2,1,0:T(8,128)(2,1)S(1)} %copy-done.3), custom_call_target="tpu_custom_call" | custom-call | flops 3000000000 | bytes 3000000 | tf_op jit(solution)/shard_map/pack_rows/pallas_call | solution.py:107
  7.5 9.6 %all-to-all-start = ((bf16[32,104,128]{2,1,0:T(8,128)(2,1)}), bf16[32,104,128]{2,1,0:T(8,128)(2,1)S(1)}, u32[]{:S(2)}, u32[]{:S(2)}) async-start(bf16[32,104,128]{2,1,0:T(8,128)(2,1)} %pack_rows.1), calls=%async_computation | async-start | bytes 1703936 | tf_op jit(solution)/shard_map/all_to_all | solution.py:533
  17.2 1.3 %collective-permute-start.2 = (bf16[192,1024]{1,0:T(8,128)(2,1)S(1)}, bf16[192,1024]{1,0:T(8,128)(2,1)S(1)}, u32[]{:S(2)}, u32[]{:S(2)}) collective-permute-start(bf16[192,1024]{1,0:T(8,128)(2,1)S(1)} %get-tuple-element.37.refs_1_), channel_id=1, source_target_pairs={{0,1},{1,0},{2,3},{3,2},{4,5},{5,4},{6,7},{7,6},{8,9},{9,8},{10,11... | collective-permute-start | bytes 1179656 | tf_op jit(solution)/shard_map/ppermute | solution.py:50
  18.5 1.8 %collective-permute-start = (bf16[192,1024]{1,0:T(8,128)(2,1)S(1)}, bf16[192,1024]{1,0:T(8,128)(2,1)S(1)}, u32[]{:S(2)}, u32[]{:S(2)}) collective-permute-start(bf16[192,1024]{1,0:T(8,128)(2,1)S(1)} %get-tuple-element.38.refs_0_), channel_id=1, source_target_pairs={{0,3},{1,2},{2,1},{3,0},{4,7},{5,6},{6,5},{7,4},{8,11},{9,10},{10,... | collective-permute-start | bytes 1179656 | tf_op jit(solution)/shard_map/ppermute | solution.py:50
  21.2 6.5 %collective-permute-done.2.refs_3_ = bf16[192,1024]{1,0:T(8,128)(2,1)S(1)} collective-permute-done((bf16[192,1024]{1,0:T(8,128)(2,1)S(1)}, bf16[192,1024]{1,0:T(8,128)(2,1)S(1)}, u32[]{:S(2)}, u32[]{:S(2)}) %collective-permute-start.2) | collective-permute-done | bytes 393248 | tf_op jit(solution)/shard_map/ppermute | solution.py:50
  27.7 2.1 %collective-permute-done.refs_4_ = bf16[192,1024]{1,0:T(8,128)(2,1)S(1)} collective-permute-done((bf16[192,1024]{1,0:T(8,128)(2,1)S(1)}, bf16[192,1024]{1,0:T(8,128)(2,1)S(1)}, u32[]{:S(2)}, u32[]{:S(2)}) %collective-permute-start) | collective-permute-done | bytes 393248 | tf_op jit(solution)/shard_map/ppermute | solution.py:50
  29.8 6.3 %collective-permute-done.4.refs_2_ = bf16[192,1024]{1,0:T(8,128)(2,1)S(1)} collective-permute-done((bf16[192,1024]{1,0:T(8,128)(2,1)S(1)}, bf16[192,1024]{1,0:T(8,128)(2,1)S(1)}, u32[]{:S(2)}, u32[]{:S(2)}) %collective-permute-start.4) | collective-permute-done | bytes 393248 | tf_op jit(solution)/shard_map/ppermute | solution.py:50
  36.1 2.1 %collective-permute-done.5.refs_5_ = bf16[192,1024]{1,0:T(8,128)(2,1)S(1)} collective-permute-done((bf16[192,1024]{1,0:T(8,128)(2,1)S(1)}, bf16[192,1024]{1,0:T(8,128)(2,1)S(1)}, u32[]{:S(2)}, u32[]{:S(2)}) %collective-permute-start.5) | collective-permute-done | bytes 393248 | tf_op jit(solution)/shard_map/ppermute | solution.py:50
  38.2 2.3 %all-to-all-done.refs_0_ = bf16[32,104,128]{2,1,0:T(8,128)(2,1)S(1)} async-done(((bf16[32,104,128]{2,1,0:T(8,128)(2,1)}), bf16[32,104,128]{2,1,0:T(8,128)(2,1)S(1)}, u32[]{:S(2)}, u32[]{:S(2)}) %all-to-all-start) | async-done | bytes 852000 | tf_op jit(solution)/shard_map/all_to_all | solution.py:533
  40.5 1.9 %route_rows.1 = bf16[32,96,128]{2,1,0:T(8,128)(2,1)} custom-call(bf16[32,104,128]{2,1,0:T(8,128)(2,1)S(1)} %all-to-all-done.refs_0_, bf16[16,128]{1,0:T(8,128)(2,1)S(1)} %slice.20.refs_1_, bf16[16,128]{1,0:T(8,128)(2,1)S(1)} %slice.21.refs_2_, bf16[16,128]{1,0:T(8,128)(2,1)S(1)} %slice.22.refs_3_, bf16[16,128]{1,0:T(8,128)(2,1)S(1)} %slice.23.refs_4_), custom_call_target="tpu_custom_call" | custom-call | flops 2000000000 | bytes 2000000 | tf_op jit(solution)/shard_map/route_rows/pallas_call | solution.py:161
  42.3 6.6 %all-to-all-start.1 = ((bf16[32,96,128]{2,1,0:T(8,128)(2,1)}), bf16[32,96,128]{2,1,0:T(8,128)(2,1)S(1)}, u32[]{:S(2)}, u32[]{:S(2)}) async-start(bf16[32,96,128]{2,1,0:T(8,128)(2,1)} %route_rows.1), calls=%async_computation.1 | async-start | bytes 1572864 | tf_op jit(solution)/shard_map/all_to_all | solution.py:535
  49.1 1.9 %collective-permute-start.3 = (bf16[192,1024]{1,0:T(8,128)(2,1)S(1)}, bf16[192,1024]{1,0:T(8,128)(2,1)S(1)}, u32[]{:S(2)}, u32[]{:S(2)}) collective-permute-start(bf16[192,1024]{1,0:T(8,128)(2,1)S(1)} %collective-permute-done.2.refs_3_), channel_id=1, source_target_pairs={{0,3},{1,2},{2,1},{3,0},{4,7},{5,6},{6,5},{7,4},{8,11},{9,10},{10,... | collective-permute-start | bytes 1179656 | tf_op jit(solution)/shard_map/ppermute | solution.py:50
  51.0 2.2 %copy-done = bf16[1,4096,512]{2,1,0:T(8,128)(2,1)S(1)} copy-done((bf16[1,4096,512]{2,1,0:T(8,128)(2,1)S(1)}, bf16[1,4096,512]{2,1,0:T(8,128)(2,1)}, u32[]{:S(2)}) %copy-start) | copy-done | bytes 4194328
  53.2 5.3 %project.2 = (f32[384,512]{1,0:T(8,128)S(1)}, f32[384,512]{1,0:T(8,128)S(1)}) custom-call(s32[2]{0:T(128)S(1)} %pad_add_fusion.place_ref.refs_0_, bf16[192,1024]{1,0:T(8,128)(2,1)S(1)} %get-tuple-element.38.refs_0_, bf16[192,1024]{1,0:T(8,128)(2,1)S(1)} %get-tuple-element.37.refs_1_, bf16[192,1024]{1,0:T(8,128)(2,1)S(1)} %collective-permute-done.4.refs_2_, ...), custom_call_target="tpu_custom_call" | custom-call | flops 7500000256 | bytes 7500000 | tf_op jit(solution)/shard_map/project/pallas_call | solution.py:239
  59.0 2.8 %project.3 = (bf16[384,512]{1,0:T(8,128)(2,1)S(1)}, bf16[384,512]{1,0:T(8,128)(2,1)S(1)}) custom-call(s32[2]{0:T(128)S(1)} %pad_add_fusion.place_ref.refs_0_, bf16[192,1024]{1,0:T(8,128)(2,1)S(1)} %collective-permute-done.1.refs_0_, bf16[192,1024]{1,0:T(8,128)(2,1)S(1)} %collective-permute-done.3.refs_1_, f32[384,512]{1,0:T(8,128)S(1)} %get-tuple-element.21.refs_2_, ...), custom_call_target="tpu_custom_call" | custom-call | flops 2500000000 | bytes 2500000 | tf_op jit(solution)/shard_map/project/pallas_call | solution.py:239
  61.8 6.9 %all-to-all-done.1.refs_1_ = bf16[32,96,128]{2,1,0:T(8,128)(2,1)S(1)} async-done(((bf16[32,96,128]{2,1,0:T(8,128)(2,1)}), bf16[32,96,128]{2,1,0:T(8,128)(2,1)S(1)}, u32[]{:S(2)}, u32[]{:S(2)}) %all-to-all-start.1) | async-done | bytes 786464 | tf_op jit(solution)/shard_map/all_to_all | solution.py:535
  69.6 4.4 %collective-permute-start.7 = (bf16[768,256]{1,0:T(8,128)(2,1)S(1)}, bf16[768,256]{1,0:T(8,128)(2,1)S(1)}, u32[]{:S(2)}, u32[]{:S(2)}) collective-permute-start(bf16[768,256]{1,0:T(8,128)(2,1)S(1)} %unpack_rows.2.refs_2_), channel_id=1, source_target_pairs={{0,128},{128,0},{1,129},{129,1},{2,130},{130,2},{3,131},{131,3},{4... | collective-permute-start | bytes 1179656 | tf_op jit(solution)/shard_map/ppermute | solution.py:45
  75.4 6.7 %attend.1 = (bf16[384,512]{1,0:T(8,128)(2,1)S(1)}, bf16[384,512]{1,0:T(8,128)(2,1)S(1)}, bf16[192,1024]{1,0:T(8,128)(2,1)S(1)}, bf16[192,1024]{1,0:T(8,128)(2,1)S(1)}) custom-call(s32[2]{0:T(128)S(1)} %pad_add_fusion.place_ref.refs_0_, bf16[384,512]{1,0:T(8,128)(2,1)S(1)} %get-tuple-element.23.refs_1_, bf16[384,512]{1,0:T(8,128)(2,1)S(1)} %get-tuple-element.24.refs_2_, ...), custom_call_target="tpu_custom_call" | custom-call | flops 8000000000 | bytes 8000000 | tf_op jit(solution)/shard_map/attend/pallas_call | solution.py:358
  82.2 1.9 %collective-permute-start.9 = (bf16[192,1024]{1,0:T(8,128)(2,1)S(1)}, bf16[192,1024]{1,0:T(8,128)(2,1)S(1)}, u32[]{:S(2)}, u32[]{:S(2)}) collective-permute-start(bf16[192,1024]{1,0:T(8,128)(2,1)S(1)} %get-tuple-element.30), channel_id=1, source_target_pairs={{0,3},{1,2},{2,1},{3,0},{4,7},{5,6},{6,5},{7,4},{8,11},{9,10},{10,... | collective-permute-start | bytes 1179656 | tf_op jit(solution)/shard_map/ppermute | solution.py:50
  84.1 3.9 %partial_terms.2 = (bf16[192,1024]{1,0:T(8,128)(2,1)S(1)}, bf16[192,1024]{1,0:T(8,128)(2,1)S(1)}, bf16[192,1024]{1,0:T(8,128)(2,1)S(1)}, bf16[192,1024]{1,0:T(8,128)(2,1)S(1)}) custom-call(s32[2]{0:T(128)S(1)} %pad_add_fusion.place_ref.refs_0_, bf16[384,512]{1,0:T(8,128)(2,1)S(1)} %get-tuple-element.25.refs_1_, ...), custom_call_target="tpu_custom_call" | custom-call | flops 4000000000 | bytes 4000000 | tf_op jit(solution)/shard_map/partial_terms/pallas_call | solution.py:404
  89.6 2.8 %collective-permute-done.8.refs_2_ = bf16[192,1024]{1,0:T(8,128)(2,1)S(1)} collective-permute-done((bf16[192,1024]{1,0:T(8,128)(2,1)S(1)}, bf16[192,1024]{1,0:T(8,128)(2,1)S(1)}, u32[]{:S(2)}, u32[]{:S(2)}) %collective-permute-start.8) | collective-permute-done | bytes 393248 | tf_op jit(solution)/shard_map/ppermute | solution.py:50
  92.5 1.3 %collective-permute-done.9.refs_3_ = bf16[192,1024]{1,0:T(8,128)(2,1)S(1)} collective-permute-done((bf16[192,1024]{1,0:T(8,128)(2,1)S(1)}, bf16[192,1024]{1,0:T(8,128)(2,1)S(1)}, u32[]{:S(2)}, u32[]{:S(2)}) %collective-permute-start.9) | collective-permute-done | bytes 393248 | tf_op jit(solution)/shard_map/ppermute | solution.py:50
  94.0 1.9 %collective-permute-start.11 = (bf16[192,1024]{1,0:T(8,128)(2,1)S(1)}, bf16[192,1024]{1,0:T(8,128)(2,1)S(1)}, u32[]{:S(2)}, u32[]{:S(2)}) collective-permute-start(bf16[192,1024]{1,0:T(8,128)(2,1)S(1)} %get-tuple-element.31.refs_7_), channel_id=1, source_target_pairs={{0,3},{1,2},{2,1},{3,0},{4,7},{5,6},{6,5},{7,4},{8,11},{9,10},{10,... | collective-permute-start | bytes 1179656 | tf_op jit(solution)/shard_map/ppermute | solution.py:50
  95.9 2.8 %partial_terms.3 = (bf16[192,1024]{1,0:T(8,128)(2,1)S(1)}, bf16[192,1024]{1,0:T(8,128)(2,1)S(1)}) custom-call(s32[2]{0:T(128)S(1)} %pad_add_fusion.place_ref.refs_0_, bf16[384,512]{1,0:T(8,128)(2,1)S(1)} %get-tuple-element.25.refs_1_, bf16[384,512]{1,0:T(8,128)(2,1)S(1)} %get-tuple-element.26.refs_2_, bf16[4096,512]{1,0:T(8,128)(2,1)S(1)} %bitcast.27, ...), custom_call_target="tpu_custom_call" | custom-call | flops 2000000000 | bytes 2000000 | tf_op jit(solution)/shard_map/partial_terms/pallas_call | solution.py:404
  98.7 2.2 %collective-permute-done.10.refs_1_ = bf16[192,1024]{1,0:T(8,128)(2,1)S(1)} collective-permute-done((bf16[192,1024]{1,0:T(8,128)(2,1)S(1)}, bf16[192,1024]{1,0:T(8,128)(2,1)S(1)}, u32[]{:S(2)}, u32[]{:S(2)}) %collective-permute-start.10) | collective-permute-done | bytes 393248 | tf_op jit(solution)/shard_map/ppermute | solution.py:50
  100.9 1.3 %collective-permute-done.12.refs_4_ = bf16[192,1024]{1,0:T(8,128)(2,1)S(1)} collective-permute-done((bf16[192,1024]{1,0:T(8,128)(2,1)S(1)}, bf16[192,1024]{1,0:T(8,128)(2,1)S(1)}, u32[]{:S(2)}, u32[]{:S(2)}) %collective-permute-start.12) | collective-permute-done | bytes 393248 | tf_op jit(solution)/shard_map/ppermute | solution.py:50
  102.2 8.4 %collective-permute-done.11.refs_2_ = bf16[192,1024]{1,0:T(8,128)(2,1)S(1)} collective-permute-done((bf16[192,1024]{1,0:T(8,128)(2,1)S(1)}, bf16[192,1024]{1,0:T(8,128)(2,1)S(1)}, u32[]{:S(2)}, u32[]{:S(2)}) %collective-permute-start.11) | collective-permute-done | bytes 393248 | tf_op jit(solution)/shard_map/ppermute | solution.py:50
  111.3 1.3 %collective-permute-start.14 = (bf16[384,512]{1,0:T(8,128)(2,1)S(1)}, bf16[384,512]{1,0:T(8,128)(2,1)S(1)}, u32[]{:S(2)}, u32[]{:S(2)}) collective-permute-start(bf16[384,512]{1,0:T(8,128)(2,1)S(1)} %sum_columns.2), channel_id=1, source_target_pairs={{0,128},{128,0},{1,129},{129,1},{2,130},{130,2},{3,131},{131,3},{4... | collective-permute-start | bytes 1179656 | tf_op jit(solution)/shard_map/ppermute | solution.py:45
  112.6 1.4 %sum_columns.3.kept_ref = bf16[768,512]{1,0:T(8,128)(2,1)} custom-call(s32[2]{0:T(128)S(1)} %pad_add_fusion.place_ref.refs_0_, bf16[192,1024]{1,0:T(8,128)(2,1)S(1)} %get-tuple-element.32.refs_0_, bf16[192,1024]{1,0:T(8,128)(2,1)S(1)} %collective-permute-done.10.refs_1_, bf16[192,1024]{1,0:T(8,128)(2,1)S(1)} %collective-permute-done.11.refs_2_, ...), custom_call_target="tpu_custom_call" | custom-call | flops 1000000000 | bytes 1000000 | tf_op jit(solution)/shard_map/sum_columns/pallas_call | solution.py:470
  114.1 1.3 %place_rows.1 = bf16[768,512]{1,0:T(8,128)(2,1)} custom-call(s32[2]{0:T(128)S(1)} %pad_add_fusion.place_ref.refs_0_, bf16[384,512]{1,0:T(8,128)(2,1)S(1)} %collective-permute-done.14.received_ref, bf16[768,512]{1,0:T(8,128)(2,1)} %sum_columns.3.kept_ref), custom_call_target="tpu_custom_call", output_to_operand_aliasing={{}: (2, {})} | custom-call | flops 1000000000 | bytes 1000000 | tf_op jit(solution)/shard_map/place_rows/pallas_call | solution.py:491
  (35 shorter events, 7.3 us)
Async XLA Ops:
  0.0 51.0 %collective-permute-start.6 = (bf16[4096,512]{1,0:T(8,128)(2,1)}, bf16[4096,512]{1,0:T(8,128)(2,1)}, u32[]{:S(2)}, u32[]{:S(2)}) collective-permute-start(bf16[4096,512]{1,0:T(8,128)(2,1)} %bitcast.21), channel_id=1, source_target_pairs={{0,128},{128,0},{1,129},{129,1},{2,130},{130,2},{3,131},{131,3},{4... | collective-permute-start | bytes 12582920 | tf_op jit(solution)/shard_map/ppermute | solution.py:45
  4.0 1.4 %copy-start.3 = (bf16[24,64,512]{2,1,0:T(8,128)(2,1)S(1)}, bf16[24,64,512]{2,1,0:T(8,128)(2,1)}, u32[]{:S(2)}) copy-start(bf16[24,64,512]{2,1,0:T(8,128)(2,1)} %refs_2_.1) | copy-start | bytes 4718596
  7.5 9.6 %copy-start.5 = (bf16[768,1024]{1,0:T(8,128)(2,1)S(1)}, bf16[768,1024]{1,0:T(8,128)(2,1)}, u32[]{:S(2)}) copy-start(bf16[768,1024]{1,0:T(8,128)(2,1)} %param.6) | copy-start | bytes 4718596
  7.5 33.0 %all-to-all-start = ((bf16[32,104,128]{2,1,0:T(8,128)(2,1)}), bf16[32,104,128]{2,1,0:T(8,128)(2,1)S(1)}, u32[]{:S(2)}, u32[]{:S(2)}) async-start(bf16[32,104,128]{2,1,0:T(8,128)(2,1)} %pack_rows.1), calls=%async_computation | async-start | bytes 1703936 | tf_op jit(solution)/shard_map/all_to_all | solution.py:533
  17.2 10.5 %collective-permute-start.2 = (bf16[192,1024]{1,0:T(8,128)(2,1)S(1)}, bf16[192,1024]{1,0:T(8,128)(2,1)S(1)}, u32[]{:S(2)}, u32[]{:S(2)}) collective-permute-start(bf16[192,1024]{1,0:T(8,128)(2,1)S(1)} %get-tuple-element.37.refs_1_), channel_id=1, source_target_pairs={{0,1},{1,0},{2,3},{3,2},{4,5},{5,4},{6,7},{7,6},{8,9},{9,8},{10,11... | collective-permute-start | bytes 1179656 | tf_op jit(solution)/shard_map/ppermute | solution.py:50
  18.5 11.3 %collective-permute-start = (bf16[192,1024]{1,0:T(8,128)(2,1)S(1)}, bf16[192,1024]{1,0:T(8,128)(2,1)S(1)}, u32[]{:S(2)}, u32[]{:S(2)}) collective-permute-start(bf16[192,1024]{1,0:T(8,128)(2,1)S(1)} %get-tuple-element.38.refs_0_), channel_id=1, source_target_pairs={{0,3},{1,2},{2,1},{3,0},{4,7},{5,6},{6,5},{7,4},{8,11},{9,10},{10,... | collective-permute-start | bytes 1179656 | tf_op jit(solution)/shard_map/ppermute | solution.py:50
  20.3 15.8 %collective-permute-start.4 = (bf16[192,1024]{1,0:T(8,128)(2,1)S(1)}, bf16[192,1024]{1,0:T(8,128)(2,1)S(1)}, u32[]{:S(2)}, u32[]{:S(2)}) collective-permute-start(bf16[192,1024]{1,0:T(8,128)(2,1)S(1)} %get-tuple-element.38.refs_0_), channel_id=1, source_target_pairs={{0,1},{1,0},{2,3},{3,2},{4,5},{5,4},{6,7},{7,6},{8,9},{9,8},{10,11... | collective-permute-start | bytes 1179656 | tf_op jit(solution)/shard_map/ppermute | solution.py:50
  20.6 17.6 %collective-permute-start.5 = (bf16[192,1024]{1,0:T(8,128)(2,1)S(1)}, bf16[192,1024]{1,0:T(8,128)(2,1)S(1)}, u32[]{:S(2)}, u32[]{:S(2)}) collective-permute-start(bf16[192,1024]{1,0:T(8,128)(2,1)S(1)} %get-tuple-element.37.refs_1_), channel_id=1, source_target_pairs={{0,3},{1,2},{2,1},{3,0},{4,7},{5,6},{6,5},{7,4},{8,11},{9,10},{10,... | collective-permute-start | bytes 1179656 | tf_op jit(solution)/shard_map/ppermute | solution.py:50
  42.3 26.4 %all-to-all-start.1 = ((bf16[32,96,128]{2,1,0:T(8,128)(2,1)}), bf16[32,96,128]{2,1,0:T(8,128)(2,1)S(1)}, u32[]{:S(2)}, u32[]{:S(2)}) async-start(bf16[32,96,128]{2,1,0:T(8,128)(2,1)} %route_rows.1), calls=%async_computation.1 | async-start | bytes 1572864 | tf_op jit(solution)/shard_map/all_to_all | solution.py:535
  49.0 9.5 %collective-permute-start.1 = (bf16[192,1024]{1,0:T(8,128)(2,1)S(1)}, bf16[192,1024]{1,0:T(8,128)(2,1)S(1)}, u32[]{:S(2)}, u32[]{:S(2)}) collective-permute-start(bf16[192,1024]{1,0:T(8,128)(2,1)S(1)} %collective-permute-done.refs_4_), channel_id=1, source_target_pairs={{0,1},{1,0},{2,3},{3,2},{4,5},{5,4},{6,7},{7,6},{8,9},{9,8},{10,11... | collective-permute-start | bytes 1179656 | tf_op jit(solution)/shard_map/ppermute | solution.py:50
  49.1 9.9 %collective-permute-start.3 = (bf16[192,1024]{1,0:T(8,128)(2,1)S(1)}, bf16[192,1024]{1,0:T(8,128)(2,1)S(1)}, u32[]{:S(2)}, u32[]{:S(2)}) collective-permute-start(bf16[192,1024]{1,0:T(8,128)(2,1)S(1)} %collective-permute-done.2.refs_3_), channel_id=1, source_target_pairs={{0,3},{1,2},{2,1},{3,0},{4,7},{5,6},{6,5},{7,4},{8,11},{9,10},{10,... | collective-permute-start | bytes 1179656 | tf_op jit(solution)/shard_map/ppermute | solution.py:50
  51.0 2.2 %copy-start = (bf16[1,4096,512]{2,1,0:T(8,128)(2,1)S(1)}, bf16[1,4096,512]{2,1,0:T(8,128)(2,1)}, u32[]{:S(2)}) copy-start(bf16[1,4096,512]{2,1,0:T(8,128)(2,1)} %param.7) | copy-start | bytes 12582916
  53.2 5.8 %copy-start.1 = (bf16[1,4096,512]{2,1,0:T(8,128)(2,1)S(1)}, bf16[1,4096,512]{2,1,0:T(8,128)(2,1)}, u32[]{:S(2)}) copy-start(bf16[1,4096,512]{2,1,0:T(8,128)(2,1)} %param.7) | copy-start | bytes 12582916
  68.7 6.7 %copy-start.2 = (bf16[1,4096,512]{2,1,0:T(8,128)(2,1)S(1)}, bf16[1,4096,512]{2,1,0:T(8,128)(2,1)}, u32[]{:S(2)}) copy-start(bf16[1,4096,512]{2,1,0:T(8,128)(2,1)} %param.7) | copy-start | bytes 12582916
  69.6 5.7 %copy-start.4 = (bf16[768,512]{1,0:T(8,128)(2,1)S(1)}, bf16[768,512]{1,0:T(8,128)(2,1)}, u32[]{:S(2)}) copy-start(bf16[768,512]{1,0:T(8,128)(2,1)} %refs_3_.1) | copy-start | bytes 2359300
  69.6 5.7 %collective-permute-start.7 = (bf16[768,256]{1,0:T(8,128)(2,1)S(1)}, bf16[768,256]{1,0:T(8,128)(2,1)S(1)}, u32[]{:S(2)}, u32[]{:S(2)}) collective-permute-start(bf16[768,256]{1,0:T(8,128)(2,1)S(1)} %unpack_rows.2.refs_2_), channel_id=1, source_target_pairs={{0,128},{128,0},{1,129},{129,1},{2,130},{130,2},{3,131},{131,3},{4... | collective-permute-start | bytes 1179656 | tf_op jit(solution)/shard_map/ppermute | solution.py:45
  82.1 10.4 %collective-permute-start.8 = (bf16[192,1024]{1,0:T(8,128)(2,1)S(1)}, bf16[192,1024]{1,0:T(8,128)(2,1)S(1)}, u32[]{:S(2)}, u32[]{:S(2)}) collective-permute-start(bf16[192,1024]{1,0:T(8,128)(2,1)S(1)} %get-tuple-element.29), channel_id=1, source_target_pairs={{0,1},{1,0},{2,3},{3,2},{4,5},{5,4},{6,7},{7,6},{8,9},{9,8},{10,11... | collective-permute-start | bytes 1179656 | tf_op jit(solution)/shard_map/ppermute | solution.py:50
  82.2 11.6 %collective-permute-start.9 = (bf16[192,1024]{1,0:T(8,128)(2,1)S(1)}, bf16[192,1024]{1,0:T(8,128)(2,1)S(1)}, u32[]{:S(2)}, u32[]{:S(2)}) collective-permute-start(bf16[192,1024]{1,0:T(8,128)(2,1)S(1)} %get-tuple-element.30), channel_id=1, source_target_pairs={{0,3},{1,2},{2,1},{3,0},{4,7},{5,6},{6,5},{7,4},{8,11},{9,10},{10,... | collective-permute-start | bytes 1179656 | tf_op jit(solution)/shard_map/ppermute | solution.py:50
  87.9 13.0 %collective-permute-start.10 = (bf16[192,1024]{1,0:T(8,128)(2,1)S(1)}, bf16[192,1024]{1,0:T(8,128)(2,1)S(1)}, u32[]{:S(2)}, u32[]{:S(2)}) collective-permute-start(bf16[192,1024]{1,0:T(8,128)(2,1)S(1)} %get-tuple-element.33), channel_id=1, source_target_pairs={{0,1},{1,0},{2,3},{3,2},{4,5},{5,4},{6,7},{7,6},{8,9},{9,8},{10,11... | collective-permute-start | bytes 1179656 | tf_op jit(solution)/shard_map/ppermute | solution.py:50
  88.8 13.4 %collective-permute-start.12 = (bf16[192,1024]{1,0:T(8,128)(2,1)S(1)}, bf16[192,1024]{1,0:T(8,128)(2,1)S(1)}, u32[]{:S(2)}, u32[]{:S(2)}) collective-permute-start(bf16[192,1024]{1,0:T(8,128)(2,1)S(1)} %get-tuple-element.35), channel_id=1, source_target_pairs={{0,3},{1,2},{2,1},{3,0},{4,7},{5,6},{6,5},{7,4},{8,11},{9,10},{10,... | collective-permute-start | bytes 1179656 | tf_op jit(solution)/shard_map/ppermute | solution.py:50
  94.0 16.7 %collective-permute-start.11 = (bf16[192,1024]{1,0:T(8,128)(2,1)S(1)}, bf16[192,1024]{1,0:T(8,128)(2,1)S(1)}, u32[]{:S(2)}, u32[]{:S(2)}) collective-permute-start(bf16[192,1024]{1,0:T(8,128)(2,1)S(1)} %get-tuple-element.31.refs_7_), channel_id=1, source_target_pairs={{0,3},{1,2},{2,1},{3,0},{4,7},{5,6},{6,5},{7,4},{8,11},{9,10},{10,... | collective-permute-start | bytes 1179656 | tf_op jit(solution)/shard_map/ppermute | solution.py:50
  95.9 14.7 %collective-permute-start.13 = (bf16[192,1024]{1,0:T(8,128)(2,1)S(1)}, bf16[192,1024]{1,0:T(8,128)(2,1)S(1)}, u32[]{:S(2)}, u32[]{:S(2)}) collective-permute-start(bf16[192,1024]{1,0:T(8,128)(2,1)S(1)} %get-tuple-element.36), channel_id=1, source_target_pairs={{0,1},{1,0},{2,3},{3,2},{4,5},{5,4},{6,7},{7,6},{8,9},{9,8},{10,11... | collective-permute-start | bytes 1179656 | tf_op jit(solution)/shard_map/ppermute | solution.py:50
  111.3 2.7 %collective-permute-start.14 = (bf16[384,512]{1,0:T(8,128)(2,1)S(1)}, bf16[384,512]{1,0:T(8,128)(2,1)S(1)}, u32[]{:S(2)}, u32[]{:S(2)}) collective-permute-start(bf16[384,512]{1,0:T(8,128)(2,1)S(1)} %sum_columns.2), channel_id=1, source_target_pairs={{0,128},{128,0},{1,129},{129,1},{2,130},{130,2},{3,131},{131,3},{4... | collective-permute-start | bytes 1179656 | tf_op jit(solution)/shard_map/ppermute | solution.py:45

commit v7 on v6

--- a/solution.py
+++ b/solution.py
@@ -136,7 +136,7 @@
         held.append(jnp.concatenate(pieces, axis=1).astype(BF16))
     held = jnp.concatenate(held, axis=0)
     lanes = lax.broadcasted_iota(jnp.int32, (owned, total), 1).astype(jnp.float32)
-    per_dot = min(16, owners)
+    per_dot = min(32, owners)
     for begin in range(0, owners, per_dot):
         choose = []
         for s in range(begin, begin + per_dot):

time: 116 us -> 116 us (level)
  no operation moved by 1% of the time
where the time goes in v7:
time: 116 us
  waiting for transfers between devices  43.3 us (37%)
  starting transfers between devices  36.8 us (32%)
  Pallas kernels  30.8 us (27%)
  local copies, waits for them, and re-layouts  3.68 us (3%)
    ppermute x12, waiting for transfers between devices, swap(): return lax.ppermute(block, 'tp', [(i, i ^ mask) for i in range(count)])  33.7 us
    ppermute x12, starting transfers between devices, swap(): return lax.ppermute(block, 'tp', [(i, i ^ mask) for i in range(count)])  11.6 us
    all_to_all x1, starting transfers between devices, shards(): lax.all_to_all(packed, 'seq', split_axis=0, concat_axis=0, tiled=True)  9.6 us
    ppermute x3, starting transfers between devices, swap_cores(): return lax.ppermute(block, 'grp', [(0, 1), (1, 0)])  8.9 us
    pallas_call x2, Pallas kernels, project(): pl.pallas_call(project_last_kernel if final else project_kernel, grid_spe...  8.05 us
    all_to_all x1, waiting for transfers between devices, shards(): lax.all_to_all(routed, 'seq', split_axis=0, concat_axis=0, tiled=True)  6.92 us
    pallas_call x1, Pallas kernels, attend(): pl.pallas_call(lambda *refs: attend_kernel(tp_count, *refs), grid_spec=pl...  6.68 us
    all_to_all x1, starting transfers between devices, shards(): lax.all_to_all(routed, 'seq', split_axis=0, concat_axis=0, tiled=True)  6.65 us
  transfers between devices with their start and end apart: 17, of which 13 were waited for; matrix products, arithmetic and copies ran while one was open for 1% of the time, Pallas kernels for 18%

profile of v7, /device:TPU:1, one launch (start us, length us, event | category | flops | bytes accessed | tf_op | source)
XLA Modules:
  0.0 115.5 jit_solution(7860598432450412294)
XLA Ops:
  0.0 3.2 %collective-permute-start.6 = (bf16[4096,512]{1,0:T(8,128)(2,1)}, bf16[4096,512]{1,0:T(8,128)(2,1)}, u32[]{:S(2)}, u32[]{:S(2)}) collective-permute-start(bf16[4096,512]{1,0:T(8,128)(2,1)} %bitcast.21), channel_id=1, source_target_pairs={{0,128},{128,0},{1,129},{129,1},{2,130},{130,2},{3,131},{131,3},{4... | collective-permute-start | bytes 12582920 | tf_op jit(solution)/shard_map/ppermute | solution.py:45
  4.0 1.4 %copy-done.3 = bf16[24,64,512]{2,1,0:T(8,128)(2,1)S(1)} copy-done((bf16[24,64,512]{2,1,0:T(8,128)(2,1)S(1)}, bf16[24,64,512]{2,1,0:T(8,128)(2,1)}, u32[]{:S(2)}) %copy-start.3) | copy-done | bytes 1572888
  5.4 2.0 %pack_rows.1 = bf16[32,104,128]{2,1,0:T(8,128)(2,1)} custom-call(s32[2]{0:T(128)S(1)} %pad_add_fusion.place_ref.refs_0_, s32[2,12]{1,0:T(2,128)S(1)} %fusion.refs_1_, bf16[24,64,512]{2,1,0:T(8,128)(2,1)S(1)} %copy-done.3), custom_call_target="tpu_custom_call" | custom-call | flops 3000000000 | bytes 3000000 | tf_op jit(solution)/shard_map/pack_rows/pallas_call | solution.py:107
  7.5 9.6 %all-to-all-start = ((bf16[32,104,128]{2,1,0:T(8,128)(2,1)}), bf16[32,104,128]{2,1,0:T(8,128)(2,1)S(1)}, u32[]{:S(2)}, u32[]{:S(2)}) async-start(bf16[32,104,128]{2,1,0:T(8,128)(2,1)} %pack_rows.1), calls=%async_computation | async-start | bytes 1703936 | tf_op jit(solution)/shard_map/all_to_all | solution.py:533
  17.2 1.3 %collective-permute-start.2 = (bf16[192,1024]{1,0:T(8,128)(2,1)S(1)}, bf16[192,1024]{1,0:T(8,128)(2,1)S(1)}, u32[]{:S(2)}, u32[]{:S(2)}) collective-permute-start(bf16[192,1024]{1,0:T(8,128)(2,1)S(1)} %get-tuple-element.37.refs_1_), channel_id=1, source_target_pairs={{0,1},{1,0},{2,3},{3,2},{4,5},{5,4},{6,7},{7,6},{8,9},{9,8},{10,11... | collective-permute-start | bytes 1179656 | tf_op jit(solution)/shard_map/ppermute | solution.py:50
  18.5 1.8 %collective-permute-start = (bf16[192,1024]{1,0:T(8,128)(2,1)S(1)}, bf16[192,1024]{1,0:T(8,128)(2,1)S(1)}, u32[]{:S(2)}, u32[]{:S(2)}) collective-permute-start(bf16[192,1024]{1,0:T(8,128)(2,1)S(1)} %get-tuple-element.38.refs_0_), channel_id=1, source_target_pairs={{0,3},{1,2},{2,1},{3,0},{4,7},{5,6},{6,5},{7,4},{8,11},{9,10},{10,... | collective-permute-start | bytes 1179656 | tf_op jit(solution)/shard_map/ppermute | solution.py:50
  21.2 6.5 %collective-permute-done.2.refs_3_ = bf16[192,1024]{1,0:T(8,128)(2,1)S(1)} collective-permute-done((bf16[192,1024]{1,0:T(8,128)(2,1)S(1)}, bf16[192,1024]{1,0:T(8,128)(2,1)S(1)}, u32[]{:S(2)}, u32[]{:S(2)}) %collective-permute-start.2) | collective-permute-done | bytes 393248 | tf_op jit(solution)/shard_map/ppermute | solution.py:50
  27.7 2.1 %collective-permute-done.refs_4_ = bf16[192,1024]{1,0:T(8,128)(2,1)S(1)} collective-permute-done((bf16[192,1024]{1,0:T(8,128)(2,1)S(1)}, bf16[192,1024]{1,0:T(8,128)(2,1)S(1)}, u32[]{:S(2)}, u32[]{:S(2)}) %collective-permute-start) | collective-permute-done | bytes 393248 | tf_op jit(solution)/shard_map/ppermute | solution.py:50
  29.8 6.3 %collective-permute-done.4.refs_2_ = bf16[192,1024]{1,0:T(8,128)(2,1)S(1)} collective-permute-done((bf16[192,1024]{1,0:T(8,128)(2,1)S(1)}, bf16[192,1024]{1,0:T(8,128)(2,1)S(1)}, u32[]{:S(2)}, u32[]{:S(2)}) %collective-permute-start.4) | collective-permute-done | bytes 393248 | tf_op jit(solution)/shard_map/ppermute | solution.py:50
  36.1 2.1 %collective-permute-done.5.refs_5_ = bf16[192,1024]{1,0:T(8,128)(2,1)S(1)} collective-permute-done((bf16[192,1024]{1,0:T(8,128)(2,1)S(1)}, bf16[192,1024]{1,0:T(8,128)(2,1)S(1)}, u32[]{:S(2)}, u32[]{:S(2)}) %collective-permute-start.5) | collective-permute-done | bytes 393248 | tf_op jit(solution)/shard_map/ppermute | solution.py:50
  38.2 2.3 %all-to-all-done.refs_0_ = bf16[32,104,128]{2,1,0:T(8,128)(2,1)S(1)} async-done(((bf16[32,104,128]{2,1,0:T(8,128)(2,1)}), bf16[32,104,128]{2,1,0:T(8,128)(2,1)S(1)}, u32[]{:S(2)}, u32[]{:S(2)}) %all-to-all-start) | async-done | bytes 852000 | tf_op jit(solution)/shard_map/all_to_all | solution.py:533
  40.5 2.0 %route_rows.1 = bf16[32,96,128]{2,1,0:T(8,128)(2,1)} custom-call(bf16[32,104,128]{2,1,0:T(8,128)(2,1)S(1)} %all-to-all-done.refs_0_, bf16[16,128]{1,0:T(8,128)(2,1)S(1)} %slice.20.refs_1_, bf16[16,128]{1,0:T(8,128)(2,1)S(1)} %slice.21.refs_2_, bf16[16,128]{1,0:T(8,128)(2,1)S(1)} %slice.22.refs_3_, bf16[16,128]{1,0:T(8,128)(2,1)S(1)} %slice.23.refs_4_), custom_call_target="tpu_custom_call" | custom-call | flops 2000000000 | bytes 2000000 | tf_op jit(solution)/shard_map/route_rows/pallas_call | solution.py:161
  42.5 6.6 %all-to-all-start.1 = ((bf16[32,96,128]{2,1,0:T(8,128)(2,1)}), bf16[32,96,128]{2,1,0:T(8,128)(2,1)S(1)}, u32[]{:S(2)}, u32[]{:S(2)}) async-start(bf16[32,96,128]{2,1,0:T(8,128)(2,1)} %route_rows.1), calls=%async_computation.1 | async-start | bytes 1572864 | tf_op jit(solution)/shard_map/all_to_all | solution.py:535
  49.2 1.9 %collective-permute-start.3 = (bf16[192,1024]{1,0:T(8,128)(2,1)S(1)}, bf16[192,1024]{1,0:T(8,128)(2,1)S(1)}, u32[]{:S(2)}, u32[]{:S(2)}) collective-permute-start(bf16[192,1024]{1,0:T(8,128)(2,1)S(1)} %collective-permute-done.2.refs_3_), channel_id=1, source_target_pairs={{0,3},{1,2},{2,1},{3,0},{4,7},{5,6},{6,5},{7,4},{8,11},{9,10},{10,... | collective-permute-start | bytes 1179656 | tf_op jit(solution)/shard_map/ppermute | solution.py:50
  51.1 2.2 %copy-done = bf16[1,4096,512]{2,1,0:T(8,128)(2,1)S(1)} copy-done((bf16[1,4096,512]{2,1,0:T(8,128)(2,1)S(1)}, bf16[1,4096,512]{2,1,0:T(8,128)(2,1)}, u32[]{:S(2)}) %copy-start) | copy-done | bytes 4194328
  53.3 5.3 %project.2 = (f32[384,512]{1,0:T(8,128)S(1)}, f32[384,512]{1,0:T(8,128)S(1)}) custom-call(s32[2]{0:T(128)S(1)} %pad_add_fusion.place_ref.refs_0_, bf16[192,1024]{1,0:T(8,128)(2,1)S(1)} %get-tuple-element.38.refs_0_, bf16[192,1024]{1,0:T(8,128)(2,1)S(1)} %get-tuple-element.37.refs_1_, bf16[192,1024]{1,0:T(8,128)(2,1)S(1)} %collective-permute-done.4.refs_2_, ...), custom_call_target="tpu_custom_call" | custom-call | flops 7500000256 | bytes 7500000 | tf_op jit(solution)/shard_map/project/pallas_call | solution.py:239
  59.1 2.8 %project.3 = (bf16[384,512]{1,0:T(8,128)(2,1)S(1)}, bf16[384,512]{1,0:T(8,128)(2,1)S(1)}) custom-call(s32[2]{0:T(128)S(1)} %pad_add_fusion.place_ref.refs_0_, bf16[192,1024]{1,0:T(8,128)(2,1)S(1)} %collective-permute-done.1.refs_0_, bf16[192,1024]{1,0:T(8,128)(2,1)S(1)} %collective-permute-done.3.refs_1_, f32[384,512]{1,0:T(8,128)S(1)} %get-tuple-element.21.refs_2_, ...), custom_call_target="tpu_custom_call" | custom-call | flops 2500000000 | bytes 2500000 | tf_op jit(solution)/shard_map/project/pallas_call | solution.py:239
  61.9 6.9 %all-to-all-done.1.refs_1_ = bf16[32,96,128]{2,1,0:T(8,128)(2,1)S(1)} async-done(((bf16[32,96,128]{2,1,0:T(8,128)(2,1)}), bf16[32,96,128]{2,1,0:T(8,128)(2,1)S(1)}, u32[]{:S(2)}, u32[]{:S(2)}) %all-to-all-start.1) | async-done | bytes 786464 | tf_op jit(solution)/shard_map/all_to_all | solution.py:535
  69.8 4.4 %collective-permute-start.7 = (bf16[768,256]{1,0:T(8,128)(2,1)S(1)}, bf16[768,256]{1,0:T(8,128)(2,1)S(1)}, u32[]{:S(2)}, u32[]{:S(2)}) collective-permute-start(bf16[768,256]{1,0:T(8,128)(2,1)S(1)} %unpack_rows.2.refs_2_), channel_id=1, source_target_pairs={{0,128},{128,0},{1,129},{129,1},{2,130},{130,2},{3,131},{131,3},{4... | collective-permute-start | bytes 1179656 | tf_op jit(solution)/shard_map/ppermute | solution.py:45
  75.5 6.7 %attend.1 = (bf16[384,512]{1,0:T(8,128)(2,1)S(1)}, bf16[384,512]{1,0:T(8,128)(2,1)S(1)}, bf16[192,1024]{1,0:T(8,128)(2,1)S(1)}, bf16[192,1024]{1,0:T(8,128)(2,1)S(1)}) custom-call(s32[2]{0:T(128)S(1)} %pad_add_fusion.place_ref.refs_0_, bf16[384,512]{1,0:T(8,128)(2,1)S(1)} %get-tuple-element.23.refs_1_, bf16[384,512]{1,0:T(8,128)(2,1)S(1)} %get-tuple-element.24.refs_2_, ...), custom_call_target="tpu_custom_call" | custom-call | flops 8000000000 | bytes 8000000 | tf_op jit(solution)/shard_map/attend/pallas_call | solution.py:358
  82.3 1.9 %collective-permute-start.9 = (bf16[192,1024]{1,0:T(8,128)(2,1)S(1)}, bf16[192,1024]{1,0:T(8,128)(2,1)S(1)}, u32[]{:S(2)}, u32[]{:S(2)}) collective-permute-start(bf16[192,1024]{1,0:T(8,128)(2,1)S(1)} %get-tuple-element.30), channel_id=1, source_target_pairs={{0,3},{1,2},{2,1},{3,0},{4,7},{5,6},{6,5},{7,4},{8,11},{9,10},{10,... | collective-permute-start | bytes 1179656 | tf_op jit(solution)/shard_map/ppermute | solution.py:50
  84.2 3.9 %partial_terms.2 = (bf16[192,1024]{1,0:T(8,128)(2,1)S(1)}, bf16[192,1024]{1,0:T(8,128)(2,1)S(1)}, bf16[192,1024]{1,0:T(8,128)(2,1)S(1)}, bf16[192,1024]{1,0:T(8,128)(2,1)S(1)}) custom-call(s32[2]{0:T(128)S(1)} %pad_add_fusion.place_ref.refs_0_, bf16[384,512]{1,0:T(8,128)(2,1)S(1)} %get-tuple-element.25.refs_1_, ...), custom_call_target="tpu_custom_call" | custom-call | flops 4000000000 | bytes 4000000 | tf_op jit(solution)/shard_map/partial_terms/pallas_call | solution.py:404
  89.8 2.8 %collective-permute-done.8.refs_2_ = bf16[192,1024]{1,0:T(8,128)(2,1)S(1)} collective-permute-done((bf16[192,1024]{1,0:T(8,128)(2,1)S(1)}, bf16[192,1024]{1,0:T(8,128)(2,1)S(1)}, u32[]{:S(2)}, u32[]{:S(2)}) %collective-permute-start.8) | collective-permute-done | bytes 393248 | tf_op jit(solution)/shard_map/ppermute | solution.py:50
  92.6 1.3 %collective-permute-done.9.refs_3_ = bf16[192,1024]{1,0:T(8,128)(2,1)S(1)} collective-permute-done((bf16[192,1024]{1,0:T(8,128)(2,1)S(1)}, bf16[192,1024]{1,0:T(8,128)(2,1)S(1)}, u32[]{:S(2)}, u32[]{:S(2)}) %collective-permute-start.9) | collective-permute-done | bytes 393248 | tf_op jit(solution)/shard_map/ppermute | solution.py:50
  94.1 1.9 %collective-permute-start.11 = (bf16[192,1024]{1,0:T(8,128)(2,1)S(1)}, bf16[192,1024]{1,0:T(8,128)(2,1)S(1)}, u32[]{:S(2)}, u32[]{:S(2)}) collective-permute-start(bf16[192,1024]{1,0:T(8,128)(2,1)S(1)} %get-tuple-element.31.refs_7_), channel_id=1, source_target_pairs={{0,3},{1,2},{2,1},{3,0},{4,7},{5,6},{6,5},{7,4},{8,11},{9,10},{10,... | collective-permute-start | bytes 1179656 | tf_op jit(solution)/shard_map/ppermute | solution.py:50
  96.0 2.7 %partial_terms.3 = (bf16[192,1024]{1,0:T(8,128)(2,1)S(1)}, bf16[192,1024]{1,0:T(8,128)(2,1)S(1)}) custom-call(s32[2]{0:T(128)S(1)} %pad_add_fusion.place_ref.refs_0_, bf16[384,512]{1,0:T(8,128)(2,1)S(1)} %get-tuple-element.25.refs_1_, bf16[384,512]{1,0:T(8,128)(2,1)S(1)} %get-tuple-element.26.refs_2_, bf16[4096,512]{1,0:T(8,128)(2,1)S(1)} %bitcast.27, ...), custom_call_target="tpu_custom_call" | custom-call | flops 2000000000 | bytes 2000000 | tf_op jit(solution)/shard_map/partial_terms/pallas_call | solution.py:404
  98.8 2.3 %collective-permute-done.10.refs_1_ = bf16[192,1024]{1,0:T(8,128)(2,1)S(1)} collective-permute-done((bf16[192,1024]{1,0:T(8,128)(2,1)S(1)}, bf16[192,1024]{1,0:T(8,128)(2,1)S(1)}, u32[]{:S(2)}, u32[]{:S(2)}) %collective-permute-start.10) | collective-permute-done | bytes 393248 | tf_op jit(solution)/shard_map/ppermute | solution.py:50
  101.0 1.3 %collective-permute-done.12.refs_4_ = bf16[192,1024]{1,0:T(8,128)(2,1)S(1)} collective-permute-done((bf16[192,1024]{1,0:T(8,128)(2,1)S(1)}, bf16[192,1024]{1,0:T(8,128)(2,1)S(1)}, u32[]{:S(2)}, u32[]{:S(2)}) %collective-permute-start.12) | collective-permute-done | bytes 393248 | tf_op jit(solution)/shard_map/ppermute | solution.py:50
  102.4 8.4 %collective-permute-done.11.refs_2_ = bf16[192,1024]{1,0:T(8,128)(2,1)S(1)} collective-permute-done((bf16[192,1024]{1,0:T(8,128)(2,1)S(1)}, bf16[192,1024]{1,0:T(8,128)(2,1)S(1)}, u32[]{:S(2)}, u32[]{:S(2)}) %collective-permute-start.11) | collective-permute-done | bytes 393248 | tf_op jit(solution)/shard_map/ppermute | solution.py:50
  111.5 1.3 %collective-permute-start.14 = (bf16[384,512]{1,0:T(8,128)(2,1)S(1)}, bf16[384,512]{1,0:T(8,128)(2,1)S(1)}, u32[]{:S(2)}, u32[]{:S(2)}) collective-permute-start(bf16[384,512]{1,0:T(8,128)(2,1)S(1)} %sum_columns.2), channel_id=1, source_target_pairs={{0,128},{128,0},{1,129},{129,1},{2,130},{130,2},{3,131},{131,3},{4... | collective-permute-start | bytes 1179656 | tf_op jit(solution)/shard_map/ppermute | solution.py:45
  112.8 1.4 %sum_columns.3.kept_ref = bf16[768,512]{1,0:T(8,128)(2,1)} custom-call(s32[2]{0:T(128)S(1)} %pad_add_fusion.place_ref.refs_0_, bf16[192,1024]{1,0:T(8,128)(2,1)S(1)} %get-tuple-element.32.refs_0_, bf16[192,1024]{1,0:T(8,128)(2,1)S(1)} %collective-permute-done.10.refs_1_, bf16[192,1024]{1,0:T(8,128)(2,1)S(1)} %collective-permute-done.11.refs_2_, ...), custom_call_target="tpu_custom_call" | custom-call | flops 1000000000 | bytes 1000000 | tf_op jit(solution)/shard_map/sum_columns/pallas_call | solution.py:470
  114.2 1.3 %place_rows.1 = bf16[768,512]{1,0:T(8,128)(2,1)} custom-call(s32[2]{0:T(128)S(1)} %pad_add_fusion.place_ref.refs_0_, bf16[384,512]{1,0:T(8,128)(2,1)S(1)} %collective-permute-done.14.received_ref, bf16[768,512]{1,0:T(8,128)(2,1)} %sum_columns.3.kept_ref), custom_call_target="tpu_custom_call", output_to_operand_aliasing={{}: (2, {})} | custom-call | flops 1000000000 | bytes 1000000 | tf_op jit(solution)/shard_map/place_rows/pallas_call | solution.py:491
  (35 shorter events, 7.3 us)
Async XLA Ops:
  0.0 51.1 %collective-permute-start.6 = (bf16[4096,512]{1,0:T(8,128)(2,1)}, bf16[4096,512]{1,0:T(8,128)(2,1)}, u32[]{:S(2)}, u32[]{:S(2)}) collective-permute-start(bf16[4096,512]{1,0:T(8,128)(2,1)} %bitcast.21), channel_id=1, source_target_pairs={{0,128},{128,0},{1,129},{129,1},{2,130},{130,2},{3,131},{131,3},{4... | collective-permute-start | bytes 12582920 | tf_op jit(solution)/shard_map/ppermute | solution.py:45
  4.0 1.4 %copy-start.3 = (bf16[24,64,512]{2,1,0:T(8,128)(2,1)S(1)}, bf16[24,64,512]{2,1,0:T(8,128)(2,1)}, u32[]{:S(2)}) copy-start(bf16[24,64,512]{2,1,0:T(8,128)(2,1)} %refs_2_.1) | copy-start | bytes 4718596
  7.5 9.6 %copy-start.5 = (bf16[768,1024]{1,0:T(8,128)(2,1)S(1)}, bf16[768,1024]{1,0:T(8,128)(2,1)}, u32[]{:S(2)}) copy-start(bf16[768,1024]{1,0:T(8,128)(2,1)} %param.6) | copy-start | bytes 4718596
  7.5 33.0 %all-to-all-start = ((bf16[32,104,128]{2,1,0:T(8,128)(2,1)}), bf16[32,104,128]{2,1,0:T(8,128)(2,1)S(1)}, u32[]{:S(2)}, u32[]{:S(2)}) async-start(bf16[32,104,128]{2,1,0:T(8,128)(2,1)} %pack_rows.1), calls=%async_computation | async-start | bytes 1703936 | tf_op jit(solution)/shard_map/all_to_all | solution.py:533
  17.2 10.5 %collective-permute-start.2 = (bf16[192,1024]{1,0:T(8,128)(2,1)S(1)}, bf16[192,1024]{1,0:T(8,128)(2,1)S(1)}, u32[]{:S(2)}, u32[]{:S(2)}) collective-permute-start(bf16[192,1024]{1,0:T(8,128)(2,1)S(1)} %get-tuple-element.37.refs_1_), channel_id=1, source_target_pairs={{0,1},{1,0},{2,3},{3,2},{4,5},{5,4},{6,7},{7,6},{8,9},{9,8},{10,11... | collective-permute-start | bytes 1179656 | tf_op jit(solution)/shard_map/ppermute | solution.py:50
  18.5 11.3 %collective-permute-start = (bf16[192,1024]{1,0:T(8,128)(2,1)S(1)}, bf16[192,1024]{1,0:T(8,128)(2,1)S(1)}, u32[]{:S(2)}, u32[]{:S(2)}) collective-permute-start(bf16[192,1024]{1,0:T(8,128)(2,1)S(1)} %get-tuple-element.38.refs_0_), channel_id=1, source_target_pairs={{0,3},{1,2},{2,1},{3,0},{4,7},{5,6},{6,5},{7,4},{8,11},{9,10},{10,... | collective-permute-start | bytes 1179656 | tf_op jit(solution)/shard_map/ppermute | solution.py:50
  20.3 15.8 %collective-permute-start.4 = (bf16[192,1024]{1,0:T(8,128)(2,1)S(1)}, bf16[192,1024]{1,0:T(8,128)(2,1)S(1)}, u32[]{:S(2)}, u32[]{:S(2)}) collective-permute-start(bf16[192,1024]{1,0:T(8,128)(2,1)S(1)} %get-tuple-element.38.refs_0_), channel_id=1, source_target_pairs={{0,1},{1,0},{2,3},{3,2},{4,5},{5,4},{6,7},{7,6},{8,9},{9,8},{10,11... | collective-permute-start | bytes 1179656 | tf_op jit(solution)/shard_map/ppermute | solution.py:50
  20.6 17.6 %collective-permute-start.5 = (bf16[192,1024]{1,0:T(8,128)(2,1)S(1)}, bf16[192,1024]{1,0:T(8,128)(2,1)S(1)}, u32[]{:S(2)}, u32[]{:S(2)}) collective-permute-start(bf16[192,1024]{1,0:T(8,128)(2,1)S(1)} %get-tuple-element.37.refs_1_), channel_id=1, source_target_pairs={{0,3},{1,2},{2,1},{3,0},{4,7},{5,6},{6,5},{7,4},{8,11},{9,10},{10,... | collective-permute-start | bytes 1179656 | tf_op jit(solution)/shard_map/ppermute | solution.py:50
  42.5 26.4 %all-to-all-start.1 = ((bf16[32,96,128]{2,1,0:T(8,128)(2,1)}), bf16[32,96,128]{2,1,0:T(8,128)(2,1)S(1)}, u32[]{:S(2)}, u32[]{:S(2)}) async-start(bf16[32,96,128]{2,1,0:T(8,128)(2,1)} %route_rows.1), calls=%async_computation.1 | async-start | bytes 1572864 | tf_op jit(solution)/shard_map/all_to_all | solution.py:535
  49.1 9.5 %collective-permute-start.1 = (bf16[192,1024]{1,0:T(8,128)(2,1)S(1)}, bf16[192,1024]{1,0:T(8,128)(2,1)S(1)}, u32[]{:S(2)}, u32[]{:S(2)}) collective-permute-start(bf16[192,1024]{1,0:T(8,128)(2,1)S(1)} %collective-permute-done.refs_4_), channel_id=1, source_target_pairs={{0,1},{1,0},{2,3},{3,2},{4,5},{5,4},{6,7},{7,6},{8,9},{9,8},{10,11... | collective-permute-start | bytes 1179656 | tf_op jit(solution)/shard_map/ppermute | solution.py:50
  49.2 9.9 %collective-permute-start.3 = (bf16[192,1024]{1,0:T(8,128)(2,1)S(1)}, bf16[192,1024]{1,0:T(8,128)(2,1)S(1)}, u32[]{:S(2)}, u32[]{:S(2)}) collective-permute-start(bf16[192,1024]{1,0:T(8,128)(2,1)S(1)} %collective-permute-done.2.refs_3_), channel_id=1, source_target_pairs={{0,3},{1,2},{2,1},{3,0},{4,7},{5,6},{6,5},{7,4},{8,11},{9,10},{10,... | collective-permute-start | bytes 1179656 | tf_op jit(solution)/shard_map/ppermute | solution.py:50
  51.1 2.2 %copy-start = (bf16[1,4096,512]{2,1,0:T(8,128)(2,1)S(1)}, bf16[1,4096,512]{2,1,0:T(8,128)(2,1)}, u32[]{:S(2)}) copy-start(bf16[1,4096,512]{2,1,0:T(8,128)(2,1)} %param.7) | copy-start | bytes 12582916
  53.3 5.8 %copy-start.1 = (bf16[1,4096,512]{2,1,0:T(8,128)(2,1)S(1)}, bf16[1,4096,512]{2,1,0:T(8,128)(2,1)}, u32[]{:S(2)}) copy-start(bf16[1,4096,512]{2,1,0:T(8,128)(2,1)} %param.7) | copy-start | bytes 12582916
  68.8 6.7 %copy-start.2 = (bf16[1,4096,512]{2,1,0:T(8,128)(2,1)S(1)}, bf16[1,4096,512]{2,1,0:T(8,128)(2,1)}, u32[]{:S(2)}) copy-start(bf16[1,4096,512]{2,1,0:T(8,128)(2,1)} %param.7) | copy-start | bytes 12582916
  69.8 5.7 %copy-start.4 = (bf16[768,512]{1,0:T(8,128)(2,1)S(1)}, bf16[768,512]{1,0:T(8,128)(2,1)}, u32[]{:S(2)}) copy-start(bf16[768,512]{1,0:T(8,128)(2,1)} %refs_3_.1) | copy-start | bytes 2359300
  69.8 5.7 %collective-permute-start.7 = (bf16[768,256]{1,0:T(8,128)(2,1)S(1)}, bf16[768,256]{1,0:T(8,128)(2,1)S(1)}, u32[]{:S(2)}, u32[]{:S(2)}) collective-permute-start(bf16[768,256]{1,0:T(8,128)(2,1)S(1)} %unpack_rows.2.refs_2_), channel_id=1, source_target_pairs={{0,128},{128,0},{1,129},{129,1},{2,130},{130,2},{3,131},{131,3},{4... | collective-permute-start | bytes 1179656 | tf_op jit(solution)/shard_map/ppermute | solution.py:45
  82.2 10.4 %collective-permute-start.8 = (bf16[192,1024]{1,0:T(8,128)(2,1)S(1)}, bf16[192,1024]{1,0:T(8,128)(2,1)S(1)}, u32[]{:S(2)}, u32[]{:S(2)}) collective-permute-start(bf16[192,1024]{1,0:T(8,128)(2,1)S(1)} %get-tuple-element.29), channel_id=1, source_target_pairs={{0,1},{1,0},{2,3},{3,2},{4,5},{5,4},{6,7},{7,6},{8,9},{9,8},{10,11... | collective-permute-start | bytes 1179656 | tf_op jit(solution)/shard_map/ppermute | solution.py:50
  82.3 11.6 %collective-permute-start.9 = (bf16[192,1024]{1,0:T(8,128)(2,1)S(1)}, bf16[192,1024]{1,0:T(8,128)(2,1)S(1)}, u32[]{:S(2)}, u32[]{:S(2)}) collective-permute-start(bf16[192,1024]{1,0:T(8,128)(2,1)S(1)} %get-tuple-element.30), channel_id=1, source_target_pairs={{0,3},{1,2},{2,1},{3,0},{4,7},{5,6},{6,5},{7,4},{8,11},{9,10},{10,... | collective-permute-start | bytes 1179656 | tf_op jit(solution)/shard_map/ppermute | solution.py:50
  88.1 13.0 %collective-permute-start.10 = (bf16[192,1024]{1,0:T(8,128)(2,1)S(1)}, bf16[192,1024]{1,0:T(8,128)(2,1)S(1)}, u32[]{:S(2)}, u32[]{:S(2)}) collective-permute-start(bf16[192,1024]{1,0:T(8,128)(2,1)S(1)} %get-tuple-element.33), channel_id=1, source_target_pairs={{0,1},{1,0},{2,3},{3,2},{4,5},{5,4},{6,7},{7,6},{8,9},{9,8},{10,11... | collective-permute-start | bytes 1179656 | tf_op jit(solution)/shard_map/ppermute | solution.py:50
  88.9 13.4 %collective-permute-start.12 = (bf16[192,1024]{1,0:T(8,128)(2,1)S(1)}, bf16[192,1024]{1,0:T(8,128)(2,1)S(1)}, u32[]{:S(2)}, u32[]{:S(2)}) collective-permute-start(bf16[192,1024]{1,0:T(8,128)(2,1)S(1)} %get-tuple-element.35), channel_id=1, source_target_pairs={{0,3},{1,2},{2,1},{3,0},{4,7},{5,6},{6,5},{7,4},{8,11},{9,10},{10,... | collective-permute-start | bytes 1179656 | tf_op jit(solution)/shard_map/ppermute | solution.py:50
  94.1 16.7 %collective-permute-start.11 = (bf16[192,1024]{1,0:T(8,128)(2,1)S(1)}, bf16[192,1024]{1,0:T(8,128)(2,1)S(1)}, u32[]{:S(2)}, u32[]{:S(2)}) collective-permute-start(bf16[192,1024]{1,0:T(8,128)(2,1)S(1)} %get-tuple-element.31.refs_7_), channel_id=1, source_target_pairs={{0,3},{1,2},{2,1},{3,0},{4,7},{5,6},{6,5},{7,4},{8,11},{9,10},{10,... | collective-permute-start | bytes 1179656 | tf_op jit(solution)/shard_map/ppermute | solution.py:50
  96.0 14.8 %collective-permute-start.13 = (bf16[192,1024]{1,0:T(8,128)(2,1)S(1)}, bf16[192,1024]{1,0:T(8,128)(2,1)S(1)}, u32[]{:S(2)}, u32[]{:S(2)}) collective-permute-start(bf16[192,1024]{1,0:T(8,128)(2,1)S(1)} %get-tuple-element.36), channel_id=1, source_target_pairs={{0,1},{1,0},{2,3},{3,2},{4,5},{5,4},{6,7},{7,6},{8,9},{9,8},{10,11... | collective-permute-start | bytes 1179656 | tf_op jit(solution)/shard_map/ppermute | solution.py:50
  111.5 2.7 %collective-permute-start.14 = (bf16[384,512]{1,0:T(8,128)(2,1)S(1)}, bf16[384,512]{1,0:T(8,128)(2,1)S(1)}, u32[]{:S(2)}, u32[]{:S(2)}) collective-permute-start(bf16[384,512]{1,0:T(8,128)(2,1)S(1)} %sum_columns.2), channel_id=1, source_target_pairs={{0,128},{128,0},{1,129},{129,1},{2,130},{130,2},{3,131},{131,3},{4... | collective-permute-start | bytes 1179656 | tf_op jit(solution)/shard_map/ppermute | solution.py:45
